TPU v7x, 128 devices: a whole 4x4x4 slice. The times are simulated.
128 devices in a mesh: rep: 2 (over z_hi), shard: 64 (over y, z_lo, x, core).
Axes of the slice: x: 4, y: 4, z: 4 (z_hi: 2, z_lo: 2; z = z_hi * 2 + z_lo), core: 2. Of those that a mesh axis runs over, the one named last changes fastest.
Arguments:
- tokens: bfloat16 [16384, 2048], P(('rep', 'shard')), may hold values from -6 to 6
- cotangent: bfloat16 [16384, 2048], P(('rep', 'shard')), may hold values from -6 to 6
- segment_ids: int32 [16384], P(('rep', 'shard')), may hold values from 1 to 16384, as said below
- position_ids: int32 [16384], P(('rep', 'shard')), may hold values from 0 to 1023, as said below
- w_qkv: float32 [2048, 2560], P('shard'), may hold values from -0.125 to 0.125
- w_out: float32 [2048, 2048], P('shard'), may hold values from -1.5 to 1.5
- w_gate_up: float32 [2048, 11264], P('shard'), may hold values from -0.125 to 0.125
- w_down: float32 [5632, 2048], P('shard'), may hold values from -0.078125 to 0.078125
- gains: float32 [2, 2048], P(None, 'shard'), may hold values from 0.5 to 1.5
- m_qkv: float32 [2048, 2560], P('shard'), may hold values from -80 to 80
- v_qkv: float32 [2048, 2560], P('shard'), may hold values from 425.984 to 6881.28
- m_out: float32 [2048, 2048], P('shard'), may hold values from -8 to 8
- v_out: float32 [2048, 2048], P('shard'), may hold values from 4.308992 to 68.8128
- m_gate_up: float32 [2048, 11264], P('shard'), may hold values from -24 to 24
- v_gate_up: float32 [2048, 11264], P('shard'), may hold values from 38.83008 to 620.9536
- m_down: float32 [5632, 2048], P('shard'), may hold values from -40 to 40
- v_down: float32 [5632, 2048], P('shard'), may hold values from 107.80672 to 1720.32
- m_gains: float32 [2, 2048], P(None, 'shard'), may hold values from -80 to 80
- v_gains: float32 [2, 2048], P(None, 'shard'), may hold values from 425.984 to 6881.28
Outputs:
- mixed: float32 [16384, 2048], P(('rep', 'shard'))
- d_tokens: float32 [16384, 2048], P(('rep', 'shard'))
- new_qkv: float32 [2048, 2560], P('shard')
- new_m_qkv: float32 [2048, 2560], P('shard')
- new_v_qkv: float32 [2048, 2560], P('shard')
- new_out: float32 [2048, 2048], P('shard')
- new_m_out: float32 [2048, 2048], P('shard')
- new_v_out: float32 [2048, 2048], P('shard')
- new_gate_up: float32 [2048, 11264], P('shard')
- new_m_gate_up: float32 [2048, 11264], P('shard')
- new_v_gate_up: float32 [2048, 11264], P('shard')
- new_down: float32 [5632, 2048], P('shard')
- new_m_down: float32 [5632, 2048], P('shard')
- new_v_down: float32 [5632, 2048], P('shard')
- new_gains: float32 [2, 2048], P(None, 'shard')
- new_m_gains: float32 [2, 2048], P(None, 'shard')
- new_v_gains: float32 [2, 2048], P(None, 'shard')
Inputs may be any that keep to these rules, and one draw needn't show every extreme that they name: `segment_ids`: tokens form sequences of 1024 consecutive tokens; documents never cross a sequence's end; every document but a sequence's last holds 200 tokens or more; numbers rise along the tokens, and no two documents share one; the last document of the k-th sequence (from 0) is numbered (k + 1) * 1024; in each draw one sequence is a single document. `position_ids`: positions count from 0 at each document's first token.
All inputs are finite; a program needn't handle non-finite values.
Results may differ from a plain program's by a relative error of at most 0.02.
Values may be sent and summed in bfloat16 or wider, within the bound.
No kernel may reach another device: no remote copies, remote signals or barrier semaphores. Data moves between devices by JAX's collectives and lax.ppermute only.
A program may use at most 448 MiB of HBM per device.

v0:
```python
import jax
import jax.numpy as jnp
from jax import lax
from jax.sharding import PartitionSpec as P

HEADS = 32
KV_HEADS = 4
HEAD_DIM = 64
FF = 5632
SEQ_DEV = 8
STEP = 10


EPSILON = 1e-05
BETA_ONE = 0.9
BETA_TWO = 0.95
ADAM_EPSILON = 1e-08
DECAY = 0.1
RATE_QKV = 0.02
RATE_OUT = 0.25
RATE_GATE_UP = 0.02
RATE_DOWN = 0.013
RATE_GAINS = 0.3


def rows_first(arrays, axis, dims):
    turned = [jnp.moveaxis(a, dim, 0) for a, dim in zip(arrays, dims)]
    widths = [t[0].size for t in turned]
    both = jnp.concatenate([t.reshape(-1, w) for t, w in zip(turned, widths)], axis=1)
    result = lax.all_gather(both, axis, axis=0, tiled=True)
    blocks = jnp.split(result, [sum(widths[:k]) for k in range(1, len(widths))], axis=1)
    return tuple(
        (
            jnp.moveaxis(b.reshape(-1, *t.shape[1:]), 0, dim)
            for b, t, dim in zip(blocks, turned, dims)
        )
    )


def shifted(x, axis, by):
    length = lax.axis_size(axis)
    pairs = [(i, i + by) for i in range(length) if 0 <= i + by < length]
    return lax.ppermute(x, axis, pairs)


def sent_to_all(x, axis):
    length = lax.axis_size(axis)
    return lax.all_to_all(jnp.broadcast_to(x[None], (length, *x.shape)), axis, 0, 0, tiled=True)


def of_everyone(x, axis):
    everything = sent_to_all(x, axis)
    return jnp.sum(everything.astype(jnp.float32), axis=0)


def in_one_piece(arrays, axis, dim, along):
    widths = [a.shape[along] for a in arrays]
    both = jnp.concatenate(arrays, axis=along)
    result = lax.psum_scatter(both, axis, scatter_dimension=dim, tiled=True)
    return tuple(jnp.split(result, [sum(widths[:k]) for k in range(1, len(widths))], axis=along))


def rms_norm(values, gain):
    return values * lax.rsqrt(jnp.mean(values * values, axis=-1, keepdims=True) + EPSILON) * gain


def rotate_pairs(values, positions):
    half = values.shape[-1] // 2
    freqs = 10000.0 ** (-jnp.arange(half).astype(jnp.float32) * 2.0 / values.shape[-1])
    angles = positions.astype(jnp.float32)[:, None] * freqs[None, :]
    cosine = jnp.cos(angles)[:, None, :]
    sine = jnp.sin(angles)[:, None, :]
    first = values[..., :half]
    second = values[..., half:]
    return jnp.concatenate(
        [first * cosine - second * sine, second * cosine + first * sine], axis=-1
    )


def gated_unit(gate, upward):
    return jax.nn.silu(gate) * upward


def adam_step(weight, grad, first, second, rate):
    first_new = BETA_ONE * first + (1.0 - BETA_ONE) * grad
    second_new = BETA_TWO * second + (1.0 - BETA_TWO) * grad * grad
    first_hat = first_new / (1.0 - BETA_ONE**STEP)
    second_hat = second_new / (1.0 - BETA_TWO**STEP)
    weight_new = weight - rate * (
        first_hat / (jnp.sqrt(second_hat) + ADAM_EPSILON) + DECAY * weight
    )
    return (weight_new, first_new, second_new)


def on_device(
    tokens,
    cotangent,
    segment_ids,
    position_ids,
    w_qkv,
    w_out,
    w_gate_up,
    w_down,
    gains,
    m_qkv,
    v_qkv,
    m_out,
    v_out,
    m_gate_up,
    v_gate_up,
    m_down,
    v_down,
    m_gains,
    v_gains,
):
    rows_here = tokens.shape[0]
    kv_width = KV_HEADS * HEAD_DIM
    att_width = HEADS * HEAD_DIM
    ratio = HEADS // KV_HEADS
    score_scale = HEAD_DIM ** (-0.5)
    qkv_local = w_qkv.astype(jnp.bfloat16)
    out_local = w_out.astype(jnp.bfloat16)
    gate_local = w_gate_up.astype(jnp.bfloat16)
    down_local = w_down.astype(jnp.bfloat16)
    qkv_full, out_full, gain_full = rows_first(
        (qkv_local, out_local, gains.astype(jnp.bfloat16)), "shard", (0, 0, 1)
    )
    gate_full, down_full = (
        lax.all_gather(gate_local, "shard", axis=0, tiled=True),
        lax.all_gather(down_local, "shard", axis=0, tiled=True),
    )
    gain_float = gain_full.astype(jnp.float32)
    inputs = tokens.astype(jnp.float32)
    normed_f, norm_one_back = jax.vjp(rms_norm, inputs, gain_float[0])
    normed = normed_f.astype(jnp.bfloat16)
    projected = jnp.dot(normed, qkv_full, preferred_element_type=jnp.float32)

    def turn(values):
        return rotate_pairs(values, position_ids)

    query_rot, query_back = jax.vjp(
        turn, projected[:, :att_width].reshape(rows_here, HEADS, HEAD_DIM)
    )
    key_rot, key_back = jax.vjp(
        turn, projected[:, att_width : att_width + kv_width].reshape(rows_here, KV_HEADS, HEAD_DIM)
    )
    queries = query_rot.astype(jnp.bfloat16).reshape(rows_here, KV_HEADS, ratio, HEAD_DIM)
    key_flat = key_rot.astype(jnp.bfloat16).reshape(rows_here, kv_width)
    value_flat = projected[:, att_width + kv_width :].astype(jnp.bfloat16)
    key_list = [key_flat]
    value_list = [value_flat]
    segment_list = [segment_ids]
    place_list = [position_ids]
    for offset in range(1, SEQ_DEV):
        key_in, value_in, segment_in, place_in = shifted(
            (key_flat, value_flat, segment_ids, position_ids), "shard", offset
        )
        key_list.append(key_in)
        value_list.append(value_in)
        segment_list.append(segment_in)
        place_list.append(place_in)
    key_rows = SEQ_DEV * rows_here
    keys_all = jnp.concatenate(key_list, axis=0).reshape(key_rows, KV_HEADS, HEAD_DIM)
    values_all = jnp.concatenate(value_list, axis=0).reshape(key_rows, KV_HEADS, HEAD_DIM)
    segments_all = jnp.concatenate(segment_list, axis=0)
    places_all = jnp.concatenate(place_list, axis=0)
    allowed = (segment_ids[:, None] == segments_all[None, :]) & (
        places_all[None, :] <= position_ids[:, None]
    )

    def masked_scores():
        raw = (
            jnp.einsum("qgrd,kgd->grqk", queries, keys_all, preferred_element_type=jnp.float32)
            * score_scale
        )
        return jnp.where(allowed[None, None], raw, -1e30)

    scores = masked_scores()
    row_peak = jnp.max(scores, axis=-1, keepdims=True)
    expo = jnp.exp(scores - row_peak)
    row_total = jnp.sum(expo, axis=-1, keepdims=True)
    probs = expo / row_total
    log_total = row_peak + jnp.log(row_total)
    probs_low = probs.astype(jnp.bfloat16)
    heads_f = jnp.einsum(
        "grqk,kgd->qgrd", probs_low, values_all, preferred_element_type=jnp.float32
    )
    heads_out = heads_f.reshape(rows_here, att_width).astype(jnp.bfloat16)
    middle = inputs + jnp.dot(heads_out, out_full, preferred_element_type=jnp.float32)
    normed_two_f, norm_two_back = jax.vjp(rms_norm, middle, gain_float[1])
    normed_two = normed_two_f.astype(jnp.bfloat16)
    gate_up = jnp.dot(normed_two, gate_full, preferred_element_type=jnp.float32)
    hidden_f, hidden_back = jax.vjp(gated_unit, gate_up[:, :FF], gate_up[:, FF:])
    hidden = hidden_f.astype(jnp.bfloat16)
    mixed = middle + jnp.dot(hidden, down_full, preferred_element_type=jnp.float32)
    gate_back_w, down_back_w = (gate_full, down_full)
    qkv_back_w, out_back_w = (qkv_full, out_full)
    grad_out_f = cotangent.astype(jnp.float32)
    grad_hidden = jnp.einsum(
        "td,fd->tf", cotangent, down_back_w, preferred_element_type=jnp.float32
    )
    grad_gate, grad_up = hidden_back(grad_hidden)
    grad_gu_low = jnp.concatenate([grad_gate, grad_up], axis=1).astype(jnp.bfloat16)
    grad_gate_up = jnp.einsum(
        "td,tf->df", normed_two, grad_gu_low, preferred_element_type=jnp.float32
    )
    grad_normed_two = jnp.einsum(
        "tf,df->td", grad_gu_low, gate_back_w, preferred_element_type=jnp.float32
    )
    grad_middle_norm, grad_gain_two = norm_two_back(grad_normed_two)
    grad_middle = grad_out_f + grad_middle_norm
    hidden_owned = lax.all_to_all(hidden, "shard", split_axis=1, concat_axis=0, tiled=True)
    down_owned = jnp.einsum(
        "tf,td->fd",
        hidden_owned,
        lax.all_gather(cotangent, "shard", axis=0, tiled=True),
        preferred_element_type=jnp.float32,
    )
    gate_owned = lax.psum_scatter(grad_gate_up, "shard", scatter_dimension=0, tiled=True)
    mlp_parts = (gate_owned, down_owned)
    mlp_parts = (
        of_everyone(mlp_parts[0].astype(jnp.bfloat16), "rep").astype(jnp.float32),
        of_everyone(mlp_parts[1].astype(jnp.bfloat16), "rep").astype(jnp.float32),
    )
    grad_attn_low = grad_middle.astype(jnp.bfloat16)
    grad_w_out = jnp.einsum(
        "to,td->od", heads_out, grad_attn_low, preferred_element_type=jnp.float32
    )
    grad_heads = jnp.einsum(
        "td,od->to", grad_attn_low, out_back_w, preferred_element_type=jnp.float32
    )
    grad_heads_low = grad_heads.astype(jnp.bfloat16).reshape(rows_here, KV_HEADS, ratio, HEAD_DIM)
    probs_again = jnp.exp(masked_scores() - log_total)
    grad_probs = jnp.einsum(
        "qgrd,kgd->grqk", grad_heads_low, values_all, preferred_element_type=jnp.float32
    )
    row_inner = jnp.sum(probs_again * grad_probs, axis=-1, keepdims=True)
    grad_scores = (probs_again * (grad_probs - row_inner)).astype(jnp.bfloat16)
    grad_queries = (
        jnp.einsum("grqk,kgd->qgrd", grad_scores, keys_all, preferred_element_type=jnp.float32)
        * score_scale
    )
    grad_keys_all = (
        jnp.einsum("grqk,qgrd->kgd", grad_scores, queries, preferred_element_type=jnp.float32)
        * score_scale
    ).reshape(key_rows, kv_width)
    grad_values_all = jnp.einsum(
        "grqk,qgrd->kgd",
        probs_again.astype(jnp.bfloat16),
        grad_heads_low,
        preferred_element_type=jnp.float32,
    ).reshape(key_rows, kv_width)
    grad_keys = grad_keys_all[:rows_here]
    grad_values = grad_values_all[:rows_here]
    for offset in range(1, SEQ_DEV):
        key_ret, value_ret = (
            shifted(
                grad_keys_all[offset * rows_here : (offset + 1) * rows_here].astype(jnp.bfloat16),
                "shard",
                -offset,
            ).astype(jnp.float32),
            shifted(
                grad_values_all[offset * rows_here : (offset + 1) * rows_here].astype(jnp.bfloat16),
                "shard",
                -offset,
            ).astype(jnp.float32),
        )
        grad_keys = grad_keys + key_ret
        grad_values = grad_values + value_ret
    grad_query_raw = query_back(grad_queries.reshape(rows_here, HEADS, HEAD_DIM))[0].reshape(
        rows_here, att_width
    )
    grad_key_raw = key_back(grad_keys.reshape(rows_here, KV_HEADS, HEAD_DIM))[0].reshape(
        rows_here, kv_width
    )
    grad_proj_low = jnp.concatenate([grad_query_raw, grad_key_raw, grad_values], axis=1).astype(
        jnp.bfloat16
    )
    grad_w_qkv = jnp.einsum("td,tc->dc", normed, grad_proj_low, preferred_element_type=jnp.float32)
    grad_normed = jnp.einsum(
        "tc,dc->td", grad_proj_low, qkv_back_w, preferred_element_type=jnp.float32
    )
    grad_input_norm, grad_gain_one = norm_one_back(grad_normed)
    d_tokens = grad_middle + grad_input_norm
    attn_parts = (
        *in_one_piece((grad_w_qkv, grad_w_out), "shard", 0, 1),
        lax.psum_scatter(
            jnp.stack([grad_gain_one, grad_gain_two]), "shard", scatter_dimension=1, tiled=True
        ),
    )
    attn_parts = (
        of_everyone(attn_parts[0].astype(jnp.bfloat16), "rep").astype(jnp.float32),
        of_everyone(attn_parts[1].astype(jnp.bfloat16), "rep").astype(jnp.float32),
        of_everyone(attn_parts[2].astype(jnp.bfloat16), "rep").astype(jnp.float32),
    )
    qkv_new = adam_step(w_qkv, attn_parts[0], m_qkv, v_qkv, RATE_QKV)
    out_new = adam_step(w_out, attn_parts[1], m_out, v_out, RATE_OUT)
    gate_new = adam_step(w_gate_up, mlp_parts[0], m_gate_up, v_gate_up, RATE_GATE_UP)
    down_new = adam_step(w_down, mlp_parts[1], m_down, v_down, RATE_DOWN)
    gains_new = adam_step(gains, attn_parts[2], m_gains, v_gains, RATE_GAINS)
    return (
        mixed,
        d_tokens,
        qkv_new[0],
        qkv_new[1],
        qkv_new[2],
        out_new[0],
        out_new[1],
        out_new[2],
        gate_new[0],
        gate_new[1],
        gate_new[2],
        down_new[0],
        down_new[1],
        down_new[2],
        gains_new[0],
        gains_new[1],
        gains_new[2],
    )


def solution(mesh):
    return jax.shard_map(
        on_device,
        mesh=mesh,
        in_specs=(
            P(("rep", "shard"), None),
            P(("rep", "shard"), None),
            P(("rep", "shard")),
            P(("rep", "shard")),
            P("shard", None),
            P("shard", None),
            P("shard", None),
            P("shard", None),
            P(None, "shard"),
            P("shard", None),
            P("shard", None),
            P("shard", None),
            P("shard", None),
            P("shard", None),
            P("shard", None),
            P("shard", None),
            P("shard", None),
            P(None, "shard"),
            P(None, "shard"),
        ),
        out_specs=(
            P(("rep", "shard"), None),
            P(("rep", "shard"), None),
            P("shard", None),
            P("shard", None),
            P("shard", None),
            P("shard", None),
            P("shard", None),
            P("shard", None),
            P("shard", None),
            P("shard", None),
            P("shard", None),
            P("shard", None),
            P("shard", None),
            P("shard", None),
            P(None, "shard"),
            P(None, "shard"),
            P(None, "shard"),
        ),
        check_vma=False,
    )
```

profile of v0, /device:TPU:6, one launch (start us, length us, event | category | flops | bytes accessed | tf_op | source)
XLA Modules:
  0.0 2060.4 jit_solution(11998188038263228832)
XLA Ops:
  17.1 3.7 collective-permute-start.15
  20.9 4.3 collective-permute-start.16
  28.8 3.8 collective-permute-start.18
  41.9 4.7 collective-permute-start.8
  50.3 4.3 collective-permute-start.10
  60.4 3.7 collective-permute-start.13
  65.8 72.3 %all-gather.5.cloned.1.call-done = bf16[2048,4610]{1,0:T(8,128)(2,1)} async-done(((bf16[32,4610]{1,0:T(8,128)(2,1)}), bf16[2048,4610]{1,0:T(8,128)(2,1)}) %all-gather.5.cloned.1.call-update) | async-done | bytes 18882576 | tf_op jit(solution)/shard_map/all_gather | solution.py:30
  140.1 5.0 fusion.7
  148.0 4.2 collective-permute-start.1
  155.5 4.6 collective-permute-start.3
  176.8 4.3 collective-permute-start.22
  185.7 4.1 collective-permute-start.24
  190.4 3.9 collective-permute-start.25
  198.2 4.0 collective-permute-start.27
  204.9 7.4 fusion.17
  212.2 9.5 fusion.3
  221.8 8.4 fusion.38
  230.1 5.1 multiply_reduce_fusion.2
  235.9 167.5 %all-gather.7.cloned.1.call-done = bf16[2048,11264]{1,0:T(8,128)(2,1)} async-done(((bf16[32,11264]{1,0:T(8,128)(2,1)}), bf16[2048,11264]{1,0:T(8,128)(2,1)}) %all-gather.7.cloned.1.call-update) | async-done | bytes 46137360 | tf_op jit(solution)/shard_map/all_gather | solution.py:129
  403.4 20.1 fusion.85
  423.5 122.3 %all-gather.9.cloned.1.call-done = bf16[5632,2048]{1,0:T(8,128)(2,1)} async-done(((bf16[88,2048]{1,0:T(8,128)(2,1)}), bf16[5632,2048]{1,0:T(8,128)(2,1)}) %all-gather.9.cloned.1.call-update) | async-done | bytes 23068688 | tf_op jit(solution)/shard_map/all_gather | solution.py:130
  545.8 15.1 fusion.20
  560.9 22.9 %multiply_reduce_fusion = (f32[2048]{0:T(1024)}, f32[128]{0:T(128)S(1)}, f32[128,2048]{1,0:T(8,128)}) fusion(f32[128,2048]{1,0:T(8,128)S(1)} %get-tuple-element.74, f32[128]{0:T(128)S(1)} %fusion.74, f32[2048]{0:T(1024)S(1)} %get-tuple-element.21, bf16[2048,11264]{1,0:T(8,128)(2,1)} %all-gather.7.cloned.1.call-done, ...), kind=kOutput, calls=%fused_computation.71 | convolution fusion | flops 5912918016 | bytes 51135488 | tf_op jit(solution)/shard_map/tf,df->td/dot_general | solution.py:207
  585.5 7.1 fusion.25
  594.6 11.0 fusion.93
  605.6 12.8 fusion
  618.4 11.1 fusion.2
  629.5 6.2 fusion.94
  672.3 9.1 fusion.42
  683.8 9.2 fusion.54
  693.0 9.3 fusion.52
  702.3 24.7 %pad_maximum_fusion = f32[2048,4608]{1,0:T(8,128)} fusion(f32[2048,2048]{1,0:T(8,128)} %fusion.54, f32[2048,2560]{1,0:T(8,128)} %fusion.52), kind=kLoop, calls=%fused_computation | loop fusion | flops 9437184 | bytes 75497472 | tf_op jit(solution)/shard_map/concatenate | solution.py:58
  728.4 33.3 %fusion.28 = f32[2048,11264]{1,0:T(8,128)} fusion(bf16[128,5632]{1,0:T(8,128)(2,1)} %get-tuple-element.43, bf16[128,5632]{1,0:T(8,128)(2,1)S(1)} %copy-done.3, f32[128,2048]{1,0:T(8,128)S(1)} %get-tuple-element.74, f32[2048]{0:T(1024)S(1)} %get-tuple-element.21, f32[128]{0:T(128)S(1)} %fusion.74), kind=kOutput, calls=%fused_computation.43 | convolution fusion | flops 5912133632 | bytes 96215552 | tf_op jit(solution)/shard_map/td,tf->df/dot_general | solution.py:204
  764.5 24.8 %all-to-all-start.3 = ((bf16[128,64,88]{0,2,1:T(8,128)(2,1)}), bf16[128,64,88]{0,2,1:T(8,128)(2,1)S(1)}, u32[]{:S(2)}, u32[]{:S(2)}) async-start(bf16[128,64,88]{0,2,1:T(8,128)(2,1)} %bitcast.159), calls=%async_computation.5 | async-start | bytes 2883584 | tf_op jit(solution)/shard_map/all_to_all | solution.py:212
  789.4 12.2 convolution_add_fusion
  801.6 168.5 %reduce-scatter.10.cloned.1.call-done = f32[32,2]{1,0:T(8,128)} async-done(((f32[2048,2]{1,0:T(8,128)}), f32[32,2]{1,0:T(8,128)}) %reduce-scatter.10.cloned.1.call-update) | async-done | bytes 272
  971.5 4.2 all-to-all-start.5
  975.7 197.0 %all-gather.11.cloned.1.call-done = bf16[8192,2048]{1,0:T(8,128)(2,1)} async-done(((bf16[128,2048]{1,0:T(8,128)(2,1)}), bf16[8192,2048]{1,0:T(8,128)(2,1)}) %all-gather.11.cloned.1.call-update) | async-done | bytes 33554448 | tf_op jit(solution)/shard_map/all_gather | solution.py:216
  1172.8 13.4 convolution_convert_fusion
  1187.2 4.4 all-to-all-start.4
  1194.8 27.1 %all-to-all-done.4 = bf16[2,88,2048]{2,1,0:T(8,128)(2,1)S(1)} async-done(((bf16[2,88,2048]{2,1,0:T(8,128)(2,1)}), bf16[2,88,2048]{2,1,0:T(8,128)(2,1)S(1)}, u32[]{:S(2)}, u32[]{:S(2)}) %all-to-all-start.4) | async-done | bytes 720928 | tf_op jit(solution)/shard_map/all_to_all | solution.py:48
  1222.0 282.7 %reduce-scatter.6.cloned.1.call-done = f32[32,4608]{1,0:T(8,128)} async-done(((f32[2048,4608]{1,0:T(8,128)}), f32[32,4608]{1,0:T(8,128)}) %reduce-scatter.6.cloned.1.call-update) | async-done | bytes 589840 | tf_op jit(solution)/shard_map/reduce_scatter | solution.py:59
  1506.5 4.3 all-to-all-start.1
  1522.7 6.0 all-to-all-done
  1528.8 492.6 %reduce-scatter.8.cloned.1.call-done = f32[32,11264]{1,0:T(8,128)} async-done(((f32[2048,11264]{1,0:T(8,128)}), f32[32,11264]{1,0:T(8,128)}) %reduce-scatter.8.cloned.1.call-update) | async-done | bytes 1441808 | tf_op jit(solution)/shard_map/reduce_scatter | solution.py:219
  2024.0 4.4 all-to-all-start.2
  2030.5 17.9 all-to-all-done.2
  2048.7 4.6 multiply_subtract_fusion
  (268 shorter events, 141.7 us)
Async XLA Ops:
  7.2 130.9 %all-gather.5.cloned.1.call-start = ((), (), s32[]{:S(2)}) async-start(), calls=%async_computation.9 | async-start | bytes 19701760 | tf_op jit(solution)/shard_map/all_gather | solution.py:30
  10.8 392.6 %all-gather.7.cloned.1.call-start = ((), (), s32[]{:S(2)}) async-start(), calls=%async_computation.10 | async-start | bytes 46858240 | tf_op jit(solution)/shard_map/all_gather | solution.py:129
  13.2 532.6 %all-gather.9.cloned.1.call-start = ((), (), s32[]{:S(2)}) async-start(), calls=%async_computation.11 | async-start | bytes 23429120 | tf_op jit(solution)/shard_map/all_gather | solution.py:130
  15.2 955.0 %reduce-scatter.10.cloned.1.call-start = ((), (), s32[]{:S(2)}) async-start(), calls=%async_computation.15 | async-start | bytes 1064960
  15.2 17.8 collective-permute-start.14
  17.1 19.1 collective-permute-start.15
  20.9 19.0 collective-permute-start.16
  25.2 16.7 collective-permute-start.17
  28.8 17.8 collective-permute-start.18
  33.1 17.3 collective-permute-start.19
  36.3 18.4 collective-permute-start.20
  39.9 17.5 collective-permute-start.7
  41.9 18.5 collective-permute-start.8
  46.6 17.6 collective-permute-start.9
  50.3 13.9 collective-permute-start.10
  54.7 9.6 collective-permute-start.11
  145.8 18.1 collective-permute-start
  148.0 20.3 collective-permute-start.1
  152.1 21.2 %collective-permute-start.2 = (bf16[128,256]{1,0:T(8,128)(2,1)S(1)}, bf16[128,256]{1,0:T(8,128)(2,1)}, u32[]{:S(2)}, u32[]{:S(2)}) collective-permute-start(bf16[128,256]{1,0:T(8,128)(2,1)S(1)} %get-tuple-element.41), channel_id=1, source_target_pairs={{0,3},{1,4},{2,5},{3,6},{4,7},{5,8},{6,9},{7,10},{8,11},{9,12},{10... | collective-permute-start | bytes 196616 | tf_op jit(solution)/shard_map/ppermute | solution.py:43
  155.5 21.3 %collective-permute-start.3 = (bf16[128,256]{1,0:T(8,128)(2,1)S(1)}, bf16[128,256]{1,0:T(8,128)(2,1)S(1)}, u32[]{:S(2)}, u32[]{:S(2)}) collective-permute-start(bf16[128,256]{1,0:T(8,128)(2,1)S(1)} %get-tuple-element.41), channel_id=1, source_target_pairs={{0,4},{1,5},{2,6},{3,7},{4,8},{5,9},{6,10},{7,11},{8,12},{9,13},{1... | collective-permute-start | bytes 196616 | tf_op jit(solution)/shard_map/ppermute | solution.py:43
  160.0 21.7 %collective-permute-start.4 = (bf16[128,256]{1,0:T(8,128)(2,1)S(1)}, bf16[128,256]{1,0:T(8,128)(2,1)S(1)}, u32[]{:S(2)}, u32[]{:S(2)}) collective-permute-start(bf16[128,256]{1,0:T(8,128)(2,1)S(1)} %get-tuple-element.41), channel_id=1, source_target_pairs={{0,5},{1,6},{2,7},{3,8},{4,9},{5,10},{6,11},{7,12},{8,13},{9,14},{... | collective-permute-start | bytes 196616 | tf_op jit(solution)/shard_map/ppermute | solution.py:43
  163.9 21.8 %collective-permute-start.5 = (bf16[128,256]{1,0:T(8,128)(2,1)S(1)}, bf16[128,256]{1,0:T(8,128)(2,1)S(1)}, u32[]{:S(2)}, u32[]{:S(2)}) collective-permute-start(bf16[128,256]{1,0:T(8,128)(2,1)S(1)} %get-tuple-element.41), channel_id=1, source_target_pairs={{0,6},{1,7},{2,8},{3,9},{4,10},{5,11},{6,12},{7,13},{8,14},{9,15},... | collective-permute-start | bytes 196616 | tf_op jit(solution)/shard_map/ppermute | solution.py:43
  168.2 22.2 %collective-permute-start.6 = (bf16[128,256]{1,0:T(8,128)(2,1)S(1)}, bf16[128,256]{1,0:T(8,128)(2,1)S(1)}, u32[]{:S(2)}, u32[]{:S(2)}) collective-permute-start(bf16[128,256]{1,0:T(8,128)(2,1)S(1)} %get-tuple-element.41), channel_id=1, source_target_pairs={{0,7},{1,8},{2,9},{3,10},{4,11},{5,12},{6,13},{7,14},{8,15},{9,16}... | collective-permute-start | bytes 196616 | tf_op jit(solution)/shard_map/ppermute | solution.py:43
  173.4 22.9 %collective-permute-start.21 = (bf16[128,256]{0,1:T(8,128)(2,1)S(1)}, bf16[128,256]{0,1:T(8,128)(2,1)S(1)}, u32[]{:S(2)}, u32[]{:S(2)}) collective-permute-start(bf16[128,256]{0,1:T(8,128)(2,1)S(1)} %bitcast.193), channel_id=1, source_target_pairs={{0,1},{1,2},{2,3},{3,4},{4,5},{5,6},{6,7},{7,8},{8,9},{9,10},{10,1... | collective-permute-start | bytes 196616 | tf_op jit(solution)/shard_map/ppermute | solution.py:43
  176.8 21.4 %collective-permute-start.22 = (bf16[128,256]{0,1:T(8,128)(2,1)S(1)}, bf16[128,256]{0,1:T(8,128)(2,1)S(1)}, u32[]{:S(2)}, u32[]{:S(2)}) collective-permute-start(bf16[128,256]{0,1:T(8,128)(2,1)S(1)} %bitcast.194), channel_id=1, source_target_pairs={{0,2},{1,3},{2,4},{3,5},{4,6},{5,7},{6,8},{7,9},{8,10},{9,11},{10,... | collective-permute-start | bytes 196616 | tf_op jit(solution)/shard_map/ppermute | solution.py:43
  181.7 20.5 collective-permute-start.23
  185.7 16.6 collective-permute-start.24
  190.4 11.9 collective-permute-start.25
  638.3 10.8 collective-permute-start.34
  639.6 11.4 collective-permute-start.33
  643.0 10.1 collective-permute-start.32
  644.9 9.5 collective-permute-start.31
  646.8 9.5 collective-permute-start.30
  653.1 9.2 collective-permute-start.41
  654.4 10.0 collective-permute-start.40
  656.3 10.1 collective-permute-start.39
  658.3 10.5 collective-permute-start.38
  660.2 9.2 collective-permute-start.37
  662.2 9.9 collective-permute-start.36
  682.8 490.0 %all-gather.11.cloned.1.call-start = ((), (), s32[]{:S(2)}) async-start(), calls=%async_computation.14 | async-start | bytes 34078720 | tf_op jit(solution)/shard_map/all_gather | solution.py:216
  683.4 821.3 %reduce-scatter.6.cloned.1.call-start = ((), (), s32[]{:S(2)}) async-start(), calls=%async_computation.12 | async-start | bytes 38338560 | tf_op jit(solution)/shard_map/reduce_scatter | solution.py:59
  727.0 1294.3 %reduce-scatter.8.cloned.1.call-start = ((), (), s32[]{:S(2)}) async-start(), calls=%async_computation.13 | async-start | bytes 93716480 | tf_op jit(solution)/shard_map/reduce_scatter | solution.py:219
  764.5 206.4 %all-to-all-start.3 = ((bf16[128,64,88]{0,2,1:T(8,128)(2,1)}), bf16[128,64,88]{0,2,1:T(8,128)(2,1)S(1)}, u32[]{:S(2)}, u32[]{:S(2)}) async-start(bf16[128,64,88]{0,2,1:T(8,128)(2,1)} %bitcast.159), calls=%async_computation.5 | async-start | bytes 2883584 | tf_op jit(solution)/shard_map/all_to_all | solution.py:212
  971.5 214.7 %all-to-all-start.5 = ((bf16[2,2,32]{2,1,0:T(2,128)(2,1)}), bf16[2,2,32]{2,1,0:T(2,128)(2,1)S(1)}, u32[]{:S(2)}, u32[]{:S(2)}) async-start(bf16[2,2,32]{2,1,0:T(2,128)(2,1)} %broadcast_in_dim.38), calls=%async_computation.7 | async-start | bytes 2048 | tf_op jit(solution)/shard_map/all_to_all | solution.py:48
  1187.2 34.7 %all-to-all-start.4 = ((bf16[2,88,2048]{2,1,0:T(8,128)(2,1)}), bf16[2,88,2048]{2,1,0:T(8,128)(2,1)S(1)}, u32[]{:S(2)}, u32[]{:S(2)}) async-start(bf16[2,88,2048]{2,1,0:T(8,128)(2,1)} %broadcast_in_dim.37), calls=%async_computation.6 | async-start | bytes 1441792 | tf_op jit(solution)/shard_map/all_to_all | solution.py:48
  1506.5 11.0 all-to-all-start.1
  1518.2 10.5 all-to-all-start
  2024.0 24.5 %all-to-all-start.2 = ((bf16[2,32,11264]{2,1,0:T(8,128)(2,1)}), bf16[2,32,11264]{2,1,0:T(8,128)(2,1)S(1)}, u32[]{:S(2)}, u32[]{:S(2)}) async-start(bf16[2,32,11264]{2,1,0:T(8,128)(2,1)} %broadcast_in_dim.36), calls=%async_computation.4 | async-start | bytes 2883584 | tf_op jit(solution)/shard_map/all_to_all | solution.py:48
  (48 other events, 3897.6 us)
Sparse Core Ops, SparseCore 0:
  11.0 127.1 all-gather.4
  140.4 262.9 all-gather.6
  405.7 140.0 all-gather.8
  682.9 287.2 reduce-scatter.9
  971.8 200.9 all-gather.10
  1175.2 329.4 reduce-scatter.5
  1507.2 514.0 reduce-scatter.7
where the time goes:
time: 2070 us; the launch traced here: 2060 us
  waiting for transfers between devices  1570 us (76%)
  matrix products  209 us (10%)
  starting transfers between devices  169 us (8%)
  other arithmetic  74.5 us (4%)
  local copies, waits for them, and re-layouts  24.5 us (1%)
    reduce_scatter x1, waiting for transfers between devices, on_device(): lax.psum_scatter(grad_gate_up, 'shard', scatter_dimension=0, tiled=True)  493 us
    reduce_scatter x1, waiting for transfers between devices, in_one_piece(): result = lax.psum_scatter(both, axis, scatter_dimension=dim, tiled=True)  283 us
    all_gather x1, waiting for transfers between devices, on_device(): lax.all_gather(cotangent, 'shard', axis=0, tiled=True)  197 us
    unnamed x8, waiting for transfers between devices  169 us
    all_gather x1, waiting for transfers between devices, on_device(): lax.all_gather(gate_local, 'shard', axis=0, tiled=True)  168 us
    ppermute x42, starting transfers between devices, shifted(): return lax.ppermute(x, axis, pairs)  122 us
    all_gather x1, waiting for transfers between devices, on_device(): lax.all_gather(down_local, 'shard', axis=0, tiled=True)  122 us
    all_gather x1, waiting for transfers between devices, rows_first(): result = lax.all_gather(both, axis, axis=0, tiled=True)  72.3 us
  transfers between devices with their start and end apart: 55, of which 18 were waited for; matrix products, arithmetic and copies ran while one was open for 9% of the time, Pallas kernels for 0%

commit v1 on v0

v1 whole, which is shorter than its diff:
```python
import jax
import jax.numpy as jnp
from jax import lax
from jax.experimental import pallas as pl
from jax.experimental.pallas import tpu as pltpu
from jax.sharding import PartitionSpec as P

HEADS = 32
KV_HEADS = 4
HEAD_DIM = 64
D = 2048
FF = 5632
STEP = 10
ROWS = 128
GROUP = 8
TOK = ROWS * GROUP
HALF = TOK // 2
HEADS_HERE = HEADS // GROUP
Q_HERE = HEADS_HERE * HEAD_DIM
PROJ_HERE = Q_HERE + 2 * HEAD_DIM
FF_HERE = FF // GROUP
Q_BLOCK = 256

EPSILON = 1e-05
BETA_ONE = 0.9
BETA_TWO = 0.95
ADAM_EPSILON = 1e-08
DECAY = 0.1
RATE_QKV = 0.02
RATE_OUT = 0.25
RATE_GATE_UP = 0.02
RATE_DOWN = 0.013
RATE_GAINS = 0.3

BF = jnp.bfloat16
F32 = jnp.float32
BOTH = ("rep", "shard")
LINES = [[8 * b + a for a in range(8)] for b in range(8)]
COLUMNS = [[16 * y + r for y in range(4)] for r in range(16)]


def index_of(r, y, z, x, c):
    return r * 64 + y * 16 + z * 8 + x * 2 + c


def places():
    return [
        (r, y, z, x, c)
        for r in range(2)
        for y in range(4)
        for z in range(2)
        for x in range(4)
        for c in range(2)
    ]


def come_from(v, y=0, x=0, c=0, zz=0):
    pairs = []
    for r, yy, z, xx, cc in places():
        ring = (2 * r + z + zz) % 4
        source = index_of(ring // 2, (yy + y) % 4, ring % 2, (xx + x) % 4, cc ^ c)
        pairs.append((source, index_of(r, yy, z, xx, cc)))
    return lax.ppermute(v, BOTH, pairs)


def turned(v):
    pairs = [(index_of(r, x, c, y, z), index_of(r, y, z, x, c)) for r, y, z, x, c in places()]
    return lax.ppermute(v, BOTH, pairs)


def dot(left, right):
    return jnp.dot(left, right, preferred_element_type=F32)


def dot_nt(left, right):
    return lax.dot_general(left, right, (((1,), (1,)), ((), ())), preferred_element_type=F32)


def dot_tn(left, right):
    return lax.dot_general(left, right, (((0,), (0,)), ((), ())), preferred_element_type=F32)


def line_gather(v):
    near = jnp.concatenate([v] + [come_from(v, x=k) for k in (1, 2, 3)], axis=0)
    return near, come_from(near, c=1)


def line_scatter(near, far, product):
    came = come_from(product(far).astype(BF), c=1)
    mine = product(near) + came.astype(F32)
    low = mine[ROWS:].astype(BF)
    total = mine[:ROWS]
    for k in (1, 2, 3):
        total = total + come_from(low[(k - 1) * ROWS : k * ROWS], x=-k).astype(F32)
    return total


def column_exchange(v):
    return lax.all_to_all(v, "shard", 0, 0, tiled=True, axis_index_groups=COLUMNS)


def plane_gather(v, axis):
    z = (lax.axis_index("shard") // 8) % 2
    column = column_exchange(jnp.broadcast_to(v[None], (4, *v.shape)))
    first, second = jnp.split(column, 2, axis=axis + 1)
    other = jnp.concatenate([come_from(first, zz=1), come_from(second, zz=3)], axis=axis + 1)
    full = jnp.where(
        z == 0, jnp.stack([column, other], axis=1), jnp.stack([other, column], axis=1)
    )
    return full.reshape(8 * v.shape[0], v.shape[1])


def plane_scatter(v, axis):
    z = (lax.axis_index("shard") // 8) % 2
    blocks = v.reshape(4, 2, v.shape[0] // 8, v.shape[1])
    mine = lax.dynamic_index_in_dim(blocks, z, 1, keepdims=False)
    theirs = lax.dynamic_index_in_dim(blocks, 1 - z, 1, keepdims=False)
    first, second = jnp.split(theirs, 2, axis=axis + 1)
    came = jnp.concatenate([come_from(first, zz=1), come_from(second, zz=3)], axis=axis + 1)
    total = (mine.astype(F32) + came.astype(F32)).astype(BF)
    result = jnp.sum(column_exchange(total).astype(F32), axis=0)
    return result + come_from(result.astype(BF), zz=2).astype(F32)


def line_exchange(v):
    return lax.all_to_all(v, "shard", 0, 0, tiled=True, axis_index_groups=LINES)


def rate_of(values):
    return lax.rsqrt(jnp.mean(values * values, axis=-1, keepdims=True) + EPSILON)


def unit_norm(values):
    return values * rate_of(values)


def unit_norm_back(values, grad):
    rate = rate_of(values)
    unit = values * rate
    return rate * (grad - unit * jnp.mean(grad * unit, axis=-1, keepdims=True))


def gated_unit(gate, upward):
    return jax.nn.silu(gate) * upward


def adam_step(weight, grad, first, second, rate):
    first_new = BETA_ONE * first + (1.0 - BETA_ONE) * grad
    second_new = BETA_TWO * second + (1.0 - BETA_TWO) * grad * grad
    first_hat = first_new / (1.0 - BETA_ONE**STEP)
    second_hat = second_new / (1.0 - BETA_TWO**STEP)
    weight_new = weight - rate * (
        first_hat / (jnp.sqrt(second_hat) + ADAM_EPSILON) + DECAY * weight
    )
    return (weight_new, first_new, second_new)


def lanes(rows):
    return lax.broadcasted_iota(jnp.int32, (rows, 128), 1)


def rotated(v, cosine, sine, lane):
    partner = jnp.where(lane % HEAD_DIM < HEAD_DIM // 2, pltpu.roll(v, 96, 1), pltpu.roll(v, 32, 1))
    return v * cosine + partner * sine


def split_pair(pair, k_ref, v_ref, lane):
    swapped = pltpu.roll(pair, 64, 1)
    low = lane < HEAD_DIM
    zero = jnp.zeros_like(pair)
    k_ref[0] = jnp.where(low, pair, zero).astype(BF)
    k_ref[1] = jnp.where(low, zero, swapped).astype(BF)
    v_ref[0] = jnp.where(low, swapped, zero).astype(BF)
    v_ref[1] = jnp.where(low, zero, pair).astype(BF)


def barred(column_ref, row_ref):
    same = column_ref[:, 0:1] == row_ref[0:1, :]
    before = row_ref[1:2, :] <= column_ref[:, 1:2]
    return jnp.where(same & before, 0.0, -1e30)


def forward_kernel(
    proj_ref, pair_ref, cos_ref, sin_ref, cos_all_ref, sin_all_ref, column_ref, row_ref,
    out_ref, q_ref, kv_ref, total_ref, k_scr, v_scr,
):
    lane = lanes(Q_BLOCK)

    @pl.when(pl.program_id(0) == 0)
    def _():
        wide = lanes(TOK)
        pair = pair_ref[...]
        turned_pair = rotated(pair, cos_all_ref[...], sin_all_ref[...], wide)
        pair = jnp.where(wide < HEAD_DIM, turned_pair, pair).astype(BF)
        kv_ref[...] = pair
        split_pair(pair.astype(F32), k_scr, v_scr, wide)

    bar = barred(column_ref, row_ref)
    totals = jnp.zeros((Q_BLOCK, 128), F32)
    for chunk in range(HEADS_HERE // 2):
        span = slice(128 * chunk, 128 * (chunk + 1))
        queries = rotated(proj_ref[:, span], cos_ref[...], sin_ref[...], lane).astype(BF)
        queries = (queries.astype(F32) * HEAD_DIM**-0.5).astype(BF)
        q_ref[:, span] = queries
        out = jnp.zeros((Q_BLOCK, 128), F32)
        for side in range(2):
            scores = dot_nt(queries, k_scr[side]) + bar
            peak = jnp.max(scores, axis=1, keepdims=True)
            expo = jnp.exp(scores - peak)
            total = jnp.sum(expo, axis=1, keepdims=True)
            probs = (expo * (1.0 / total)).astype(BF)
            out = out + dot(probs, v_scr[side])
            totals = jnp.where(lane == 2 * chunk + side, peak + jnp.log(total), totals)
        out_ref[:, span] = out.astype(BF)
    total_ref[...] = totals


def backward_kernel(
    do_ref, q_ref, kv_ref, total_ref, cos_ref, sin_ref, cos_all_ref, sin_all_ref, column_ref, row_ref,
    dq_ref, dkv_ref, k_scr, v_scr, dk_scr, dv_scr,
):
    lane = lanes(Q_BLOCK)
    step = pl.program_id(0)

    @pl.when(step == 0)
    def _():
        split_pair(kv_ref[...].astype(F32), k_scr, v_scr, lanes(TOK))
        dk_scr[...] = jnp.zeros_like(dk_scr)
        dv_scr[...] = jnp.zeros_like(dv_scr)

    bar = barred(column_ref, row_ref)
    for chunk in range(HEADS_HERE // 2):
        span = slice(128 * chunk, 128 * (chunk + 1))
        queries = q_ref[:, span]
        grads = do_ref[:, span]
        dq = jnp.zeros((Q_BLOCK, 128), F32)
        for side in range(2):
            held = (lane >= HEAD_DIM) == (side == 1)
            head = 2 * chunk + side
            scores = dot_nt(queries, k_scr[side]) + bar
            probs = jnp.exp(scores - total_ref[:, head : head + 1])
            dp = dot_nt(grads, v_scr[side])
            inner = jnp.sum(probs * dp, axis=1, keepdims=True)
            ds = (probs * (dp - inner)).astype(BF)
            dq = dq + dot(ds, k_scr[side])
            dk_scr[...] += dot_tn(ds, jnp.where(held, queries, jnp.zeros_like(queries)))
            dv_scr[...] += dot_tn(
                probs.astype(BF), jnp.where(held, grads, jnp.zeros_like(grads))
            )
        dq = dq * HEAD_DIM**-0.5
        dq_ref[:, span] = rotated(dq, cos_ref[...], -sin_ref[...], lane).astype(BF)

    @pl.when(step == pl.num_programs(0) - 1)
    def _():
        wide = lanes(TOK)
        dk = dk_scr[...] + pltpu.roll(dk_scr[...], 64, 1)
        dv = dv_scr[...] + pltpu.roll(dv_scr[...], 64, 1)
        dk = rotated(dk, cos_all_ref[...], -sin_all_ref[...], wide)
        dkv_ref[...] = jnp.where(wide < HEAD_DIM, dk, dv).astype(BF)


def blocked(cols):
    return pl.BlockSpec((Q_BLOCK, cols), lambda i: (i, 0))


def whole(rows, cols):
    return pl.BlockSpec((rows, cols), lambda i: (0, 0))


def attend(projected, cosine, sine, column, row):
    return pl.pallas_call(
        forward_kernel,
        grid=(TOK // Q_BLOCK,),
        in_specs=[
            blocked(Q_HERE),
            pl.BlockSpec((TOK, 128), lambda i: (0, Q_HERE // 128)),
            blocked(128),
            blocked(128),
            whole(TOK, 128),
            whole(TOK, 128),
            blocked(2),
            whole(2, TOK),
        ],
        out_specs=[blocked(Q_HERE), blocked(Q_HERE), whole(TOK, 128), blocked(128)],
        out_shape=[
            jax.ShapeDtypeStruct((TOK, Q_HERE), BF),
            jax.ShapeDtypeStruct((TOK, Q_HERE), BF),
            jax.ShapeDtypeStruct((TOK, 128), BF),
            jax.ShapeDtypeStruct((TOK, 128), F32),
        ],
        scratch_shapes=[pltpu.VMEM((2, TOK, 128), BF), pltpu.VMEM((2, TOK, 128), BF)],
        compiler_params=pltpu.CompilerParams(vmem_limit_bytes=40 * 2**20),
        cost_estimate=pl.CostEstimate(
            flops=8 * TOK * TOK * 128 * 2, bytes_accessed=6 * 2**20, transcendentals=4 * TOK * TOK
        ),
        name="attention_forward",
    )(projected, projected, cosine, sine, cosine, sine, column, row)


def attend_back(grads, queries, pair, totals, cosine, sine, column, row):
    return pl.pallas_call(
        backward_kernel,
        grid=(TOK // Q_BLOCK,),
        in_specs=[
            blocked(Q_HERE),
            blocked(Q_HERE),
            whole(TOK, 128),
            blocked(128),
            blocked(128),
            blocked(128),
            whole(TOK, 128),
            whole(TOK, 128),
            blocked(2),
            whole(2, TOK),
        ],
        out_specs=[blocked(Q_HERE), whole(TOK, 128)],
        out_shape=[
            jax.ShapeDtypeStruct((TOK, Q_HERE), BF),
            jax.ShapeDtypeStruct((TOK, 128), BF),
        ],
        scratch_shapes=[
            pltpu.VMEM((2, TOK, 128), BF),
            pltpu.VMEM((2, TOK, 128), BF),
            pltpu.VMEM((TOK, 128), F32),
            pltpu.VMEM((TOK, 128), F32),
        ],
        compiler_params=pltpu.CompilerParams(vmem_limit_bytes=40 * 2**20),
        cost_estimate=pl.CostEstimate(
            flops=20 * TOK * TOK * 128 * 2, bytes_accessed=6 * 2**20, transcendentals=4 * TOK * TOK
        ),
        name="attention_backward",
    )(grads, queries, pair, totals, cosine, sine, cosine, sine, column, row)


def small_rows(segment_ids, position_ids):
    parts = [position_ids // 32, position_ids % 32, segment_ids // 128, segment_ids % 128]
    flat = jnp.concatenate([p.astype(BF) for p in parts] + [jnp.zeros((256,), BF)])
    return jnp.concatenate([flat.reshape(2, PROJ_HERE), jnp.zeros((6, PROJ_HERE), BF)], axis=0)


def small_read(rows):
    s = lax.axis_index("shard")
    x, c = (s // 2) % 4, s % 2
    line = rows[:, :2].reshape(4, 2, 6, 128).astype(F32)
    line = lax.dynamic_slice(jnp.concatenate([line, line], axis=0), (x, 0, 0, 0), (4, 2, 6, 128))
    line = jnp.where(c == 0, line, line[:, ::-1]).transpose(1, 0, 2, 3).reshape(8, 6, 128)
    position = (line[:, 0] * 32.0 + line[:, 1]).reshape(TOK)
    segment = (line[:, 2] * 128.0 + line[:, 3]).reshape(TOK)
    return position, segment


def on_device(
    tokens,
    cotangent,
    segment_ids,
    position_ids,
    w_qkv,
    w_out,
    w_gate_up,
    w_down,
    gains,
    m_qkv,
    v_qkv,
    m_out,
    v_out,
    m_gate_up,
    v_gate_up,
    m_down,
    v_down,
    m_gains,
    v_gains,
):
    gain_rows = gains.astype(BF).astype(F32).T
    qkv_low = w_qkv.astype(BF).astype(F32)
    gate_low = w_gate_up.astype(BF).astype(F32)

    with jax.named_scope("qkv_weights_line"):
        low = (qkv_low * gain_rows[:, 0:1]).astype(BF)
        q_cols = low[:, :D].reshape(32, 8, Q_HERE)
        kv_cols = low[:, D:].reshape(32, 2, KV_HEADS, HEAD_DIM).transpose(0, 2, 1, 3)
        kv_cols = jnp.repeat(kv_cols.reshape(32, KV_HEADS, 2 * HEAD_DIM), 2, axis=1)
        qkv_cut = jnp.concatenate([q_cols, kv_cols], axis=2).transpose(1, 0, 2)
        small = jnp.broadcast_to(small_rows(segment_ids, position_ids)[None], (8, 8, PROJ_HERE))
        qkv_line = line_exchange(jnp.concatenate([qkv_cut, small], axis=1))
        positions, segments = small_read(qkv_line[:, 32:])
    with jax.named_scope("tokens_line"):
        tokens_halves = line_gather(tokens)
    with jax.named_scope("qkv_weights_plane"):
        qkv_full = plane_gather(qkv_line[:, :32].reshape(256, -1), 0)
    with jax.named_scope("out_down_turn"):
        out_down = turned(jnp.concatenate([w_out.astype(BF), w_down.astype(BF)], axis=0))
    with jax.named_scope("out_weights_plane"):
        out_full = plane_gather(out_down[:32], 1)
    with jax.named_scope("gate_weights_line"):
        low = (gate_low * gain_rows[:, 1:2]).astype(BF)
        gate_cut = low.reshape(32, 2, 8, FF_HERE).transpose(2, 0, 1, 3)
        gate_line = line_exchange(gate_cut.reshape(8, 32, -1)).reshape(256, -1)
    with jax.named_scope("gate_weights_plane"):
        gate_full = plane_gather(gate_line, 0)
    with jax.named_scope("down_weights_plane"):
        down_full = plane_gather(out_down[32:], 1)
    with jax.named_scope("cotangent_line"):
        cotangent_halves = line_gather(cotangent)

    freqs = 10000.0 ** (-jnp.arange(HEAD_DIM // 2).astype(F32) * 2.0 / HEAD_DIM)
    angles = positions[:, None] * freqs[None, :]
    cosine = jnp.tile(jnp.cos(angles), (1, 4))
    sine = jnp.sin(angles)
    sine = jnp.concatenate([-sine, sine, -sine, sine], axis=1)
    row = jnp.stack([segments, positions])
    column = row.T
    with jax.named_scope("projections"):
        normed = [unit_norm(t.astype(F32)).astype(BF) for t in tokens_halves]
        projected = jnp.concatenate([dot(n, qkv_full) for n in normed], axis=0)
    heads_out, queries, pair, totals = attend(projected, cosine, sine, column, row)
    inputs = tokens.astype(F32)
    with jax.named_scope("heads_out_line"):
        middle = inputs + line_scatter(
            heads_out[:HALF], heads_out[HALF:], lambda v: dot(v, out_full)
        )

    with jax.named_scope("normed_two_line"):
        normed_two = line_gather(unit_norm(middle).astype(BF))
    hidden, grad_gu = [], []
    for rows, grads in zip(normed_two, cotangent_halves):
        with jax.named_scope("feed_forward"):
            gate_up = dot(rows, gate_full)
            hid, back = jax.vjp(gated_unit, gate_up[:, :FF_HERE], gate_up[:, FF_HERE:])
            hidden.append(hid.astype(BF))
            grad_gu.append(jnp.concatenate(back(dot_nt(grads, down_full)), axis=1).astype(BF))
    with jax.named_scope("grad_normed_two_line"):
        grad_unit = line_scatter(*grad_gu, lambda v: dot_nt(v, gate_full))
        grad_middle = cotangent.astype(F32) + unit_norm_back(middle, grad_unit)
    with jax.named_scope("grad_attn_line"):
        grad_attn = line_gather(grad_middle.astype(BF))
    with jax.named_scope("mixed_line"):
        mixed = middle + line_scatter(*hidden, lambda v: dot(v, down_full))
    with jax.named_scope("grad_gate_plane"):
        grad_gate = dot_tn(jnp.concatenate(normed_two), jnp.concatenate(grad_gu)).astype(BF)
        grad_gate = plane_scatter(grad_gate, 0).astype(BF)
    with jax.named_scope("grad_gate_line"):
        grad_gate = line_exchange(grad_gate.reshape(8, 32, 2 * FF_HERE)).astype(F32)
        grad_gate = grad_gate.reshape(8, 32, 2, FF_HERE).transpose(1, 2, 0, 3).reshape(32, 2 * FF)
    with jax.named_scope("grad_down_plane"):
        grad_down = dot_tn(jnp.concatenate(hidden), jnp.concatenate(cotangent_halves)).astype(BF)
        grad_down = turned(plane_scatter(grad_down, 1).astype(BF)).astype(F32)

    with jax.named_scope("grad_heads"):
        grad_heads = jnp.concatenate([dot_nt(g, out_full) for g in grad_attn], axis=0).astype(BF)
    grad_q, grad_kv = attend_back(
        grad_heads, queries, pair, totals, cosine, sine, column, row
    )
    grad_proj = jnp.concatenate([grad_q, grad_kv], axis=1)
    with jax.named_scope("grad_normed_line"):
        grad_unit = line_scatter(grad_proj[:HALF], grad_proj[HALF:], lambda v: dot_nt(v, qkv_full))
        d_tokens = grad_middle + unit_norm_back(inputs, grad_unit)
    with jax.named_scope("grad_out_plane"):
        grad_out = dot_tn(heads_out, jnp.concatenate(grad_attn)).astype(BF)
        grad_out = turned(plane_scatter(grad_out, 1).astype(BF)).astype(F32)
    with jax.named_scope("grad_qkv_plane"):
        grad_qkv = dot_tn(jnp.concatenate(normed), grad_proj).astype(BF)
        grad_qkv = plane_scatter(grad_qkv, 0)
    with jax.named_scope("grad_qkv_line"):
        grad_qkv = line_exchange(grad_qkv.astype(BF).reshape(8, 32, -1)).astype(F32)
        q_part = grad_qkv[:, :, :Q_HERE].transpose(1, 0, 2).reshape(32, D)
        kv_part = grad_qkv[:, :, Q_HERE:].reshape(KV_HEADS, 2, 32, 2, HEAD_DIM).sum(axis=1)
        kv_part = kv_part.transpose(1, 2, 0, 3).reshape(32, 2 * KV_HEADS * HEAD_DIM)
        grad_qkv = jnp.concatenate([q_part, kv_part], axis=1)

    grad_gains = jnp.stack(
        [jnp.sum(qkv_low * grad_qkv, axis=1), jnp.sum(gate_low * grad_gate, axis=1)]
    )
    qkv_new = adam_step(w_qkv, grad_qkv * gain_rows[:, 0:1], m_qkv, v_qkv, RATE_QKV)
    out_new = adam_step(w_out, grad_out, m_out, v_out, RATE_OUT)
    gate_new = adam_step(w_gate_up, grad_gate * gain_rows[:, 1:2], m_gate_up, v_gate_up, RATE_GATE_UP)
    down_new = adam_step(w_down, grad_down, m_down, v_down, RATE_DOWN)
    gains_new = adam_step(gains, grad_gains, m_gains, v_gains, RATE_GAINS)
    return (mixed, d_tokens, *qkv_new, *out_new, *gate_new, *down_new, *gains_new)


def solution(mesh):
    tokens = P(BOTH, None)
    ids = P(BOTH)
    rows = P("shard", None)
    columns = P(None, "shard")
    return jax.shard_map(
        on_device,
        mesh=mesh,
        in_specs=(tokens, tokens, ids, ids, rows, rows, rows, rows, columns)
        + (rows,) * 8
        + (columns,) * 2,
        out_specs=(tokens, tokens) + (rows,) * 12 + (columns,) * 3,
        check_vma=False,
    )
```

time: 2070 us -> 598 us (0.29)
  waiting for transfers between devices: 1570 us -> 214 us
  matrix products: 209 us -> 76.9 us
  local copies, waits for them, and re-layouts: 24.5 us -> 64.4 us
  starting transfers between devices: 169 us -> 138 us
  Pallas kernels: 0 us -> 28.6 us
    reduce_scatter x2 -> x0, waiting for transfers between devices: 775 us -> none  [the longest x1 493 us: on_device(): lax.psum_scatter(grad_gate_up, 'shard', scatter_dimension=0, tiled=True)]
    all_gather x4 -> x0, waiting for transfers between devices: 559 us -> none  [the longest x1 197 us: on_device(): lax.all_gather(cotangent, 'shard', axis=0, tiled=True)]
    unnamed x8 -> x0, waiting for transfers between devices: 169 us -> none
    ppermute x42 -> x55, waiting for transfers between devices: 9.72 us -> 178 us  [the longest x52 140 us: come_from(): return lax.ppermute(v, BOTH, pairs)]
    dot_general x18 -> x20, matrix products: 209 us -> 76.9 us  [the longest x8 31.9 us: dot_nt(): lax.dot_general(left, right, (((1,), (1,)), ((), ())), preferred_element_...]
    ppermute x42 -> x55, starting transfers between devices: 122 us -> 81.4 us  [the longest x52 62.8 us: come_from(): return lax.ppermute(v, BOTH, pairs)]
    pallas_call x0 -> x2, Pallas kernels: none -> 28.6 us  [the longest x1 17.5 us: attend_back(): pl.pallas_call(backward_kernel, grid=(TOK // Q_BLOCK,), in_specs=[blocked...]
    concatenate x2 -> x10, other arithmetic: 25.4 us -> 4.38 us  [the longest x2 1.97 us: line_gather(): near = jnp.concatenate([v] + [come_from(v, x=k) for k in (1, 2, 3)], axis=0)]
  transfers between devices with their start and end apart: 55 -> 67, of which waited for: 18 -> 31; matrix products, arithmetic and copies ran while one was open for 9% -> 29% of each run, Pallas kernels for 0% -> 2%
where the time goes in v1:
time: 598 us; the launch traced here: 593 us
  waiting for transfers between devices  214 us (36%)
  starting transfers between devices  138 us (23%)
  matrix products  76.9 us (13%)
  other arithmetic  67.8 us (11%)
  local copies, waits for them, and re-layouts  64.4 us (11%)
  Pallas kernels  28.6 us (5%)
    ppermute x52, waiting for transfers between devices, come_from(): return lax.ppermute(v, BOTH, pairs)  140 us
    ppermute x52, starting transfers between devices, come_from(): return lax.ppermute(v, BOTH, pairs)  62.8 us
    ppermute x3, waiting for transfers between devices, turned(): return lax.ppermute(v, BOTH, pairs)  38.1 us
    all_to_all x8, starting transfers between devices, column_exchange(): lax.all_to_all(v, 'shard', 0, 0, tiled=True, axis_index_groups=COLUMNS)  33 us
    dot_general x8, matrix products, dot_nt(): lax.dot_general(left, right, (((1,), (1,)), ((), ())), preferred_element_...  31.9 us
    dot_general x8, matrix products, dot(): return jnp.dot(left, right, preferred_element_type=F32)  28.5 us
    all_to_all x8, waiting for transfers between devices, column_exchange(): lax.all_to_all(v, 'shard', 0, 0, tiled=True, axis_index_groups=COLUMNS)  24.7 us
    all_to_all x4, starting transfers between devices, line_exchange(): return lax.all_to_all(v, 'shard', 0, 0, tiled=True, axis_index_groups=LINES)  24 us
  transfers between devices with their start and end apart: 67, of which 31 were waited for; matrix products, arithmetic and copies ran while one was open for 29% of the time, Pallas kernels for 2%

profile of v1, /device:TPU:6, one launch (start us, length us, event | category | flops | bytes accessed | tf_op | source)
XLA Modules:
  0.0 592.8 jit_solution(675925060102068429)
XLA Ops:
  10.1 4.8 all-to-all-start
  15.8 4.5 collective-permute-start.6
  26.7 4.6 all-to-all-done
  36.3 28.5 %collective-permute-done.6 = bf16[120,2048]{1,0:T(8,128)(2,1)S(1)} collective-permute-done((bf16[120,2048]{1,0:T(8,128)(2,1)}, bf16[120,2048]{1,0:T(8,128)(2,1)S(1)}, u32[]{:S(2)}, u32[]{:S(2)}) %collective-permute-start.6) | collective-permute-done | bytes 491552 | tf_op jit(solution)/shard_map/out_down_turn/ppermute | solution.py:68
  91.6 5.5 all-to-all-done.1
  97.1 7.3 %all-to-all-start.3 = ((bf16[8,32,1408]{2,1,0:T(8,128)(2,1)}), bf16[8,32,1408]{2,1,0:T(8,128)(2,1)}, u32[]{:S(2)}, u32[]{:S(2)}) async-start(bf16[8,32,1408]{2,1,0:T(8,128)(2,1)} %reshape.279), calls=%async_computation.3 | async-start | bytes 1441792 | tf_op jit(solution)/shard_map/gate_weights_line/all_to_all | solution.py:126
  104.5 13.7 %collective-permute-start.3 = (bf16[4,128,384]{2,1,0:T(8,128)(2,1)S(1)}, bf16[4,128,384]{2,1,0:T(8,128)(2,1)S(1)}, u32[]{:S(2)}, u32[]{:S(2)}) collective-permute-start(bf16[4,128,384]{2,1,0:T(8,128)(2,1)S(1)} %get-tuple-element.86), channel_id=1, source_target_pairs={{8,0},{9,1},{10,2},{11,3},{12,4},{13,5},{14,6},{15,7},{64,8},{65,9... | collective-permute-start | bytes 1179656 | tf_op jit(solution)/shard_map/qkv_weights_plane/ppermute | solution.py:63
  119.3 7.8 %collective-permute-done.3 = bf16[4,128,384]{2,1,0:T(8,128)(2,1)S(1)} collective-permute-done((bf16[4,128,384]{2,1,0:T(8,128)(2,1)S(1)}, bf16[4,128,384]{2,1,0:T(8,128)(2,1)S(1)}, u32[]{:S(2)}, u32[]{:S(2)}) %collective-permute-start.3) | collective-permute-done | bytes 393248 | tf_op jit(solution)/shard_map/qkv_weights_plane/ppermute | solution.py:63
  132.1 4.3 all-to-all-start.5
  136.4 3.7 fusion.102
  145.7 9.6 %all-to-all-done.5 = bf16[4,88,2048]{2,1,0:T(8,128)(2,1)} async-done(((bf16[4,88,2048]{2,1,0:T(8,128)(2,1)}), bf16[4,88,2048]{2,1,0:T(8,128)(2,1)}, u32[]{:S(2)}, u32[]{:S(2)}) %all-to-all-start.5) | async-done | bytes 1441824 | tf_op jit(solution)/shard_map/down_weights_plane/all_to_all | solution.py:99
  158.1 4.6 all-to-all-start.4
  165.8 11.0 %attention_forward.1 = (bf16[1024,256]{1,0:T(8,128)(2,1)S(1)}, bf16[1024,256]{1,0:T(8,128)(2,1)S(1)}, bf16[1024,128]{1,0:T(8,128)(2,1)S(1)}, f32[1024,128]{1,0:T(8,128)S(1)}) custom-call(f32[1024,384]{1,0:T(8,128)S(1)} %pad_maximum_fusion.2.proj_ref.pair_ref, f32[1024,384]{1,0:T(8,128)S(1)} %pad_maximum_fusion.2.proj_ref.pair_ref, ...), custom_call_target="tpu_custom_call" | custom-call | flops 2147483648 | bytes 6291456 | tf_op jit(solution)/shard_map/attention_forward/pallas_call | solution.py:271
  188.9 10.0 %collective-permute-done.18 = bf16[4,88,1024]{2,1,0:T(8,128)(2,1)S(1)} collective-permute-done((bf16[4,88,1024]{2,1,0:T(8,128)(2,1)S(1)}, bf16[4,88,1024]{2,1,0:T(8,128)(2,1)S(1)}, u32[]{:S(2)}, u32[]{:S(2)}) %collective-permute-start.18) | collective-permute-done | bytes 720928 | tf_op jit(solution)/shard_map/down_weights_plane/ppermute | solution.py:63
  218.4 19.4 %collective-permute-done.16 = bf16[4,128,1408]{2,1,0:T(8,128)(2,1)S(1)} collective-permute-done((bf16[4,128,1408]{2,1,0:T(8,128)(2,1)S(1)}, bf16[4,128,1408]{2,1,0:T(8,128)(2,1)S(1)}, u32[]{:S(2)}, u32[]{:S(2)}) %collective-permute-start.16) | collective-permute-done | bytes 1441824 | tf_op jit(solution)/shard_map/gate_weights_plane/ppermute | solution.py:63
  244.4 4.1 maximum_select_fusion
  248.5 7.7 %collective-permute-done.15 = bf16[128,2048]{1,0:T(8,128)(2,1)S(1)} collective-permute-done((bf16[128,2048]{1,0:T(8,128)(2,1)S(1)}, bf16[128,2048]{1,0:T(8,128)(2,1)S(1)}, u32[]{:S(2)}, u32[]{:S(2)}) %collective-permute-start.15) | collective-permute-done | bytes 524320 | tf_op jit(solution)/shard_map/normed_two_line/ppermute | solution.py:63
  258.5 8.4 %collective-permute-done.13 = bf16[128,2048]{1,0:T(8,128)(2,1)S(1)} collective-permute-done((bf16[128,2048]{1,0:T(8,128)(2,1)S(1)}, bf16[128,2048]{1,0:T(8,128)(2,1)S(1)}, u32[]{:S(2)}, u32[]{:S(2)}) %collective-permute-start.13) | collective-permute-done | bytes 524320 | tf_op jit(solution)/shard_map/normed_two_line/ppermute | solution.py:63
  271.2 4.0 fusion.18
  279.1 4.0 fusion.21
  292.6 4.7 convolution_convert_fusion.5
  298.1 7.1 %convolution_convert_fusion = bf16[2048,1408]{1,0:T(8,128)(2,1)S(1)} fusion(bf16[1024,2048]{1,0:T(8,128)(2,1)S(1)} %constant_dynamic-update-slice_fusion.17, bf16[512,1408]{1,0:T(8,128)(2,1)S(1)} %pad_maximum_fusion.4, bf16[512,1408]{1,0:T(8,128)(2,1)S(1)} %pad_maximum_fusion.3), kind=kOutput, calls=%fused_computation | convolution fusion | flops 5914230784 | bytes 12845056 | tf_op jit(solution)/shard_map/grad_gate_plane/dot_general | solution.py:80
  313.2 4.7 all-to-all-start.11
  317.9 6.5 %fusion.87 = (bf16[512,2048]{1,0:T(8,128)(2,1)S(1)}, f32[512,2048]{1,0:T(8,128)}) fusion(bf16[512,2048]{1,0:T(8,128)(2,1)} %collective-permute-done.21, bf16[512,704]{1,0:T(8,128)(2,1)} %copy-done.38, bf16[704,2048]{1,0:T(8,128)(2,1)} %bitcast.121), kind=kOutput, calls=%fused_computation.224 | convolution fusion | flops 1479540736 | bytes 11993088 | tf_op jit(solution)/shard_map/mixed_line/dot_general | solution.py:72
  329.3 8.1 %fusion.86 = (bf16[512,2048]{1,0:T(8,128)(2,1)S(1)}, f32[512,2048]{1,0:T(8,128)}) fusion(bf16[512,2048]{1,0:T(8,128)(2,1)} %collective-permute-done.29, bf16[512,1408]{1,0:T(8,128)(2,1)S(1)} %copy-done.34, bf16[2048,1408]{1,0:T(8,128)(2,1)} %bitcast.131), kind=kOutput, calls=%fused_computation.223 | convolution fusion | flops 2955935744 | bytes 15597568 | tf_op jit(solution)/shard_map/grad_normed_two_line/dot_general | solution.py:76
  338.6 4.8 collective-permute-done.48
  349.3 4.2 fusion
  353.5 4.7 all-to-all-start.9
  365.0 9.3 %collective-permute-done.31 = bf16[128,2048]{1,0:T(8,128)(2,1)} collective-permute-done((bf16[128,2048]{1,0:T(8,128)(2,1)}, bf16[128,2048]{1,0:T(8,128)(2,1)}, u32[]{:S(2)}, u32[]{:S(2)}) %collective-permute-start.31) | collective-permute-done | bytes 524320 | tf_op jit(solution)/shard_map/grad_normed_two_line/ppermute | solution.py:63
  374.3 4.0 multiply_reduce_fusion
  378.3 3.6 constant_dynamic-update-slice_fusion.16
  385.9 6.1 %collective-permute-start.54 = (bf16[88,2048]{1,0:T(8,128)(2,1)}, bf16[88,2048]{1,0:T(8,128)(2,1)}, u32[]{:S(2)}, u32[]{:S(2)}) collective-permute-start(bf16[88,2048]{1,0:T(8,128)(2,1)} %add_convert_fusion.1), channel_id=1, source_target_pairs={{0,0},{8,1},{16,2},{24,3},{32,4},{40,5},{48,6},{56,7},{1,8},{9,9},... | collective-permute-start | bytes 1081352 | tf_op jit(solution)/shard_map/grad_down_plane/ppermute | solution.py:68
  392.0 19.3 %collective-permute-done.35 = bf16[128,2048]{1,0:T(8,128)(2,1)S(1)} collective-permute-done((bf16[128,2048]{1,0:T(8,128)(2,1)S(1)}, bf16[128,2048]{1,0:T(8,128)(2,1)S(1)}, u32[]{:S(2)}, u32[]{:S(2)}) %collective-permute-start.35) | collective-permute-done | bytes 524320 | tf_op jit(solution)/shard_map/grad_attn_line/ppermute | solution.py:63
  415.8 9.6 %collective-permute-done.54 = bf16[88,2048]{1,0:T(8,128)(2,1)} collective-permute-done((bf16[88,2048]{1,0:T(8,128)(2,1)}, bf16[88,2048]{1,0:T(8,128)(2,1)}, u32[]{:S(2)}, u32[]{:S(2)}) %collective-permute-start.54) | collective-permute-done | bytes 360480 | tf_op jit(solution)/shard_map/grad_down_plane/ppermute | solution.py:68
  429.0 9.7 %collective-permute-done.50 = bf16[256,1408]{1,0:T(8,128)(2,1)S(1)} collective-permute-done((bf16[256,1408]{1,0:T(8,128)(2,1)S(1)}, bf16[256,1408]{1,0:T(8,128)(2,1)S(1)}, u32[]{:S(2)}, u32[]{:S(2)}) %collective-permute-start.50) | collective-permute-done | bytes 720928 | tf_op jit(solution)/shard_map/grad_gate_plane/ppermute | solution.py:63
  439.6 6.2 %all-to-all-start.10 = ((bf16[8,32,1408]{2,1,0:T(8,128)(2,1)}), bf16[8,32,1408]{2,1,0:T(8,128)(2,1)}, u32[]{:S(2)}, u32[]{:S(2)}) async-start(bf16[8,32,1408]{2,1,0:T(8,128)(2,1)} %bitcast.140), calls=%async_computation.10 | async-start | bytes 1441792 | tf_op jit(solution)/shard_map/grad_gate_line/all_to_all | solution.py:126
  459.7 3.6 copy.130
  469.3 3.5 convolution_convert_fusion.6
  475.4 17.5 %attention_backward.1 = (bf16[1024,256]{1,0:T(8,128)(2,1)S(1)}, bf16[1024,128]{1,0:T(8,128)(2,1)S(1)}) custom-call(bf16[1024,256]{1,0:T(8,128)(2,1)S(1)} %pad_maximum_fusion.6.do_ref, bf16[1024,256]{1,0:T(8,128)(2,1)S(1)} %get-tuple-element.24.q_ref, bf16[1024,128]{1,0:T(8,128)(2,1)S(1)} %get-tuple-element.25.kv_ref, ...), custom_call_target="tpu_custom_call" | custom-call | flops 5368709120 | bytes 6291456 | tf_op jit(solution)/shard_map/attention_backward/pallas_call | solution.py:301
  495.7 5.2 collective-permute-start.44
  507.6 3.6 collective-permute-done.45
  523.6 4.2 all-to-all-start.6
  527.9 5.3 multiply_subtract_fusion
  533.4 4.9 all-to-all-done.6
  539.9 8.0 %collective-permute-start.47 = (bf16[32,2048]{1,0:T(8,128)(2,1)S(1)}, bf16[32,2048]{1,0:T(8,128)(2,1)S(1)}, u32[]{:S(2)}, u32[]{:S(2)}) collective-permute-start(bf16[32,2048]{1,0:T(8,128)(2,1)S(1)} %add_convert_fusion.3), channel_id=1, source_target_pairs={{0,0},{8,1},{16,2},{24,3},{32,4},{40,5},{48,6},{56,7},{1,8},{9,9},... | collective-permute-start | bytes 393224 | tf_op jit(solution)/shard_map/grad_out_plane/ppermute | solution.py:68
  548.6 5.6 all-to-all-start.7
  555.3 3.7 all-to-all-done.7
  569.1 18.2 %collective-permute-done.38 = bf16[128,2048]{1,0:T(8,128)(2,1)S(1)} collective-permute-done((bf16[128,2048]{1,0:T(8,128)(2,1)S(1)}, bf16[128,2048]{1,0:T(8,128)(2,1)S(1)}, u32[]{:S(2)}, u32[]{:S(2)}) %collective-permute-start.38) | collective-permute-done | bytes 524320 | tf_op jit(solution)/shard_map/grad_normed_line/ppermute | solution.py:63
  (380 shorter events, 227.0 us)
Async XLA Ops:
  0.7 70.5 %collective-permute-start.1 = (bf16[128,2048]{1,0:T(8,128)(2,1)}, bf16[128,2048]{1,0:T(8,128)(2,1)}, u32[]{:S(2)}, u32[]{:S(2)}) collective-permute-start(bf16[128,2048]{1,0:T(8,128)(2,1)} %param.19), channel_id=1, source_target_pairs={{4,0},{5,1},{6,2},{7,3},{0,4},{1,5},{2,6},{3,7},{12,8},{13,9},{14,... | collective-permute-start | bytes 1572872 | tf_op jit(solution)/shard_map/tokens_line/ppermute | solution.py:63
  2.2 67.1 %collective-permute-start = (bf16[128,2048]{1,0:T(8,128)(2,1)}, bf16[128,2048]{1,0:T(8,128)(2,1)}, u32[]{:S(2)}, u32[]{:S(2)}) collective-permute-start(bf16[128,2048]{1,0:T(8,128)(2,1)} %param.19), channel_id=1, source_target_pairs={{2,0},{3,1},{4,2},{5,3},{6,4},{7,5},{0,6},{1,7},{10,8},{11,9},{12,... | collective-permute-start | bytes 1572872 | tf_op jit(solution)/shard_map/tokens_line/ppermute | solution.py:63
  2.2 70.9 %collective-permute-start.2 = (bf16[128,2048]{1,0:T(8,128)(2,1)}, bf16[128,2048]{1,0:T(8,128)(2,1)}, u32[]{:S(2)}, u32[]{:S(2)}) collective-permute-start(bf16[128,2048]{1,0:T(8,128)(2,1)} %param.19), channel_id=1, source_target_pairs={{6,0},{7,1},{0,2},{1,3},{2,4},{3,5},{4,6},{5,7},{14,8},{15,9},{8,1... | collective-permute-start | bytes 1572872 | tf_op jit(solution)/shard_map/tokens_line/ppermute | solution.py:63
  10.1 21.2 %all-to-all-start = ((bf16[8,40,384]{2,1,0:T(8,128)(2,1)}), bf16[8,40,384]{2,1,0:T(8,128)(2,1)}, u32[]{:S(2)}, u32[]{:S(2)}) async-start(bf16[8,40,384]{2,1,0:T(8,128)(2,1)} %copy.113), calls=%async_computation | async-start | bytes 491520 | tf_op jit(solution)/shard_map/qkv_weights_line/all_to_all | solution.py:126
  15.8 48.9 %collective-permute-start.6 = (bf16[120,2048]{1,0:T(8,128)(2,1)}, bf16[120,2048]{1,0:T(8,128)(2,1)S(1)}, u32[]{:S(2)}, u32[]{:S(2)}) collective-permute-start(bf16[120,2048]{1,0:T(8,128)(2,1)} %pad_maximum_fusion.7), channel_id=1, source_target_pairs={{0,0},{8,1},{16,2},{24,3},{32,4},{40,5},{48,6},{56,7},{1,8},{9,9},... | collective-permute-start | bytes 1474568 | tf_op jit(solution)/shard_map/out_down_turn/ppermute | solution.py:68
  20.3 164.3 %collective-permute-start.26 = (bf16[128,2048]{1,0:T(8,128)(2,1)}, bf16[128,2048]{1,0:T(8,128)(2,1)}, u32[]{:S(2)}, u32[]{:S(2)}) collective-permute-start(bf16[128,2048]{1,0:T(8,128)(2,1)} %param.20), channel_id=1, source_target_pairs={{4,0},{5,1},{6,2},{7,3},{0,4},{1,5},{2,6},{3,7},{12,8},{13,9},{14,... | collective-permute-start | bytes 1572872 | tf_op jit(solution)/shard_map/cotangent_line/ppermute | solution.py:63
  64.8 117.3 %collective-permute-start.25 = (bf16[128,2048]{1,0:T(8,128)(2,1)}, bf16[128,2048]{1,0:T(8,128)(2,1)}, u32[]{:S(2)}, u32[]{:S(2)}) collective-permute-start(bf16[128,2048]{1,0:T(8,128)(2,1)} %param.20), channel_id=1, source_target_pairs={{2,0},{3,1},{4,2},{5,3},{6,4},{7,5},{0,6},{1,7},{10,8},{11,9},{12,... | collective-permute-start | bytes 1572872 | tf_op jit(solution)/shard_map/cotangent_line/ppermute | solution.py:63
  75.0 65.2 %collective-permute-start.5 = (bf16[512,2048]{1,0:T(8,128)(2,1)}, bf16[512,2048]{1,0:T(8,128)(2,1)}, u32[]{:S(2)}, u32[]{:S(2)}) collective-permute-start(bf16[512,2048]{1,0:T(8,128)(2,1)} %constant_dynamic-update-slice_fusion), channel_id=1, source_target_pairs={{1,0},{0,1},{3,2},{2,3},{5,4},{4,5},{7,6},{6,7},{9,8},{8,9},{11,10... | collective-permute-start | bytes 6291464 | tf_op jit(solution)/shard_map/tokens_line/ppermute | solution.py:63
  85.2 19.3 %collective-permute-start.7 = (bf16[4,32,1024]{2,1,0:T(8,128)(2,1)}, bf16[4,32,1024]{2,1,0:T(8,128)(2,1)S(1)}, u32[]{:S(2)}, u32[]{:S(2)}) collective-permute-start(bf16[4,32,1024]{2,1,0:T(8,128)(2,1)} %get-tuple-element.100), channel_id=1, source_target_pairs={{8,0},{9,1},{10,2},{11,3},{12,4},{13,5},{14,6},{15,7},{64,8},{65,9... | collective-permute-start | bytes 786440 | tf_op jit(solution)/shard_map/out_weights_plane/ppermute | solution.py:63
  88.3 29.9 %collective-permute-start.8 = (bf16[4,32,1024]{2,1,0:T(8,128)(2,1)}, bf16[4,32,1024]{2,1,0:T(8,128)(2,1)S(1)}, u32[]{:S(2)}, u32[]{:S(2)}) collective-permute-start(bf16[4,32,1024]{2,1,0:T(8,128)(2,1)} %get-tuple-element.101), channel_id=1, source_target_pairs={{72,0},{73,1},{74,2},{75,3},{76,4},{77,5},{78,6},{79,7},{0,8},{1,9... | collective-permute-start | bytes 786440 | tf_op jit(solution)/shard_map/out_weights_plane/ppermute | solution.py:63
  97.1 33.5 %all-to-all-start.3 = ((bf16[8,32,1408]{2,1,0:T(8,128)(2,1)}), bf16[8,32,1408]{2,1,0:T(8,128)(2,1)}, u32[]{:S(2)}, u32[]{:S(2)}) async-start(bf16[8,32,1408]{2,1,0:T(8,128)(2,1)} %reshape.279), calls=%async_computation.3 | async-start | bytes 1441792 | tf_op jit(solution)/shard_map/gate_weights_line/all_to_all | solution.py:126
  104.5 22.6 %collective-permute-start.3 = (bf16[4,128,384]{2,1,0:T(8,128)(2,1)S(1)}, bf16[4,128,384]{2,1,0:T(8,128)(2,1)S(1)}, u32[]{:S(2)}, u32[]{:S(2)}) collective-permute-start(bf16[4,128,384]{2,1,0:T(8,128)(2,1)S(1)} %get-tuple-element.86), channel_id=1, source_target_pairs={{8,0},{9,1},{10,2},{11,3},{12,4},{13,5},{14,6},{15,7},{64,8},{65,9... | collective-permute-start | bytes 1179656 | tf_op jit(solution)/shard_map/qkv_weights_plane/ppermute | solution.py:63
  127.1 59.7 %collective-permute-start.27 = (bf16[128,2048]{1,0:T(8,128)(2,1)}, bf16[128,2048]{1,0:T(8,128)(2,1)}, u32[]{:S(2)}, u32[]{:S(2)}) collective-permute-start(bf16[128,2048]{1,0:T(8,128)(2,1)} %param.20), channel_id=1, source_target_pairs={{6,0},{7,1},{0,2},{1,3},{2,4},{3,5},{4,6},{5,7},{14,8},{15,9},{8,1... | collective-permute-start | bytes 1572872 | tf_op jit(solution)/shard_map/cotangent_line/ppermute | solution.py:63
  132.1 23.1 %all-to-all-start.5 = ((bf16[4,88,2048]{2,1,0:T(8,128)(2,1)}), bf16[4,88,2048]{2,1,0:T(8,128)(2,1)}, u32[]{:S(2)}, u32[]{:S(2)}) async-start(bf16[4,88,2048]{2,1,0:T(8,128)(2,1)} %broadcast_in_dim.26), calls=%async_computation.5 | async-start | bytes 2883584 | tf_op jit(solution)/shard_map/down_weights_plane/all_to_all | solution.py:99
  158.1 44.7 %all-to-all-start.4 = ((bf16[4,256,1408]{2,1,0:T(8,128)(2,1)}), bf16[4,256,1408]{2,1,0:T(8,128)(2,1)}, u32[]{:S(2)}, u32[]{:S(2)}) async-start(bf16[4,256,1408]{2,1,0:T(8,128)(2,1)} %broadcast_in_dim.25), calls=%async_computation.4 | async-start | bytes 5767168 | tf_op jit(solution)/shard_map/gate_weights_plane/all_to_all | solution.py:99
  178.9 30.4 %collective-permute-start.9 = (bf16[512,2048]{1,0:T(8,128)(2,1)}, bf16[512,2048]{1,0:T(8,128)(2,1)}, u32[]{:S(2)}, u32[]{:S(2)}) collective-permute-start(bf16[512,2048]{1,0:T(8,128)(2,1)} %convolution_convert_fusion.2), channel_id=1, source_target_pairs={{1,0},{0,1},{3,2},{2,3},{5,4},{4,5},{7,6},{6,7},{9,8},{8,9},{11,10... | collective-permute-start | bytes 6291464 | tf_op jit(solution)/shard_map/heads_out_line/ppermute | solution.py:63
  182.1 19.5 %collective-permute-start.19 = (bf16[4,88,1024]{2,1,0:T(8,128)(2,1)S(1)}, bf16[4,88,1024]{2,1,0:T(8,128)(2,1)S(1)}, u32[]{:S(2)}, u32[]{:S(2)}) collective-permute-start(bf16[4,88,1024]{2,1,0:T(8,128)(2,1)S(1)} %get-tuple-element.81), channel_id=1, source_target_pairs={{72,0},{73,1},{74,2},{75,3},{76,4},{77,5},{78,6},{79,7},{0,8},{1,9... | collective-permute-start | bytes 2162696 | tf_op jit(solution)/shard_map/down_weights_plane/ppermute | solution.py:63
  188.9 26.0 %collective-permute-start.28 = (bf16[512,2048]{1,0:T(8,128)(2,1)}, bf16[512,2048]{1,0:T(8,128)(2,1)}, u32[]{:S(2)}, u32[]{:S(2)}) collective-permute-start(bf16[512,2048]{1,0:T(8,128)(2,1)} %get-tuple-element.90), channel_id=1, source_target_pairs={{1,0},{0,1},{3,2},{2,3},{5,4},{4,5},{7,6},{6,7},{9,8},{8,9},{11,10... | collective-permute-start | bytes 6291464 | tf_op jit(solution)/shard_map/cotangent_line/ppermute | solution.py:63
  204.9 33.0 %collective-permute-start.16 = (bf16[4,128,1408]{2,1,0:T(8,128)(2,1)S(1)}, bf16[4,128,1408]{2,1,0:T(8,128)(2,1)S(1)}, u32[]{:S(2)}, u32[]{:S(2)}) collective-permute-start(bf16[4,128,1408]{2,1,0:T(8,128)(2,1)S(1)} %get-tuple-element.64), channel_id=1, source_target_pairs={{8,0},{9,1},{10,2},{11,3},{12,4},{13,5},{14,6},{15,7},{64,8},{65,9... | collective-permute-start | bytes 4325384 | tf_op jit(solution)/shard_map/gate_weights_plane/ppermute | solution.py:63
  205.2 34.1 %collective-permute-start.17 = (bf16[4,128,1408]{2,1,0:T(8,128)(2,1)S(1)}, bf16[4,128,1408]{2,1,0:T(8,128)(2,1)S(1)}, u32[]{:S(2)}, u32[]{:S(2)}) collective-permute-start(bf16[4,128,1408]{2,1,0:T(8,128)(2,1)S(1)} %get-tuple-element.65), channel_id=1, source_target_pairs={{72,0},{73,1},{74,2},{75,3},{76,4},{77,5},{78,6},{79,7},{0,8},{1,9... | collective-permute-start | bytes 4325384 | tf_op jit(solution)/shard_map/gate_weights_plane/ppermute | solution.py:63
  212.9 26.7 %collective-permute-start.10 = (bf16[128,2048]{1,0:T(8,128)(2,1)S(1)}, bf16[128,2048]{1,0:T(8,128)(2,1)S(1)}, u32[]{:S(2)}, u32[]{:S(2)}) collective-permute-start(bf16[128,2048]{1,0:T(8,128)(2,1)S(1)} %get-tuple-element.75), channel_id=1, source_target_pairs={{6,0},{7,1},{0,2},{1,3},{2,4},{3,5},{4,6},{5,7},{14,8},{15,9},{8,1... | collective-permute-start | bytes 1572872 | tf_op jit(solution)/shard_map/heads_out_line/ppermute | solution.py:63
  213.6 26.0 %collective-permute-start.12 = (bf16[128,2048]{1,0:T(8,128)(2,1)S(1)}, bf16[128,2048]{1,0:T(8,128)(2,1)S(1)}, u32[]{:S(2)}, u32[]{:S(2)}) collective-permute-start(bf16[128,2048]{1,0:T(8,128)(2,1)S(1)} %get-tuple-element.76), channel_id=1, source_target_pairs={{2,0},{3,1},{4,2},{5,3},{6,4},{7,5},{0,6},{1,7},{10,8},{11,9},{12,... | collective-permute-start | bytes 1572872 | tf_op jit(solution)/shard_map/heads_out_line/ppermute | solution.py:63
  215.0 24.7 %collective-permute-start.11 = (bf16[128,2048]{1,0:T(8,128)(2,1)S(1)}, bf16[128,2048]{1,0:T(8,128)(2,1)S(1)}, u32[]{:S(2)}, u32[]{:S(2)}) collective-permute-start(bf16[128,2048]{1,0:T(8,128)(2,1)S(1)} %get-tuple-element.77), channel_id=1, source_target_pairs={{4,0},{5,1},{6,2},{7,3},{0,4},{1,5},{2,6},{3,7},{12,8},{13,9},{14,... | collective-permute-start | bytes 1572872 | tf_op jit(solution)/shard_map/heads_out_line/ppermute | solution.py:63
  244.3 22.6 %collective-permute-start.13 = (bf16[128,2048]{1,0:T(8,128)(2,1)S(1)}, bf16[128,2048]{1,0:T(8,128)(2,1)S(1)}, u32[]{:S(2)}, u32[]{:S(2)}) collective-permute-start(bf16[128,2048]{1,0:T(8,128)(2,1)S(1)} %get-tuple-element.39), channel_id=1, source_target_pairs={{2,0},{3,1},{4,2},{5,3},{6,4},{7,5},{0,6},{1,7},{10,8},{11,9},{12,... | collective-permute-start | bytes 1572872 | tf_op jit(solution)/shard_map/normed_two_line/ppermute | solution.py:63
  289.9 21.6 %collective-permute-start.51 = (bf16[4,88,1024]{2,1,0:T(8,128)(2,1)S(1)}, bf16[4,88,1024]{2,1,0:T(8,128)(2,1)S(1)}, u32[]{:S(2)}, u32[]{:S(2)}) collective-permute-start(bf16[4,88,1024]{2,1,0:T(8,128)(2,1)S(1)} %get-tuple-element.78), channel_id=1, source_target_pairs={{8,0},{9,1},{10,2},{11,3},{12,4},{13,5},{14,6},{15,7},{64,8},{65,9... | collective-permute-start | bytes 2162696 | tf_op jit(solution)/shard_map/grad_down_plane/ppermute | solution.py:63
  290.7 20.9 %collective-permute-start.52 = (bf16[4,88,1024]{2,1,0:T(8,128)(2,1)S(1)}, bf16[4,88,1024]{2,1,0:T(8,128)(2,1)S(1)}, u32[]{:S(2)}, u32[]{:S(2)}) collective-permute-start(bf16[4,88,1024]{2,1,0:T(8,128)(2,1)S(1)} %get-tuple-element.79), channel_id=1, source_target_pairs={{72,0},{73,1},{74,2},{75,3},{76,4},{77,5},{78,6},{79,7},{0,8},{1,9... | collective-permute-start | bytes 2162696 | tf_op jit(solution)/shard_map/grad_down_plane/ppermute | solution.py:63
  297.3 20.6 %collective-permute-start.21 = (bf16[512,2048]{1,0:T(8,128)(2,1)}, bf16[512,2048]{1,0:T(8,128)(2,1)}, u32[]{:S(2)}, u32[]{:S(2)}) collective-permute-start(bf16[512,2048]{1,0:T(8,128)(2,1)} %convolution_convert_fusion.4), channel_id=1, source_target_pairs={{1,0},{0,1},{3,2},{2,3},{5,4},{4,5},{7,6},{6,7},{9,8},{8,9},{11,10... | collective-permute-start | bytes 6291464 | tf_op jit(solution)/shard_map/mixed_line/ppermute | solution.py:63
  297.3 30.2 %collective-permute-start.29 = (bf16[512,2048]{1,0:T(8,128)(2,1)}, bf16[512,2048]{1,0:T(8,128)(2,1)}, u32[]{:S(2)}, u32[]{:S(2)}) collective-permute-start(bf16[512,2048]{1,0:T(8,128)(2,1)} %convolution_convert_fusion.5), channel_id=1, source_target_pairs={{1,0},{0,1},{3,2},{2,3},{5,4},{4,5},{7,6},{6,7},{9,8},{8,9},{11,10... | collective-permute-start | bytes 6291464 | tf_op jit(solution)/shard_map/grad_normed_two_line/ppermute | solution.py:63
  309.6 33.8 %collective-permute-start.48 = (bf16[4,128,1408]{2,1,0:T(8,128)(2,1)}, bf16[4,128,1408]{2,1,0:T(8,128)(2,1)}, u32[]{:S(2)}, u32[]{:S(2)}) collective-permute-start(bf16[4,128,1408]{2,1,0:T(8,128)(2,1)} %get-tuple-element.60), channel_id=1, source_target_pairs={{8,0},{9,1},{10,2},{11,3},{12,4},{13,5},{14,6},{15,7},{64,8},{65,9... | collective-permute-start | bytes 4325384 | tf_op jit(solution)/shard_map/grad_gate_plane/ppermute | solution.py:63
  311.5 34.7 %collective-permute-start.49 = (bf16[4,128,1408]{2,1,0:T(8,128)(2,1)}, bf16[4,128,1408]{2,1,0:T(8,128)(2,1)}, u32[]{:S(2)}, u32[]{:S(2)}) collective-permute-start(bf16[4,128,1408]{2,1,0:T(8,128)(2,1)} %get-tuple-element.61), channel_id=1, source_target_pairs={{72,0},{73,1},{74,2},{75,3},{76,4},{77,5},{78,6},{79,7},{0,8},{1,9... | collective-permute-start | bytes 4325384 | tf_op jit(solution)/shard_map/grad_gate_plane/ppermute | solution.py:63
  313.2 40.3 %all-to-all-start.11 = ((bf16[4,88,2048]{2,1,0:T(8,128)(2,1)}), bf16[4,88,2048]{2,1,0:T(8,128)(2,1)}, u32[]{:S(2)}, u32[]{:S(2)}) async-start(bf16[4,88,2048]{2,1,0:T(8,128)(2,1)} %fusion.12), calls=%async_computation.11 | async-start | bytes 2883584 | tf_op jit(solution)/shard_map/grad_down_plane/all_to_all | solution.py:99
  325.5 21.4 %collective-permute-start.22 = (bf16[128,2048]{1,0:T(8,128)(2,1)S(1)}, bf16[128,2048]{1,0:T(8,128)(2,1)S(1)}, u32[]{:S(2)}, u32[]{:S(2)}) collective-permute-start(bf16[128,2048]{1,0:T(8,128)(2,1)S(1)} %get-tuple-element.72), channel_id=1, source_target_pairs={{6,0},{7,1},{0,2},{1,3},{2,4},{3,5},{4,6},{5,7},{14,8},{15,9},{8,1... | collective-permute-start | bytes 1572872 | tf_op jit(solution)/shard_map/mixed_line/ppermute | solution.py:63
  326.3 33.8 %collective-permute-start.24 = (bf16[128,2048]{1,0:T(8,128)(2,1)}, bf16[128,2048]{1,0:T(8,128)(2,1)}, u32[]{:S(2)}, u32[]{:S(2)}) collective-permute-start(bf16[128,2048]{1,0:T(8,128)(2,1)} %get-tuple-element.73), channel_id=1, source_target_pairs={{2,0},{3,1},{4,2},{5,3},{6,4},{7,5},{0,6},{1,7},{10,8},{11,9},{12,... | collective-permute-start | bytes 1572872 | tf_op jit(solution)/shard_map/mixed_line/ppermute | solution.py:63
  327.5 33.1 %collective-permute-start.23 = (bf16[128,2048]{1,0:T(8,128)(2,1)}, bf16[128,2048]{1,0:T(8,128)(2,1)}, u32[]{:S(2)}, u32[]{:S(2)}) collective-permute-start(bf16[128,2048]{1,0:T(8,128)(2,1)} %get-tuple-element.74), channel_id=1, source_target_pairs={{4,0},{5,1},{6,2},{7,3},{0,4},{1,5},{2,6},{3,7},{12,8},{13,9},{14,... | collective-permute-start | bytes 1572872 | tf_op jit(solution)/shard_map/mixed_line/ppermute | solution.py:63
  343.4 19.6 %collective-permute-start.30 = (bf16[128,2048]{1,0:T(8,128)(2,1)}, bf16[128,2048]{1,0:T(8,128)(2,1)}, u32[]{:S(2)}, u32[]{:S(2)}) collective-permute-start(bf16[128,2048]{1,0:T(8,128)(2,1)} %get-tuple-element.69), channel_id=1, source_target_pairs={{6,0},{7,1},{0,2},{1,3},{2,4},{3,5},{4,6},{5,7},{14,8},{15,9},{8,1... | collective-permute-start | bytes 1572872 | tf_op jit(solution)/shard_map/grad_normed_two_line/ppermute | solution.py:63
  347.7 26.6 %collective-permute-start.31 = (bf16[128,2048]{1,0:T(8,128)(2,1)}, bf16[128,2048]{1,0:T(8,128)(2,1)}, u32[]{:S(2)}, u32[]{:S(2)}) collective-permute-start(bf16[128,2048]{1,0:T(8,128)(2,1)} %get-tuple-element.71), channel_id=1, source_target_pairs={{4,0},{5,1},{6,2},{7,3},{0,4},{1,5},{2,6},{3,7},{12,8},{13,9},{14,... | collective-permute-start | bytes 1572872 | tf_op jit(solution)/shard_map/grad_normed_two_line/ppermute | solution.py:63
  353.5 59.7 %all-to-all-start.9 = ((bf16[4,256,1408]{2,1,0:T(8,128)(2,1)}), bf16[4,256,1408]{2,1,0:T(8,128)(2,1)}, u32[]{:S(2)}, u32[]{:S(2)}) async-start(bf16[4,256,1408]{2,1,0:T(8,128)(2,1)} %fusion), calls=%async_computation.9 | async-start | bytes 5767168 | tf_op jit(solution)/shard_map/grad_gate_plane/all_to_all | solution.py:99
  360.1 25.0 %collective-permute-start.53 = (bf16[88,2048]{1,0:T(8,128)(2,1)S(1)}, bf16[88,2048]{1,0:T(8,128)(2,1)S(1)}, u32[]{:S(2)}, u32[]{:S(2)}) collective-permute-start(bf16[88,2048]{1,0:T(8,128)(2,1)S(1)} %convert_element_type.346), channel_id=1, source_target_pairs={{64,0},{65,1},{66,2},{67,3},{68,4},{69,5},{70,6},{71,7},{72,8},{73... | collective-permute-start | bytes 1081352 | tf_op jit(solution)/shard_map/grad_down_plane/ppermute | solution.py:63
  381.9 29.4 %collective-permute-start.35 = (bf16[128,2048]{1,0:T(8,128)(2,1)S(1)}, bf16[128,2048]{1,0:T(8,128)(2,1)S(1)}, u32[]{:S(2)}, u32[]{:S(2)}) collective-permute-start(bf16[128,2048]{1,0:T(8,128)(2,1)S(1)} %get-tuple-element.44), channel_id=1, source_target_pairs={{6,0},{7,1},{0,2},{1,3},{2,4},{3,5},{4,6},{5,7},{14,8},{15,9},{8,1... | collective-permute-start | bytes 1572872 | tf_op jit(solution)/shard_map/grad_attn_line/ppermute | solution.py:63
  382.9 28.4 %collective-permute-start.34 = (bf16[128,2048]{1,0:T(8,128)(2,1)S(1)}, bf16[128,2048]{1,0:T(8,128)(2,1)S(1)}, u32[]{:S(2)}, u32[]{:S(2)}) collective-permute-start(bf16[128,2048]{1,0:T(8,128)(2,1)S(1)} %get-tuple-element.44), channel_id=1, source_target_pairs={{4,0},{5,1},{6,2},{7,3},{0,4},{1,5},{2,6},{3,7},{12,8},{13,9},{14,... | collective-permute-start | bytes 1572872 | tf_op jit(solution)/shard_map/grad_attn_line/ppermute | solution.py:63
  383.7 27.7 %collective-permute-start.33 = (bf16[128,2048]{1,0:T(8,128)(2,1)S(1)}, bf16[128,2048]{1,0:T(8,128)(2,1)S(1)}, u32[]{:S(2)}, u32[]{:S(2)}) collective-permute-start(bf16[128,2048]{1,0:T(8,128)(2,1)S(1)} %get-tuple-element.44), channel_id=1, source_target_pairs={{2,0},{3,1},{4,2},{5,3},{6,4},{7,5},{0,6},{1,7},{10,8},{11,9},{12,... | collective-permute-start | bytes 1572872 | tf_op jit(solution)/shard_map/grad_attn_line/ppermute | solution.py:63
  385.9 39.5 %collective-permute-start.54 = (bf16[88,2048]{1,0:T(8,128)(2,1)}, bf16[88,2048]{1,0:T(8,128)(2,1)}, u32[]{:S(2)}, u32[]{:S(2)}) collective-permute-start(bf16[88,2048]{1,0:T(8,128)(2,1)} %add_convert_fusion.1), channel_id=1, source_target_pairs={{0,0},{8,1},{16,2},{24,3},{32,4},{40,5},{48,6},{56,7},{1,8},{9,9},... | collective-permute-start | bytes 1081352 | tf_op jit(solution)/shard_map/grad_down_plane/ppermute | solution.py:68
  413.1 53.0 %collective-permute-start.36 = (bf16[512,2048]{1,0:T(8,128)(2,1)}, bf16[512,2048]{1,0:T(8,128)(2,1)}, u32[]{:S(2)}, u32[]{:S(2)}) collective-permute-start(bf16[512,2048]{1,0:T(8,128)(2,1)} %pad_maximum_fusion.1), channel_id=1, source_target_pairs={{1,0},{0,1},{3,2},{2,3},{5,4},{4,5},{7,6},{6,7},{9,8},{8,9},{11,10... | collective-permute-start | bytes 6291464 | tf_op jit(solution)/shard_map/grad_attn_line/ppermute | solution.py:63
  415.7 22.9 %collective-permute-start.50 = (bf16[256,1408]{1,0:T(8,128)(2,1)S(1)}, bf16[256,1408]{1,0:T(8,128)(2,1)S(1)}, u32[]{:S(2)}, u32[]{:S(2)}) collective-permute-start(bf16[256,1408]{1,0:T(8,128)(2,1)S(1)} %convert_element_type.337), channel_id=1, source_target_pairs={{64,0},{65,1},{66,2},{67,3},{68,4},{69,5},{70,6},{71,7},{72,8},{73... | collective-permute-start | bytes 2162696 | tf_op jit(solution)/shard_map/grad_gate_plane/ppermute | solution.py:63
  518.3 41.5 %collective-permute-start.37 = (bf16[512,2048]{1,0:T(8,128)(2,1)}, bf16[512,2048]{1,0:T(8,128)(2,1)}, u32[]{:S(2)}, u32[]{:S(2)}) collective-permute-start(bf16[512,2048]{1,0:T(8,128)(2,1)} %convolution_convert_fusion.3), channel_id=1, source_target_pairs={{1,0},{0,1},{3,2},{2,3},{5,4},{4,5},{7,6},{6,7},{9,8},{8,9},{11,10... | collective-permute-start | bytes 6291464 | tf_op jit(solution)/shard_map/grad_normed_line/ppermute | solution.py:63
  562.9 24.3 %collective-permute-start.38 = (bf16[128,2048]{1,0:T(8,128)(2,1)S(1)}, bf16[128,2048]{1,0:T(8,128)(2,1)S(1)}, u32[]{:S(2)}, u32[]{:S(2)}) collective-permute-start(bf16[128,2048]{1,0:T(8,128)(2,1)S(1)} %get-tuple-element.66), channel_id=1, source_target_pairs={{6,0},{7,1},{0,2},{1,3},{2,4},{3,5},{4,6},{5,7},{14,8},{15,9},{8,1... | collective-permute-start | bytes 1572872 | tf_op jit(solution)/shard_map/grad_normed_line/ppermute | solution.py:63
  565.1 25.6 %collective-permute-start.40 = (bf16[128,2048]{1,0:T(8,128)(2,1)S(1)}, bf16[128,2048]{1,0:T(8,128)(2,1)S(1)}, u32[]{:S(2)}, u32[]{:S(2)}) collective-permute-start(bf16[128,2048]{1,0:T(8,128)(2,1)S(1)} %get-tuple-element.67), channel_id=1, source_target_pairs={{2,0},{3,1},{4,2},{5,3},{6,4},{7,5},{0,6},{1,7},{10,8},{11,9},{12,... | collective-permute-start | bytes 1572872 | tf_op jit(solution)/shard_map/grad_normed_line/ppermute | solution.py:63
  565.1 25.6 %collective-permute-start.39 = (bf16[128,2048]{1,0:T(8,128)(2,1)S(1)}, bf16[128,2048]{1,0:T(8,128)(2,1)S(1)}, u32[]{:S(2)}, u32[]{:S(2)}) collective-permute-start(bf16[128,2048]{1,0:T(8,128)(2,1)S(1)} %get-tuple-element.68), channel_id=1, source_target_pairs={{4,0},{5,1},{6,2},{7,3},{0,4},{1,5},{2,6},{3,7},{12,8},{13,9},{14,... | collective-permute-start | bytes 1572872 | tf_op jit(solution)/shard_map/grad_normed_line/ppermute | solution.py:63
  (79 other events, 987.6 us)

commit v2 on v1

v2 whole, which is shorter than its diff:
```python
import functools

import jax
import jax.numpy as jnp
from jax import lax
from jax.experimental import pallas as pl
from jax.experimental.pallas import tpu as pltpu
from jax.sharding import PartitionSpec as P

HEADS = 32
KV_HEADS = 4
HEAD_DIM = 64
D = 2048
FF = 5632
STEP = 10
ROWS = 128
GROUP = 8
TOK = ROWS * GROUP
HALF = TOK // 2
HEADS_HERE = HEADS // GROUP
Q_HERE = HEADS_HERE * HEAD_DIM
PROJ_HERE = Q_HERE + 2 * HEAD_DIM
FF_HERE = FF // GROUP
FF_MAIN = FF_HERE // 128 * 128
FF_REST = FF_HERE - FF_MAIN
Q_BLOCK = 256
VMEM = 60 * 2**20

EPSILON = 1e-05
BETA_ONE = 0.9
BETA_TWO = 0.95
ADAM_EPSILON = 1e-08
DECAY = 0.1
RATE_QKV = 0.02
RATE_OUT = 0.25
RATE_GATE_UP = 0.02
RATE_DOWN = 0.013
RATE_GAINS = 0.3

BF = jnp.bfloat16
F32 = jnp.float32
BOTH = ("rep", "shard")
LINES = [[8 * b + a for a in range(8)] for b in range(8)]
PLANES = [[8 * b + a for b in range(8)] for a in range(8)]


def index_of(r, y, z, x, c):
    return r * 64 + y * 16 + z * 8 + x * 2 + c


def places():
    return [
        (r, y, z, x, c)
        for r in range(2)
        for y in range(4)
        for z in range(2)
        for x in range(4)
        for c in range(2)
    ]


def come_from(v, y=0, x=0, c=0, zz=0):
    pairs = []
    for r, yy, z, xx, cc in places():
        ring = (2 * r + z + zz) % 4
        source = index_of(ring // 2, (yy + y) % 4, ring % 2, (xx + x) % 4, cc ^ c)
        pairs.append((source, index_of(r, yy, z, xx, cc)))
    return lax.ppermute(v, BOTH, pairs)


def turned(v):
    pairs = [(index_of(r, x, c, y, z), index_of(r, y, z, x, c)) for r, y, z, x, c in places()]
    return lax.ppermute(v, BOTH, pairs)


def dot(left, right):
    return jnp.dot(left, right, preferred_element_type=F32)


def dot_nt(left, right):
    return lax.dot_general(left, right, (((1,), (1,)), ((), ())), preferred_element_type=F32)


def dot_tn(left, right):
    return lax.dot_general(left, right, (((0,), (0,)), ((), ())), preferred_element_type=F32)


def after(v, *events):
    for event in events:
        last = event[(-1,) * event.ndim]
        v = jnp.where(last == last, v, jnp.zeros_like(v))
    return v


def settled(v):
    return lax.optimization_barrier(v)


def halves_gather(v):
    pieces = line_pieces(v)
    near, far = line_halves(v, pieces)
    return near, far, pieces[0]


def line_pieces(v):
    return [come_from(v, x=k) for k in (1, 2, 3)]


def line_halves(v, pieces):
    near = settled(jnp.concatenate([v] + pieces, axis=0))
    return near, come_from(near, c=1)


def plane_exchange(v):
    return lax.all_to_all(v, "shard", 0, 0, tiled=True, axis_index_groups=PLANES)


def plane_spread(v):
    parts = plane_exchange(jnp.broadcast_to(v[None], (8, *v.shape)))
    return parts.reshape(8 * v.shape[0], v.shape[1])


def plane_gather(v):
    return lax.all_gather(v, "shard", axis=0, tiled=True, axis_index_groups=PLANES)


def plane_scatter(v):
    return lax.psum_scatter(
        v, "shard", scatter_dimension=0, tiled=True, axis_index_groups=PLANES
    )


def rep_sum(total):
    return total + come_from(total.astype(BF), zz=2).astype(F32)


def line_exchange(v):
    return lax.all_to_all(v, "shard", 0, 0, tiled=True, axis_index_groups=LINES)


def rate_of(values):
    return lax.rsqrt(jnp.mean(values * values, axis=-1, keepdims=True) + EPSILON)


def unit_norm(values):
    return values * rate_of(values)


def unit_norm_back(values, grad):
    rate = rate_of(values)
    unit = values * rate
    return rate * (grad - unit * jnp.mean(grad * unit, axis=-1, keepdims=True))


def adam_step(weight, grad, first, second, rate):
    first_new = BETA_ONE * first + (1.0 - BETA_ONE) * grad
    second_new = BETA_TWO * second + (1.0 - BETA_TWO) * grad * grad
    first_hat = first_new / (1.0 - BETA_ONE**STEP)
    second_hat = second_new / (1.0 - BETA_TWO**STEP)
    weight_new = weight - rate * (
        first_hat / (jnp.sqrt(second_hat) + ADAM_EPSILON) + DECAY * weight
    )
    return (weight_new, first_new, second_new)


TINY = pl.CostEstimate(flops=1, bytes_accessed=1, transcendentals=0)
ANY = pl.BlockSpec(memory_space=pl.ANY)


def cost(flops):
    return pl.CostEstimate(flops=int(flops), bytes_accessed=1, transcendentals=0)


def core_sum_kernel(near_ref, came_ref, *refs):
    own_ref, *piece_refs = refs[-4:]
    total = near_ref[...].astype(F32) + came_ref[...].astype(F32)
    step = pl.program_id(0)

    @pl.when(step == 0)
    def _():
        own_ref[...] = total

    for k in (1, 2, 3):

        @pl.when(step == k)
        def _(k=k):
            piece_refs[k - 1][...] = total.astype(BF)


def line_scatter(near, far, *events):
    here = pl.BlockSpec((ROWS, D), lambda i: (0, 0))
    own, *pieces = pl.pallas_call(
        core_sum_kernel,
        grid=(4,),
        in_specs=[pl.BlockSpec((ROWS, D), lambda i: (i, 0))] * 2 + [ANY] * len(events),
        out_specs=[here] * 4,
        out_shape=[jax.ShapeDtypeStruct((ROWS, D), F32)]
        + [jax.ShapeDtypeStruct((ROWS, D), BF)] * 3,
        cost_estimate=TINY,
        compiler_params=pltpu.CompilerParams(vmem_limit_bytes=VMEM),
        name="core_sum",
    )(near, come_from(far, c=1), *events)
    return own, [come_from(piece, x=-k) for k, piece in zip((1, 2, 3), pieces)]


def pieces_sum(refs):
    total = refs[0][...]
    for ref in refs[1:4]:
        total = total + ref[...].astype(F32)
    return total


def middle_kernel(*refs):
    tokens_ref, middle_ref, normed_ref = refs[4], refs[-2], refs[-1]
    middle = tokens_ref[...].astype(F32) + pieces_sum(refs)
    middle_ref[...] = middle
    normed_ref[...] = unit_norm(middle).astype(BF)


def middle_back_kernel(*refs):
    middle_ref, cotangent_ref, grad_ref, low_ref = refs[4], refs[5], refs[-2], refs[-1]
    grad = cotangent_ref[...].astype(F32) + unit_norm_back(middle_ref[...], pieces_sum(refs))
    grad_ref[...] = grad
    low_ref[...] = grad.astype(BF)


def tokens_back_kernel(*refs):
    tokens_ref, middle_ref, out_ref = refs[4], refs[5], refs[-1]
    out_ref[...] = middle_ref[...] + unit_norm_back(tokens_ref[...].astype(F32), pieces_sum(refs))


def mixed_kernel(*refs):
    refs[-1][...] = refs[4][...] + pieces_sum(refs)


def row_kernel(kernel, own, pieces, others, outs, events=()):
    count = 1 + len(pieces) + len(others)
    spec = pl.BlockSpec((ROWS, D), lambda: (0, 0))
    return pl.pallas_call(
        kernel,
        in_specs=[spec] * count + [ANY] * len(events),
        out_specs=[spec] * len(outs),
        out_shape=[jax.ShapeDtypeStruct((ROWS, D), t) for t in outs],
        cost_estimate=TINY,
        compiler_params=pltpu.CompilerParams(vmem_limit_bytes=VMEM),
        name=kernel.__name__,
    )(own, *pieces, *others, *events)


def parts_sum_kernel(parts_ref, *refs):
    total = parts_ref[0].astype(F32)
    for k in range(1, parts_ref.shape[0]):
        total = total + parts_ref[k].astype(F32)
    refs[-2][...] = total
    refs[-1][...] = total.astype(BF)


def parts_sum(parts, block, *events):
    n, rows, cols = parts.shape
    out = pl.BlockSpec((block, cols), lambda i: (i, 0))
    return pl.pallas_call(
        parts_sum_kernel,
        grid=(rows // block,),
        in_specs=[pl.BlockSpec((n, block, cols), lambda i: (0, i, 0))] + [ANY] * len(events),
        out_specs=[out] * 2,
        out_shape=[jax.ShapeDtypeStruct((rows, cols), t) for t in (F32, BF)],
        cost_estimate=TINY,
        compiler_params=pltpu.CompilerParams(vmem_limit_bytes=VMEM),
        name="parts_sum",
    )(parts, *events)


def lanes(rows):
    return lax.broadcasted_iota(jnp.int32, (rows, 128), 1)


def rotated(v, cosine, sine, lane):
    partner = jnp.where(lane % HEAD_DIM < HEAD_DIM // 2, pltpu.roll(v, 96, 1), pltpu.roll(v, 32, 1))
    return v * cosine + partner * sine


def split_pair(pair, k_ref, v_ref, lane):
    swapped = pltpu.roll(pair, 64, 1)
    low = lane < HEAD_DIM
    zero = jnp.zeros_like(pair)
    k_ref[0] = jnp.where(low, pair, zero).astype(BF)
    k_ref[1] = jnp.where(low, zero, swapped).astype(BF)
    v_ref[0] = jnp.where(low, swapped, zero).astype(BF)
    v_ref[1] = jnp.where(low, zero, pair).astype(BF)


def barred(column_ref, row_ref):
    same = column_ref[:, 0:1] == row_ref[0:1, :]
    before = row_ref[1:2, :] <= column_ref[:, 1:2]
    return jnp.where(same & before, 0.0, -1e30)


def forward_kernel(*refs):
    near_ref, far_ref, w_qkv_ref, cos_ref, sin_ref, cos_all_ref, sin_all_ref, column_ref, row_ref = refs[:9]
    out_ref, q_ref, kv_ref, total_ref, proj_scr, k_scr, v_scr = refs[-7:]
    lane = lanes(Q_BLOCK)
    step = pl.program_id(0)

    @pl.when(step == 0)
    def _():
        for i in range(TOK // Q_BLOCK):
            ref = near_ref if i * Q_BLOCK < HALF else far_ref
            rows = ref[i * Q_BLOCK % HALF : i * Q_BLOCK % HALF + Q_BLOCK]
            proj_scr[i * Q_BLOCK : (i + 1) * Q_BLOCK] = dot(rows, w_qkv_ref[...])
        wide = lanes(TOK)
        pair = proj_scr[:, Q_HERE:]
        turned_pair = rotated(pair, cos_all_ref[...], sin_all_ref[...], wide)
        pair = jnp.where(wide < HEAD_DIM, turned_pair, pair).astype(BF)
        kv_ref[...] = pair
        split_pair(pair.astype(F32), k_scr, v_scr, wide)

    bar = barred(column_ref, row_ref)
    totals = jnp.zeros((Q_BLOCK, 128), F32)
    here = pl.ds(pl.multiple_of(step * Q_BLOCK, Q_BLOCK), Q_BLOCK)
    for chunk in range(HEADS_HERE // 2):
        span = slice(128 * chunk, 128 * (chunk + 1))
        queries = rotated(proj_scr[here, span], cos_ref[...], sin_ref[...], lane).astype(BF)
        queries = (queries.astype(F32) * HEAD_DIM**-0.5).astype(BF)
        q_ref[:, span] = queries
        out = jnp.zeros((Q_BLOCK, 128), F32)
        for side in range(2):
            scores = dot_nt(queries, k_scr[side]) + bar
            peak = jnp.max(scores, axis=1, keepdims=True)
            expo = jnp.exp(scores - peak)
            total = jnp.sum(expo, axis=1, keepdims=True)
            probs = (expo * (1.0 / total)).astype(BF)
            out = out + dot(probs, v_scr[side])
            totals = jnp.where(lane == 2 * chunk + side, peak + jnp.log(total), totals)
        out_ref[:, span] = out.astype(BF)
    total_ref[...] = totals


def backward_kernel(*refs):
    near_ref, far_ref, w_out_ref, q_ref, kv_ref, total_ref, cos_ref, sin_ref, cos_all_ref, sin_all_ref = refs[:10]
    column_ref, row_ref = refs[10:12]
    dproj_ref, do_scr, k_scr, v_scr, dk_scr, dv_scr = refs[-6:]
    lane = lanes(Q_BLOCK)
    step = pl.program_id(0)

    @pl.when(step == 0)
    def _():
        split_pair(kv_ref[...].astype(F32), k_scr, v_scr, lanes(TOK))
        dk_scr[...] = jnp.zeros_like(dk_scr)
        dv_scr[...] = jnp.zeros_like(dv_scr)

    @pl.when(step < HALF // Q_BLOCK)
    def _():
        do_scr[...] = dot_nt(near_ref[...], w_out_ref[...]).astype(BF)

    @pl.when(step >= HALF // Q_BLOCK)
    def _():
        do_scr[...] = dot_nt(far_ref[...], w_out_ref[...]).astype(BF)

    bar = barred(column_ref, row_ref)
    here = pl.ds(pl.multiple_of(step * Q_BLOCK, Q_BLOCK), Q_BLOCK)
    for chunk in range(HEADS_HERE // 2):
        span = slice(128 * chunk, 128 * (chunk + 1))
        queries = q_ref[:, span]
        grads = do_scr[:, span]
        dq = jnp.zeros((Q_BLOCK, 128), F32)
        for side in range(2):
            held = (lane >= HEAD_DIM) == (side == 1)
            head = 2 * chunk + side
            scores = dot_nt(queries, k_scr[side]) + bar
            probs = jnp.exp(scores - total_ref[:, head : head + 1])
            dp = dot_nt(grads, v_scr[side])
            inner = jnp.sum(probs * dp, axis=1, keepdims=True)
            ds = (probs * (dp - inner)).astype(BF)
            dq = dq + dot(ds, k_scr[side])
            dk_scr[...] += dot_tn(ds, jnp.where(held, queries, jnp.zeros_like(queries)))
            dv_scr[...] += dot_tn(
                probs.astype(BF), jnp.where(held, grads, jnp.zeros_like(grads))
            )
        dq = dq * HEAD_DIM**-0.5
        dproj_ref[here, span] = rotated(dq, cos_ref[...], -sin_ref[...], lane).astype(BF)

    @pl.when(step == pl.num_programs(0) - 1)
    def _():
        wide = lanes(TOK)
        dk = dk_scr[...] + pltpu.roll(dk_scr[...], 64, 1)
        dv = dv_scr[...] + pltpu.roll(dv_scr[...], 64, 1)
        dk = rotated(dk, cos_all_ref[...], -sin_all_ref[...], wide)
        dproj_ref[:, Q_HERE:] = jnp.where(wide < HEAD_DIM, dk, dv).astype(BF)


def blocked(cols):
    return pl.BlockSpec((Q_BLOCK, cols), lambda i: (i, 0))


def whole(rows, cols):
    return pl.BlockSpec((rows, cols), lambda i: (0, 0), pipeline_mode=pl.Buffered(1))


def near_block(cols):
    return pl.BlockSpec((Q_BLOCK, cols), lambda i: (jnp.minimum(i, HALF // Q_BLOCK - 1), 0))


def far_block(cols):
    return pl.BlockSpec((Q_BLOCK, cols), lambda i: (jnp.maximum(i - HALF // Q_BLOCK, 0), 0))


def attend(near, far, w_qkv, cosine, sine, column, row, *events):
    return pl.pallas_call(
        forward_kernel,
        grid=(TOK // Q_BLOCK,),
        in_specs=[
            whole(HALF, D),
            whole(HALF, D),
            whole(D, PROJ_HERE),
            blocked(128),
            blocked(128),
            whole(TOK, 128),
            whole(TOK, 128),
            blocked(2),
            whole(2, TOK),
        ]
        + [ANY] * len(events),
        out_specs=[
            blocked(Q_HERE),
            blocked(Q_HERE),
            pl.BlockSpec((TOK, 128), lambda i: (0, 0)),
            blocked(128),
        ],
        out_shape=[
            jax.ShapeDtypeStruct((TOK, Q_HERE), BF),
            jax.ShapeDtypeStruct((TOK, Q_HERE), BF),
            jax.ShapeDtypeStruct((TOK, 128), BF),
            jax.ShapeDtypeStruct((TOK, 128), F32),
        ],
        scratch_shapes=[
            pltpu.VMEM((TOK, PROJ_HERE), F32),
            pltpu.VMEM((2, TOK, 128), BF),
            pltpu.VMEM((2, TOK, 128), BF),
        ],
        compiler_params=pltpu.CompilerParams(vmem_limit_bytes=VMEM),
        cost_estimate=cost(30e9),
        name="attention_forward",
    )(near, far, w_qkv, cosine, sine, cosine, sine, column, row, *events)


def attend_back(near, far, w_out, queries, pair, totals, cosine, sine, column, row, *events):
    return pl.pallas_call(
        backward_kernel,
        grid=(TOK // Q_BLOCK,),
        in_specs=[
            near_block(D),
            far_block(D),
            whole(Q_HERE, D),
            blocked(Q_HERE),
            whole(TOK, 128),
            blocked(128),
            blocked(128),
            blocked(128),
            whole(TOK, 128),
            whole(TOK, 128),
            blocked(2),
            whole(2, TOK),
        ]
        + [ANY] * len(events),
        out_specs=pl.BlockSpec((TOK, PROJ_HERE), lambda i: (0, 0)),
        out_shape=jax.ShapeDtypeStruct((TOK, PROJ_HERE), BF),
        scratch_shapes=[
            pltpu.VMEM((Q_BLOCK, Q_HERE), BF),
            pltpu.VMEM((2, TOK, 128), BF),
            pltpu.VMEM((2, TOK, 128), BF),
            pltpu.VMEM((TOK, 128), F32),
            pltpu.VMEM((TOK, 128), F32),
        ],
        compiler_params=pltpu.CompilerParams(vmem_limit_bytes=VMEM),
        cost_estimate=cost(30e9),
        name="attention_backward",
    )(near, far, w_out, queries, pair, totals, cosine, sine, cosine, sine, column, row, *events)


def line_dot_kernel(*refs, turned_weight):
    rows_ref, w_ref, near_ref, far_ref = refs[0], refs[1], refs[-2], refs[-1]
    product = dot_nt if turned_weight else dot
    part = product(rows_ref[...], w_ref[...]).astype(BF)

    @pl.when(pl.program_id(0) < HALF // Q_BLOCK)
    def _():
        near_ref[...] = part

    @pl.when(pl.program_id(0) >= HALF // Q_BLOCK)
    def _():
        far_ref[...] = part


def line_dot(rows, weight, turned_weight, *events):
    return pl.pallas_call(
        functools.partial(line_dot_kernel, turned_weight=turned_weight),
        grid=(TOK // Q_BLOCK,),
        in_specs=[blocked(rows.shape[1]), whole(*weight.shape)] + [ANY] * len(events),
        out_specs=[near_block(D), far_block(D)],
        out_shape=[jax.ShapeDtypeStruct((HALF, D), BF)] * 2,
        compiler_params=pltpu.CompilerParams(vmem_limit_bytes=VMEM),
        cost_estimate=TINY,
        name="line_dot",
    )(rows, weight, *events)


def feed_forward_kernel(
    near_ref, far_ref, grads_near_ref, grads_far_ref, gate_ref, down_ref,
    hid_near_ref, hid_far_ref, dgu_near_ref, dgu_far_ref, dn_near_ref, dn_far_ref, mix_near_ref, mix_far_ref,
):
    rows = jnp.concatenate([near_ref[...], far_ref[...]], axis=0)
    grads = jnp.concatenate([grads_near_ref[...], grads_far_ref[...]], axis=0)
    gate_up = dot(rows, gate_ref[...])
    dhid = dot_nt(grads, down_ref[...])

    def unit(gate, up, grad):
        sig = 1.0 / (1.0 + jnp.exp(-gate))
        act = gate * sig
        return act * up, grad * up * (sig + act * (1.0 - sig)), grad * act

    hid, dgate, dup = unit(
        gate_up[:, :FF_MAIN], gate_up[:, FF_MAIN : 2 * FF_MAIN], dhid[:, :FF_MAIN]
    )
    last = gate_up[:, 2 * FF_MAIN :]
    grad = jnp.concatenate([dhid[:, FF_MAIN:], dhid[:, FF_MAIN:]], axis=1)
    hid_last, dgate_last, dup_last = unit(last, pltpu.roll(last, FF_REST, 1), grad)
    low = lax.broadcasted_iota(jnp.int32, last.shape, 1) < FF_REST
    last = jnp.where(low, dgate_last, pltpu.roll(dup_last, FF_REST, 1))
    hid = hid.astype(BF)
    hid_last = hid_last[:, :FF_REST].astype(BF)
    hid_near_ref[:, :FF_MAIN] = hid[:ROWS]
    hid_near_ref[:, FF_MAIN:] = hid_last[:ROWS]
    hid_far_ref[:, :FF_MAIN] = hid[ROWS:]
    hid_far_ref[:, FF_MAIN:] = hid_last[ROWS:]
    dgu = jnp.concatenate([dgate.astype(BF), dup.astype(BF), last.astype(BF)], axis=1)
    dgu_near_ref[...] = dgu[:ROWS]
    dgu_far_ref[...] = dgu[ROWS:]
    dn = dot_nt(dgu, gate_ref[...]).astype(BF)
    dn_near_ref[...] = dn[:ROWS]
    dn_far_ref[...] = dn[ROWS:]
    mix = dot(jnp.concatenate([hid, hid_last], axis=1), down_ref[...]).astype(BF)
    mix_near_ref[...] = mix[:ROWS]
    mix_far_ref[...] = mix[ROWS:]


def feed_forward(near, far, grads_near, grads_far, gate_full, down_full):
    def side(cols):
        return pl.BlockSpec((ROWS, cols), lambda i: (i, 0))

    outs = (FF_HERE, FF_HERE, 2 * FF_HERE, 2 * FF_HERE, D, D, D, D)
    return pl.pallas_call(
        feed_forward_kernel,
        grid=(4,),
        in_specs=[side(D)] * 4 + [whole(D, 2 * FF_HERE), whole(FF_HERE, D)],
        out_specs=[side(c) for c in outs],
        out_shape=[jax.ShapeDtypeStruct((HALF, c), BF) for c in outs],
        compiler_params=pltpu.CompilerParams(vmem_limit_bytes=VMEM),
        cost_estimate=cost(30e9),
        name="feed_forward",
    )(near, far, grads_near, grads_far, gate_full, down_full)


def weight_grad_kernel(near_ref, far_ref, g_near_ref, g_far_ref, *refs):
    grad = dot_tn(near_ref[...], g_near_ref[...]) + dot_tn(far_ref[...], g_far_ref[...])
    refs[-1][...] = grad.astype(BF)


def weight_grad(near, far, grads_near, grads_far, far_block_index, block, flops, *events):
    deep, cols = near.shape[1], grads_near.shape[1]
    if block == cols:
        grid = deep // 256
        rows = pl.BlockSpec((HALF, 256), lambda i: (0, i))
        grads = [pl.BlockSpec((HALF, cols), lambda i, k=k: (k, 0)) for k in (0, far_block_index)]
        out = pl.BlockSpec((256, cols), lambda i: (i, 0))
    else:
        grid = cols // block
        rows = pl.BlockSpec((HALF, deep), lambda i: (0, 0))
        grads = [pl.BlockSpec((HALF, block), lambda i, k=k: (k, i)) for k in (0, far_block_index)]
        out = pl.BlockSpec((deep, block), lambda i: (0, i))
    return pl.pallas_call(
        weight_grad_kernel,
        grid=(grid,),
        in_specs=[rows, rows, *grads] + [ANY] * len(events),
        out_specs=out,
        out_shape=jax.ShapeDtypeStruct((deep, cols), BF),
        compiler_params=pltpu.CompilerParams(vmem_limit_bytes=VMEM),
        cost_estimate=cost(flops),
        name="weight_grad",
    )(near, far, grads_near, grads_far, *events)


def small_rows(segment_ids, position_ids):
    parts = [position_ids // 32, position_ids % 32, segment_ids // 128, segment_ids % 128]
    flat = jnp.concatenate([p.astype(BF) for p in parts])
    return jnp.pad(flat[None], ((0, 7), (0, PROJ_HERE + 2 * FF_HERE - 512)))


def small_read(rows):
    s = lax.axis_index("shard")
    x, c = (s // 2) % 4, s % 2
    line = rows[:, 0, :512].reshape(4, 2, 4, 128).astype(F32)
    line = lax.dynamic_slice(jnp.concatenate([line, line], axis=0), (x, 0, 0, 0), (4, 2, 4, 128))
    line = jnp.where(c == 0, line, line[:, ::-1]).transpose(1, 0, 2, 3).reshape(8, 4, 128)
    position = (line[:, 0] * 32.0 + line[:, 1]).reshape(TOK)
    segment = (line[:, 2] * 128.0 + line[:, 3]).reshape(TOK)
    return position, segment


def on_device(
    tokens,
    cotangent,
    segment_ids,
    position_ids,
    w_qkv,
    w_out,
    w_gate_up,
    w_down,
    gains,
    m_qkv,
    v_qkv,
    m_out,
    v_out,
    m_gate_up,
    v_gate_up,
    m_down,
    v_down,
    m_gains,
    v_gains,
):
    gain_rows = gains.astype(BF).astype(F32).T
    qkv_low = w_qkv.astype(BF).astype(F32)
    gate_low = w_gate_up.astype(BF).astype(F32)

    with jax.named_scope("qkv_weights_line"):
        low = (qkv_low * gain_rows[:, 0:1]).astype(BF)
        q_cols = low[:, :D].reshape(32, 8, Q_HERE)
        kv_cols = low[:, D:].reshape(32, 2, KV_HEADS, HEAD_DIM).transpose(0, 2, 1, 3)
        kv_cols = jnp.repeat(kv_cols.reshape(32, KV_HEADS, 2 * HEAD_DIM), 2, axis=1)
        qkv_cut = jnp.concatenate([q_cols, kv_cols], axis=2).transpose(1, 0, 2)
    with jax.named_scope("gate_weights_line"):
        low = (gate_low * gain_rows[:, 1:2]).astype(BF)
        low = low.reshape(32, 2, 8, FF_HERE)
        gate_cut = jnp.concatenate(
            [low[:, 0, :, :FF_MAIN], low[:, 1, :, :FF_MAIN], low[:, 0, :, FF_MAIN:], low[:, 1, :, FF_MAIN:]],
            axis=2,
        )
        both = jnp.concatenate([qkv_cut, gate_cut.transpose(1, 0, 2)], axis=2)
        small = small_rows(segment_ids, position_ids)
        small = jnp.broadcast_to(small[None], (8, *small.shape))
        both = line_exchange(jnp.concatenate([both, small], axis=1))
        positions, segments = small_read(both[:, 32:])
        qkv_line = both[:, :32, :PROJ_HERE].reshape(256, PROJ_HERE)
        gate_line = both[:, :32, PROJ_HERE:].reshape(256, 2 * FF_HERE)
    with jax.named_scope("gate_weights_plane"):
        gate_full = plane_gather(gate_line)
    with jax.named_scope("qkv_weights_plane"):
        qkv_full = plane_spread(qkv_line)
    with jax.named_scope("normed_line"):
        normed = unit_norm(tokens.astype(F32)).astype(BF)
        pieces = line_pieces(normed)
        near, far = line_halves(normed, pieces)
    with jax.named_scope("cotangent_line"):
        cot_pieces = line_pieces(after(cotangent, near))
    with jax.named_scope("out_turn"):
        out_turned = turned(w_out.astype(BF))
    with jax.named_scope("down_turn"):
        down_turned = turned(after(w_down.astype(BF), near))
    with jax.named_scope("out_weights_plane"):
        out_full = plane_spread(after(out_turned, qkv_full))
    with jax.named_scope("down_weights_plane"):
        down_full = plane_spread(after(down_turned, out_full))

    freqs = 10000.0 ** (-jnp.arange(HEAD_DIM // 2).astype(F32) * 2.0 / HEAD_DIM)
    angles = positions[:, None] * freqs[None, :]
    cosine = jnp.tile(jnp.cos(angles), (1, 4))
    sine = jnp.sin(angles)
    sine = jnp.concatenate([-sine, sine, -sine, sine], axis=1)
    row = jnp.stack([segments, positions])
    column = row.T
    heads_out, queries, pair, totals = attend(
        near, far, qkv_full, cosine, sine, column, row, *cot_pieces
    )
    with jax.named_scope("cotangent_line"):
        cot_near, cot_far = line_halves(after(cotangent, heads_out), cot_pieces)
    with jax.named_scope("heads_out_line"):
        own, pieces = line_scatter(*line_dot(heads_out, out_full, False, cot_near))
        middle, normed_two = row_kernel(
            middle_kernel, own, pieces, [tokens], [F32, BF], (cot_far, down_full)
        )

    with jax.named_scope("normed_two_line"):
        near_two, far_two = line_halves(normed_two, line_pieces(normed_two))
    hid_near, hid_far, dgu_near, dgu_far, dn_near, dn_far, mix_near, mix_far = feed_forward(
        near_two, far_two, cot_near, cot_far, gate_full, down_full
    )
    with jax.named_scope("grad_gate_plane"):
        grad_gate = weight_grad(near_two, far_two, dgu_near, dgu_far, 0, 2 * FF_HERE, 15e9)
        gate_owned = plane_scatter(grad_gate)
    with jax.named_scope("grad_normed_two_line"):
        own, pieces = line_scatter(dn_near, dn_far, grad_gate)
    with jax.named_scope("grad_down_plane"):
        grad_down = weight_grad(hid_near, hid_far, cot_near, cot_far, 0, 512, 1, own)
        down_parts = plane_exchange(grad_down.reshape(8, 88, D))
    with jax.named_scope("mixed_line"):
        mixed_own, mixed_pieces = line_scatter(mix_near, mix_far)
    with jax.named_scope("grad_normed_two_line"):
        grad_middle, grad_attn = row_kernel(
            middle_back_kernel, own, pieces, [middle, cotangent], [F32, BF], (grad_down, mixed_own)
        )
    with jax.named_scope("grad_attn_line"):
        pieces = line_pieces(grad_attn)
        attn_near, attn_far = line_halves(grad_attn, pieces)
    grad_proj = attend_back(
        attn_near, attn_far, out_full, queries, pair, totals, cosine, sine, column, row,
        mixed_own,
    )
    with jax.named_scope("mixed_line"):
        (mixed,) = row_kernel(mixed_kernel, mixed_own, mixed_pieces, [middle], [F32], (grad_proj,))
    with jax.named_scope("grad_qkv"):
        grad_qkv_local = weight_grad(
            near, far, grad_proj, grad_proj, 1, PROJ_HERE, 5e9, mixed
        )
        qkv_parts = plane_exchange(grad_qkv_local.reshape(8, 256, PROJ_HERE))
    with jax.named_scope("grad_out_plane"):
        grad_out = weight_grad(heads_out[:HALF], heads_out[HALF:], attn_near, attn_far, 0, 512, 1, grad_qkv_local)
    with jax.named_scope("grad_normed_line"):
        own, pieces = line_scatter(*line_dot(grad_proj, qkv_full, True, grad_out, down_parts))
    with jax.named_scope("grad_down_rep"):
        down_owned, down_low = parts_sum(down_parts, 88, pieces[0])
        down_sum = down_owned + come_from(down_low, zz=2).astype(F32)
        grad_down = turned(after(down_sum.astype(BF), pieces[0])).astype(F32)
    with jax.named_scope("grad_gate_rep"):
        gate_low_sum = after(gate_owned, pieces[0])
        gate_from_rep = come_from(gate_low_sum, zz=2)
        gate_sum = gate_low_sum.astype(F32) + gate_from_rep.astype(F32)
    with jax.named_scope("grad_normed_line"):
        (d_tokens,) = row_kernel(
            tokens_back_kernel, own, pieces, [tokens, grad_middle], [F32]
        )
    with jax.named_scope("grad_out_rep"):
        out_parts = plane_exchange(after(grad_out.reshape(8, 32, D), qkv_parts, own))
        out_owned, out_low = parts_sum(out_parts, 32, gate_from_rep)
        out_sum = out_owned + come_from(out_low, zz=2).astype(F32)
        grad_out = turned(out_sum.astype(BF)).astype(F32)
    with jax.named_scope("grad_gate_line"):
        gate_sum = after(gate_sum.astype(BF), pieces[0])
        parts = line_exchange(gate_sum.reshape(8, 32, 2 * FF_HERE)).astype(F32)
        main, rest = 2 * FF_MAIN, 2 * FF_MAIN + FF_REST
        grad_gate = jnp.stack(
            [
                jnp.concatenate([parts[:, :, :FF_MAIN], parts[:, :, main:rest]], axis=2),
                jnp.concatenate([parts[:, :, FF_MAIN:main], parts[:, :, rest:]], axis=2),
            ]
        )
        grad_gate = grad_gate.transpose(2, 0, 1, 3).reshape(32, 2 * FF)
    with jax.named_scope("grad_qkv"):
        qkv_sum, qkv_low_sum = parts_sum(qkv_parts, 256, pieces[0])
        qkv_sum = qkv_sum + come_from(qkv_low_sum, zz=2).astype(F32)
        parts = line_exchange(qkv_sum.astype(BF).reshape(8, 32, PROJ_HERE)).astype(F32)
        q_part = parts[:, :, :Q_HERE].transpose(1, 0, 2).reshape(32, D)
        kv_part = parts[:, :, Q_HERE:].reshape(KV_HEADS, 2, 32, 2, HEAD_DIM).sum(axis=1)
        kv_part = kv_part.transpose(1, 2, 0, 3).reshape(32, 2 * KV_HEADS * HEAD_DIM)
        grad_qkv = jnp.concatenate([q_part, kv_part], axis=1)

    grad_gains = jnp.stack(
        [jnp.sum(qkv_low * grad_qkv, axis=1), jnp.sum(gate_low * grad_gate, axis=1)]
    )
    qkv_new = adam_step(w_qkv, grad_qkv * gain_rows[:, 0:1], m_qkv, v_qkv, RATE_QKV)
    out_new = adam_step(w_out, grad_out, m_out, v_out, RATE_OUT)
    gate_new = adam_step(w_gate_up, grad_gate * gain_rows[:, 1:2], m_gate_up, v_gate_up, RATE_GATE_UP)
    down_new = adam_step(w_down, grad_down, m_down, v_down, RATE_DOWN)
    gains_new = adam_step(gains, grad_gains, m_gains, v_gains, RATE_GAINS)
    return (mixed, d_tokens, *qkv_new, *out_new, *gate_new, *down_new, *gains_new)


def solution(mesh):
    tokens = P(BOTH, None)
    ids = P(BOTH)
    rows = P("shard", None)
    columns = P(None, "shard")
    return jax.shard_map(
        on_device,
        mesh=mesh,
        in_specs=(tokens, tokens, ids, ids, rows, rows, rows, rows, columns)
        + (rows,) * 8
        + (columns,) * 2,
        out_specs=(tokens, tokens) + (rows,) * 12 + (columns,) * 3,
        check_vma=False,
    )
```

time: 598 us -> 575 us (0.962)
  Pallas kernels: 28.6 us -> 153 us
  matrix products: 76.9 us -> 0 us
  local copies, waits for them, and re-layouts: 64.4 us -> 33.7 us
  starting transfers between devices: 138 us -> 113 us
  other arithmetic: 67.8 us -> 43.1 us
  between operations: 2.39 us -> 24.6 us
  waiting for transfers between devices: 214 us -> 197 us
    pallas_call x2 -> x20, Pallas kernels: 28.6 us -> 153 us  [the longest x4 32 us: weight_grad(): pl.pallas_call(weight_grad_kernel, grid=(grid,), in_specs=[rows, rows, *g...]
    dot_general x20 -> x0, matrix products: 76.9 us -> none  [the longest x8 31.9 us: dot_nt(): lax.dot_general(left, right, (((1,), (1,)), ((), ())), preferred_element_...]
    all_to_all x8 -> x6, waiting for transfers between devices: 24.7 us -> 98.6 us  [plane_exchange(): lax.all_to_all(v, 'shard', 0, 0, tiled=True, axis_index_groups=PLANES)]
    ppermute x52 -> x36, waiting for transfers between devices: 140 us -> 82.5 us  [come_from(): return lax.ppermute(v, BOTH, pairs)]
    ppermute x52 -> x36, starting transfers between devices: 62.8 us -> 33.9 us  [come_from(): return lax.ppermute(v, BOTH, pairs)]
    ppermute x3 -> x4, waiting for transfers between devices: 38.1 us -> 9.5 us  [turned(): return lax.ppermute(v, BOTH, pairs)]
    convert_element_type x18 -> x6, other arithmetic: 19.2 us -> 2.66 us  [the longest x1 1.2 us: on_device(): normed = unit_norm(tokens.astype(F32)).astype(BF)]
    unnamed x139 -> x91, local copies, waits for them, and re-layouts: 23.4 us -> 8.32 us
  transfers between devices with their start and end apart: 67 -> 51, of which waited for: 31 -> 21; matrix products, arithmetic and copies ran while one was open for 29% -> 10% of each run, Pallas kernels for 2% -> 22%
where the time goes in v2:
time: 575 us; the launch traced here: 565 us
  waiting for transfers between devices  197 us (34%)
  Pallas kernels  153 us (27%)
  starting transfers between devices  113 us (20%)
  other arithmetic  43.1 us (7%)
  local copies, waits for them, and re-layouts  33.7 us (6%)
  between operations  24.6 us (4%)
    all_to_all x6, waiting for transfers between devices, plane_exchange(): lax.all_to_all(v, 'shard', 0, 0, tiled=True, axis_index_groups=PLANES)  98.6 us
    ppermute x36, waiting for transfers between devices, come_from(): return lax.ppermute(v, BOTH, pairs)  82.5 us
    all_to_all x6, starting transfers between devices, plane_exchange(): lax.all_to_all(v, 'shard', 0, 0, tiled=True, axis_index_groups=PLANES)  44.4 us
    ppermute x36, starting transfers between devices, come_from(): return lax.ppermute(v, BOTH, pairs)  33.9 us
    pallas_call x4, Pallas kernels, weight_grad(): pl.pallas_call(weight_grad_kernel, grid=(grid,), in_specs=[rows, rows, *g...  32 us
    pallas_call x1, Pallas kernels, feed_forward(): pl.pallas_call(feed_forward_kernel, grid=(4,), in_specs=[side(D)] * 4 + [...  27 us
    pallas_call x1, Pallas kernels, attend_back(): pl.pallas_call(backward_kernel, grid=(TOK // Q_BLOCK,), in_specs=[near_bl...  22.8 us
    pallas_call x4, Pallas kernels, line_scatter(): pl.pallas_call(core_sum_kernel, grid=(4,), in_specs=[pl.BlockSpec((ROWS,...  19.8 us
  transfers between devices with their start and end apart: 51, of which 21 were waited for; matrix products, arithmetic and copies ran while one was open for 10% of the time, Pallas kernels for 22%

profile of v2, /device:TPU:6, one launch (start us, length us, event | category | flops | bytes accessed | tf_op | source)
XLA Modules:
  0.0 564.9 jit_solution(4263136799424346090)
XLA Ops:
  17.9 6.7 %all-to-all-start = ((bf16[8,40,1792]{2,1,0:T(8,128)(2,1)}), bf16[8,40,1792]{2,1,0:T(8,128)(2,1)S(1)}, u32[]{:S(2)}, u32[]{:S(2)}) async-start(bf16[8,40,1792]{2,1,0:T(8,128)(2,1)} %copy.121), calls=%async_computation | async-start | bytes 2293760 | tf_op jit(solution)/shard_map/gate_weights_line/all_to_all | solution.py:138
  25.3 4.4 collective-permute-start.7
  29.8 8.2 %collective-permute-done = bf16[128,2048]{1,0:T(8,128)(2,1)} collective-permute-done((bf16[128,2048]{1,0:T(8,128)(2,1)S(1)}, bf16[128,2048]{1,0:T(8,128)(2,1)}, u32[]{:S(2)}, u32[]{:S(2)}) %collective-permute-start) | collective-permute-done | bytes 524320 | tf_op jit(solution)/shard_map/normed_line/ppermute | solution.py:68
  51.6 5.7 %all-to-all-start.1 = ((bf16[8,256,384]{2,1,0:T(8,128)(2,1)}), bf16[8,256,384]{2,1,0:T(8,128)(2,1)S(1)}, u32[]{:S(2)}, u32[]{:S(2)}) async-start(bf16[8,256,384]{2,1,0:T(8,128)(2,1)} %broadcast_in_dim.40), calls=%async_computation.1 | async-start | bytes 3145728 | tf_op jit(solution)/shard_map/qkv_weights_plane/all_to_all | solution.py:115
  70.4 9.8 %all-to-all-done.1 = bf16[8,256,384]{2,1,0:T(8,128)(2,1)S(1)} async-done(((bf16[8,256,384]{2,1,0:T(8,128)(2,1)}), bf16[8,256,384]{2,1,0:T(8,128)(2,1)S(1)}, u32[]{:S(2)}, u32[]{:S(2)}) %all-to-all-start.1) | async-done | bytes 1572896 | tf_op jit(solution)/shard_map/qkv_weights_plane/all_to_all | solution.py:115
  82.3 3.3 collective-permute-start.13
  87.6 6.2 %all-to-all-start.2 = ((bf16[8,32,2048]{2,1,0:T(8,128)(2,1)}), bf16[8,32,2048]{2,1,0:T(8,128)(2,1)}, u32[]{:S(2)}, u32[]{:S(2)}) async-start(bf16[8,32,2048]{2,1,0:T(8,128)(2,1)} %broadcast_in_dim.42), calls=%async_computation.2 | async-start | bytes 2097152 | tf_op jit(solution)/shard_map/out_weights_plane/all_to_all | solution.py:115
  93.9 16.9 %attention_forward.1 = (bf16[1024,256]{1,0:T(8,128)(2,1)}, bf16[1024,256]{1,0:T(8,128)(2,1)}, bf16[1024,128]{1,0:T(8,128)(2,1)}, f32[1024,128]{1,0:T(8,128)}) custom-call(bf16[512,2048]{1,0:T(8,128)(2,1)} %pad_maximum_fusion.refs_0_.near_ref, bf16[512,2048]{1,0:T(8,128)(2,1)} %collective-permute-done.3.refs_1_.far_ref, bf16[2048,384]{1,0:T(8,128)(2,1)} %bitcast.70, ...), custom_call_target="tpu_custom_call" | custom-call | flops 30000001024 | bytes 1 | tf_op jit(solution)/shard_map/attention_forward/pallas_call | solution.py:408
  117.1 5.7 %line_dot.2 = (bf16[512,2048]{1,0:T(8,128)(2,1)}, bf16[512,2048]{1,0:T(8,128)(2,1)}) custom-call(bf16[1024,256]{1,0:T(8,128)(2,1)} %get-tuple-element.59.refs_0_, bf16[256,2048]{1,0:T(8,128)(2,1)} %bitcast.22.refs_1_.refs_2_, bf16[512,2048]{1,0:T(8,128)(2,1)} %pad_maximum_fusion.1.refs_2_.grads_near_ref.g_near_ref), custom_call_target="tpu_custom_call" | custom-call | flops 1 | bytes 1 | tf_op jit(solution)/shard_map/heads_out_line/line_dot/pallas_call | solution.py:495
  127.6 16.7 %all-to-all-start.3 = ((bf16[8,88,2048]{2,1,0:T(8,128)(2,1)}), bf16[8,88,2048]{2,1,0:T(8,128)(2,1)}, u32[]{:S(2)}, u32[]{:S(2)}) async-start(bf16[8,88,2048]{2,1,0:T(8,128)(2,1)} %broadcast_in_dim.43), calls=%async_computation.3 | async-start | bytes 5767168 | tf_op jit(solution)/shard_map/down_weights_plane/all_to_all | solution.py:115
  144.6 4.9 core_sum.4
  151.5 44.6 %all-to-all-done.3 = bf16[8,88,2048]{2,1,0:T(8,128)(2,1)} async-done(((bf16[8,88,2048]{2,1,0:T(8,128)(2,1)}), bf16[8,88,2048]{2,1,0:T(8,128)(2,1)}, u32[]{:S(2)}, u32[]{:S(2)}) %all-to-all-start.3) | async-done | bytes 2883616 | tf_op jit(solution)/shard_map/down_weights_plane/all_to_all | solution.py:115
  197.1 3.4 middle_kernel.1
  202.4 13.0 %collective-permute-done.16 = bf16[128,2048]{1,0:T(8,128)(2,1)S(1)} collective-permute-done((bf16[128,2048]{1,0:T(8,128)(2,1)}, bf16[128,2048]{1,0:T(8,128)(2,1)S(1)}, u32[]{:S(2)}, u32[]{:S(2)}) %collective-permute-start.16) | collective-permute-done | bytes 524320 | tf_op jit(solution)/shard_map/normed_two_line/ppermute | solution.py:68
  217.0 9.5 %collective-permute-done.14 = bf16[128,2048]{1,0:T(8,128)(2,1)S(1)} collective-permute-done((bf16[128,2048]{1,0:T(8,128)(2,1)}, bf16[128,2048]{1,0:T(8,128)(2,1)S(1)}, u32[]{:S(2)}, u32[]{:S(2)}) %collective-permute-start.14) | collective-permute-done | bytes 524320 | tf_op jit(solution)/shard_map/normed_two_line/ppermute | solution.py:68
  228.0 4.3 collective-permute-done.17.far_ref
  232.3 4.9 all-gather.2.cloned.1.call-done.gate_ref
  237.2 27.0 %feed_forward.1 = (bf16[512,704]{1,0:T(8,128)(2,1)}, bf16[512,704]{1,0:T(8,128)(2,1)}, bf16[512,1408]{1,0:T(8,128)(2,1)}, bf16[512,1408]{1,0:T(8,128)(2,1)}, bf1...) custom-call(bf16[512,2048]{1,0:T(8,128)(2,1)} %copy-done.15, ...), custom_call_target="tpu_custom_call" | custom-call | flops 30000001024 | bytes 1 | tf_op jit(solution)/shard_map/feed_forward/pallas_call | solution.py:551
  264.8 11.9 %weight_grad.4.refs_0_ = bf16[2048,1408]{1,0:T(8,128)(2,1)} custom-call(bf16[512,2048]{1,0:T(8,128)(2,1)} %copy-done.15, bf16[512,2048]{1,0:T(8,128)(2,1)} %collective-permute-done.17.far_ref, bf16[512,1408]{1,0:T(8,128)(2,1)} %get-tuple-element.76.g_near_ref, bf16[512,1408]{1,0:T(8,128)(2,1)} %get-tuple-element.77.g_far_ref), custom_call_target="tpu_custom_call" | custom-call | flops 15000000512 | bytes 1 | tf_op jit(solution)/shard_map/grad_gate_plane/weight_grad/pallas_call | solution.py:580
  278.1 4.9 core_sum.6
  285.9 5.2 core_sum.5
  291.2 7.1 %weight_grad.5.refs_6_ = bf16[704,2048]{1,0:T(8,128)(2,1)} custom-call(bf16[512,704]{1,0:T(8,128)(2,1)} %get-tuple-element.82.near_ref, bf16[512,704]{1,0:T(8,128)(2,1)} %get-tuple-element.83.far_ref, bf16[512,2048]{1,0:T(8,128)(2,1)} %pad_maximum_fusion.1.refs_2_.grads_near_ref.g_near_ref, ...), custom_call_target="tpu_custom_call" | custom-call | flops 1 | bytes 1 | tf_op jit(solution)/shard_map/grad_down_plane/weight_grad/pallas_call | solution.py:580
  300.1 10.0 %collective-permute-done.25.refs_3_ = bf16[128,2048]{1,0:T(8,128)(2,1)S(1)} collective-permute-done((bf16[128,2048]{1,0:T(8,128)(2,1)}, bf16[128,2048]{1,0:T(8,128)(2,1)S(1)}, u32[]{:S(2)}, u32[]{:S(2)}) %collective-permute-start.25) | collective-permute-done | bytes 524320 | tf_op jit(solution)/shard_map/grad_normed_two_line/ppermute | solution.py:68
  311.0 4.1 middle_back_kernel.1
  318.3 11.8 %collective-permute-done.28 = bf16[128,2048]{1,0:T(8,128)(2,1)S(1)} collective-permute-done((bf16[128,2048]{1,0:T(8,128)(2,1)}, bf16[128,2048]{1,0:T(8,128)(2,1)S(1)}, u32[]{:S(2)}, u32[]{:S(2)}) %collective-permute-start.28) | collective-permute-done | bytes 524320 | tf_op jit(solution)/shard_map/grad_attn_line/ppermute | solution.py:68
  332.8 9.2 %collective-permute-done.26 = bf16[128,2048]{1,0:T(8,128)(2,1)S(1)} collective-permute-done((bf16[128,2048]{1,0:T(8,128)(2,1)}, bf16[128,2048]{1,0:T(8,128)(2,1)S(1)}, u32[]{:S(2)}, u32[]{:S(2)}) %collective-permute-start.26) | collective-permute-done | bytes 524320 | tf_op jit(solution)/shard_map/grad_attn_line/ppermute | solution.py:68
  348.7 6.5 %all-to-all-start.4 = ((bf16[8,88,2048]{2,1,0:T(8,128)(2,1)}), bf16[8,88,2048]{2,1,0:T(8,128)(2,1)S(1)}, u32[]{:S(2)}, u32[]{:S(2)}) async-start(bf16[8,88,2048]{2,1,0:T(8,128)(2,1)} %bitcast.27), calls=%async_computation.4 | async-start | bytes 5767168 | tf_op jit(solution)/shard_map/grad_down_plane/all_to_all | solution.py:115
  355.1 22.8 %attention_backward.1.refs_5_.g_near_ref.g_far_ref.refs_0_ = bf16[1024,384]{1,0:T(8,128)(2,1)} custom-call(bf16[512,2048]{1,0:T(8,128)(2,1)} %pad_maximum_fusion.3.refs_0_.g_near_ref, bf16[512,2048]{1,0:T(8,128)(2,1)} %collective-permute-done.29.refs_1_.g_far_ref, bf16[256,2048]{1,0:T(8,128)(2,1)} %bitcast.22.refs_1_.refs_2_, ...), custom_call_target="tpu_custom_call" | custom-call | flops 30000001024 | bytes 1 | tf_op jit(solution)/shard_map/attention_backward/pallas_call | solution.py:447
  378.8 3.3 mixed_kernel.1.refs_0_
  382.0 7.9 %weight_grad.6.refs_0_ = bf16[2048,384]{1,0:T(8,128)(2,1)} custom-call(bf16[512,2048]{1,0:T(8,128)(2,1)} %pad_maximum_fusion.refs_0_.near_ref, bf16[512,2048]{1,0:T(8,128)(2,1)} %collective-permute-done.3.refs_1_.far_ref, bf16[1024,384]{1,0:T(8,128)(2,1)} %attention_backward.1.refs_5_.g_near_ref.g_far_ref.refs_0_, ...), custom_call_target="tpu_custom_call" | custom-call | flops 5000000000 | bytes 1 | tf_op jit(solution)/shard_map/grad_qkv/weight_grad/pallas_call | solution.py:580
  390.0 5.0 weight_grad.7.refs_2_
  395.0 10.8 %all-to-all-done.4.refs_3_.parts_ref = bf16[8,88,2048]{2,1,0:T(8,128)(2,1)S(1)} async-done(((bf16[8,88,2048]{2,1,0:T(8,128)(2,1)}), bf16[8,88,2048]{2,1,0:T(8,128)(2,1)S(1)}, u32[]{:S(2)}, u32[]{:S(2)}) %all-to-all-start.4) | async-done | bytes 2883616 | tf_op jit(solution)/shard_map/grad_down_plane/all_to_all | solution.py:115
  407.4 6.6 %line_dot.3 = (bf16[512,2048]{1,0:T(8,128)(2,1)}, bf16[512,2048]{1,0:T(8,128)(2,1)}) custom-call(bf16[1024,384]{1,0:T(8,128)(2,1)} %attention_backward.1.refs_5_.g_near_ref.g_far_ref.refs_0_, bf16[2048,384]{1,0:T(8,128)(2,1)} %bitcast.71, bf16[256,2048]{1,0:T(8,128)(2,1)} %weight_grad.7.refs_2_, bf16[8,88,2048]{2,1,0:T(8,128)(2,1)} %copy-done), custom_call_target="tpu_custom_call" | custom-call | flops 1 | bytes 1 | tf_op jit(solution)/shard_map/grad_normed_line/line_dot/pallas_call | solution.py:495
  414.2 4.2 all-to-all-start.5
  418.5 4.8 core_sum.7
  423.4 3.0 collective-permute-start.31
  427.3 18.5 %all-to-all-done.5.parts_ref = bf16[8,256,384]{2,1,0:T(8,128)(2,1)S(1)} async-done(((bf16[8,256,384]{2,1,0:T(8,128)(2,1)}), bf16[8,256,384]{2,1,0:T(8,128)(2,1)S(1)}, u32[]{:S(2)}, u32[]{:S(2)}) %all-to-all-start.5) | async-done | bytes 1572896 | tf_op jit(solution)/shard_map/grad_qkv/all_to_all | solution.py:115
  456.4 3.2 parts_sum.5
  462.3 3.9 tokens_back_kernel.1
  469.5 6.0 %all-to-all-start.6 = ((bf16[8,32,384]{2,1,0:T(8,128)(2,1)}), bf16[8,32,384]{2,1,0:T(8,128)(2,1)S(1)}, u32[]{:S(2)}, u32[]{:S(2)}) async-start(bf16[8,32,384]{2,1,0:T(8,128)(2,1)} %bitcast.29), calls=%async_computation.6 | async-start | bytes 393216 | tf_op jit(solution)/shard_map/grad_qkv/all_to_all | solution.py:138
  476.4 4.2 collective-permute-start.39
  480.6 5.1 all-to-all-start.7
  493.2 14.0 %all-to-all-done.7.parts_ref = bf16[8,32,2048]{2,1,0:T(8,128)(2,1)S(1)} async-done(((bf16[8,32,2048]{2,1,0:T(8,128)(2,1)}), bf16[8,32,2048]{2,1,0:T(8,128)(2,1)S(1)}, u32[]{:S(2)}, u32[]{:S(2)}) %all-to-all-start.7) | async-done | bytes 1048608 | tf_op jit(solution)/shard_map/grad_out_rep/all_to_all | solution.py:115
  507.2 10.1 %collective-permute-done.35.refs_0_ = bf16[256,1408]{1,0:T(8,128)(2,1)S(1)} collective-permute-done((bf16[256,1408]{1,0:T(8,128)(2,1)}, bf16[256,1408]{1,0:T(8,128)(2,1)S(1)}, u32[]{:S(2)}, u32[]{:S(2)}) %collective-permute-start.35) | collective-permute-done | bytes 720928 | tf_op jit(solution)/shard_map/grad_gate_rep/ppermute | solution.py:68
  525.0 5.4 all-to-all-start.8
  530.5 4.5 collective-permute-start.37
  537.9 9.5 %collective-permute-done.37 = bf16[32,2048]{1,0:T(8,128)(2,1)S(1)} collective-permute-done((bf16[32,2048]{1,0:T(8,128)(2,1)S(1)}, bf16[32,2048]{1,0:T(8,128)(2,1)S(1)}, u32[]{:S(2)}, u32[]{:S(2)}) %collective-permute-start.37) | collective-permute-done | bytes 131104 | tf_op jit(solution)/shard_map/grad_out_rep/ppermute | solution.py:73
  551.8 5.3 multiply_subtract_fusion
  (256 shorter events, 116.0 us)
Async XLA Ops:
  9.8 20.0 %collective-permute-start.2 = (bf16[128,2048]{1,0:T(8,128)(2,1)S(1)}, bf16[128,2048]{1,0:T(8,128)(2,1)}, u32[]{:S(2)}, u32[]{:S(2)}) collective-permute-start(bf16[128,2048]{1,0:T(8,128)(2,1)S(1)} %fusion.4), channel_id=1, source_target_pairs={{6,0},{7,1},{0,2},{1,3},{2,4},{3,5},{4,6},{5,7},{14,8},{15,9},{8,1... | collective-permute-start | bytes 1572872 | tf_op jit(solution)/shard_map/normed_line/ppermute | solution.py:68
  10.2 19.6 %collective-permute-start.1 = (bf16[128,2048]{1,0:T(8,128)(2,1)S(1)}, bf16[128,2048]{1,0:T(8,128)(2,1)}, u32[]{:S(2)}, u32[]{:S(2)}) collective-permute-start(bf16[128,2048]{1,0:T(8,128)(2,1)S(1)} %fusion.4), channel_id=1, source_target_pairs={{4,0},{5,1},{6,2},{7,3},{0,4},{1,5},{2,6},{3,7},{12,8},{13,9},{14,... | collective-permute-start | bytes 1572872 | tf_op jit(solution)/shard_map/normed_line/ppermute | solution.py:68
  12.7 25.3 %collective-permute-start = (bf16[128,2048]{1,0:T(8,128)(2,1)S(1)}, bf16[128,2048]{1,0:T(8,128)(2,1)}, u32[]{:S(2)}, u32[]{:S(2)}) collective-permute-start(bf16[128,2048]{1,0:T(8,128)(2,1)S(1)} %fusion.4), channel_id=1, source_target_pairs={{2,0},{3,1},{4,2},{5,3},{6,4},{7,5},{0,6},{1,7},{10,8},{11,9},{12,... | collective-permute-start | bytes 1572872 | tf_op jit(solution)/shard_map/normed_line/ppermute | solution.py:68
  17.9 32.4 %all-to-all-start = ((bf16[8,40,1792]{2,1,0:T(8,128)(2,1)}), bf16[8,40,1792]{2,1,0:T(8,128)(2,1)S(1)}, u32[]{:S(2)}, u32[]{:S(2)}) async-start(bf16[8,40,1792]{2,1,0:T(8,128)(2,1)} %copy.121), calls=%async_computation | async-start | bytes 2293760 | tf_op jit(solution)/shard_map/gate_weights_line/all_to_all | solution.py:138
  25.3 57.0 %collective-permute-start.7 = (bf16[32,2048]{1,0:T(8,128)(2,1)}, bf16[32,2048]{1,0:T(8,128)(2,1)}, u32[]{:S(2)}, u32[]{:S(2)}) collective-permute-start(bf16[32,2048]{1,0:T(8,128)(2,1)} %convert_element_type.113), channel_id=1, source_target_pairs={{0,0},{8,1},{16,2},{24,3},{32,4},{40,5},{48,6},{56,7},{1,8},{9,9},... | collective-permute-start | bytes 393224 | tf_op jit(solution)/shard_map/out_turn/ppermute | solution.py:73
  44.4 49.5 %collective-permute-start.6 = (bf16[128,2048]{1,0:T(8,128)(2,1)}, bf16[128,2048]{1,0:T(8,128)(2,1)}, u32[]{:S(2)}, u32[]{:S(2)}) collective-permute-start(bf16[128,2048]{1,0:T(8,128)(2,1)} %broadcast_select_fusion.2), channel_id=1, source_target_pairs={{6,0},{7,1},{0,2},{1,3},{2,4},{3,5},{4,6},{5,7},{14,8},{15,9},{8,1... | collective-permute-start | bytes 1572872 | tf_op jit(solution)/shard_map/cotangent_line/ppermute | solution.py:68
  45.0 48.8 %collective-permute-start.5 = (bf16[128,2048]{1,0:T(8,128)(2,1)}, bf16[128,2048]{1,0:T(8,128)(2,1)}, u32[]{:S(2)}, u32[]{:S(2)}) collective-permute-start(bf16[128,2048]{1,0:T(8,128)(2,1)} %broadcast_select_fusion.2), channel_id=1, source_target_pairs={{4,0},{5,1},{6,2},{7,3},{0,4},{1,5},{2,6},{3,7},{12,8},{13,9},{14,... | collective-permute-start | bytes 1572872 | tf_op jit(solution)/shard_map/cotangent_line/ppermute | solution.py:68
  47.3 46.6 %collective-permute-start.4 = (bf16[128,2048]{1,0:T(8,128)(2,1)}, bf16[128,2048]{1,0:T(8,128)(2,1)}, u32[]{:S(2)}, u32[]{:S(2)}) collective-permute-start(bf16[128,2048]{1,0:T(8,128)(2,1)} %broadcast_select_fusion.2), channel_id=1, source_target_pairs={{2,0},{3,1},{4,2},{5,3},{6,4},{7,5},{0,6},{1,7},{10,8},{11,9},{12,... | collective-permute-start | bytes 1572872 | tf_op jit(solution)/shard_map/cotangent_line/ppermute | solution.py:68
  48.4 45.5 %collective-permute-start.3 = (bf16[512,2048]{1,0:T(8,128)(2,1)}, bf16[512,2048]{1,0:T(8,128)(2,1)}, u32[]{:S(2)}, u32[]{:S(2)}) collective-permute-start(bf16[512,2048]{1,0:T(8,128)(2,1)} %pad_maximum_fusion.refs_0_.near_ref), channel_id=1, source_target_pairs={{1,0},{0,1},{3,2},{2,3},{5,4},{4,5},{7,6},{6,7},{9,8},{8,9},{11,10... | collective-permute-start | bytes 6291464 | tf_op jit(solution)/shard_map/normed_line/ppermute | solution.py:68
  51.6 28.6 %all-to-all-start.1 = ((bf16[8,256,384]{2,1,0:T(8,128)(2,1)}), bf16[8,256,384]{2,1,0:T(8,128)(2,1)S(1)}, u32[]{:S(2)}, u32[]{:S(2)}) async-start(bf16[8,256,384]{2,1,0:T(8,128)(2,1)} %broadcast_in_dim.40), calls=%async_computation.1 | async-start | bytes 3145728 | tf_op jit(solution)/shard_map/qkv_weights_plane/all_to_all | solution.py:115
  57.4 179.8 %all-gather.2.cloned.1.call-start = ((), (), s32[]{:S(2)}) async-start(), calls=%async_computation.10 | async-start | bytes 6488064 | tf_op jit(solution)/shard_map/gate_weights_plane/all_gather | solution.py:124
  82.3 43.2 %collective-permute-start.13 = (bf16[88,2048]{1,0:T(8,128)(2,1)S(1)}, bf16[88,2048]{1,0:T(8,128)(2,1)S(1)}, u32[]{:S(2)}, u32[]{:S(2)}) collective-permute-start(bf16[88,2048]{1,0:T(8,128)(2,1)S(1)} %copy-done.30), channel_id=1, source_target_pairs={{0,0},{8,1},{16,2},{24,3},{32,4},{40,5},{48,6},{56,7},{1,8},{9,9},... | collective-permute-start | bytes 1081352 | tf_op jit(solution)/shard_map/down_turn/ppermute | solution.py:73
  87.6 29.5 %all-to-all-start.2 = ((bf16[8,32,2048]{2,1,0:T(8,128)(2,1)}), bf16[8,32,2048]{2,1,0:T(8,128)(2,1)}, u32[]{:S(2)}, u32[]{:S(2)}) async-start(bf16[8,32,2048]{2,1,0:T(8,128)(2,1)} %broadcast_in_dim.42), calls=%async_computation.2 | async-start | bytes 2097152 | tf_op jit(solution)/shard_map/out_weights_plane/all_to_all | solution.py:115
  125.4 19.2 %collective-permute-start.8 = (bf16[512,2048]{1,0:T(8,128)(2,1)}, bf16[512,2048]{1,0:T(8,128)(2,1)}, u32[]{:S(2)}, u32[]{:S(2)}) collective-permute-start(bf16[512,2048]{1,0:T(8,128)(2,1)} %get-tuple-element.61), channel_id=1, source_target_pairs={{1,0},{0,1},{3,2},{2,3},{5,4},{4,5},{7,6},{6,7},{9,8},{8,9},{11,10... | collective-permute-start | bytes 6291464 | tf_op jit(solution)/shard_map/heads_out_line/ppermute | solution.py:68
  127.6 68.5 %all-to-all-start.3 = ((bf16[8,88,2048]{2,1,0:T(8,128)(2,1)}), bf16[8,88,2048]{2,1,0:T(8,128)(2,1)}, u32[]{:S(2)}, u32[]{:S(2)}) async-start(bf16[8,88,2048]{2,1,0:T(8,128)(2,1)} %broadcast_in_dim.43), calls=%async_computation.3 | async-start | bytes 5767168 | tf_op jit(solution)/shard_map/down_weights_plane/all_to_all | solution.py:115
  144.2 341.6 %reduce-scatter.2.cloned.1.call-start = ((), (), s32[]{:S(2)}) async-start(), calls=%async_computation.11 | async-start | bytes 6488064 | tf_op jit(solution)/shard_map/grad_gate_plane/reduce_scatter | solution.py:128
  149.4 46.7 %collective-permute-start.9 = (bf16[128,2048]{1,0:T(8,128)(2,1)}, bf16[128,2048]{1,0:T(8,128)(2,1)S(1)}, u32[]{:S(2)}, u32[]{:S(2)}) collective-permute-start(bf16[128,2048]{1,0:T(8,128)(2,1)} %get-tuple-element.63), channel_id=1, source_target_pairs={{6,0},{7,1},{0,2},{1,3},{2,4},{3,5},{4,6},{5,7},{14,8},{15,9},{8,1... | collective-permute-start | bytes 1572872 | tf_op jit(solution)/shard_map/heads_out_line/ppermute | solution.py:68
  149.4 46.7 %collective-permute-start.10 = (bf16[128,2048]{1,0:T(8,128)(2,1)}, bf16[128,2048]{1,0:T(8,128)(2,1)S(1)}, u32[]{:S(2)}, u32[]{:S(2)}) collective-permute-start(bf16[128,2048]{1,0:T(8,128)(2,1)} %get-tuple-element.64), channel_id=1, source_target_pairs={{4,0},{5,1},{6,2},{7,3},{0,4},{1,5},{2,6},{3,7},{12,8},{13,9},{14,... | collective-permute-start | bytes 1572872 | tf_op jit(solution)/shard_map/heads_out_line/ppermute | solution.py:68
  149.4 46.7 %collective-permute-start.11 = (bf16[128,2048]{1,0:T(8,128)(2,1)}, bf16[128,2048]{1,0:T(8,128)(2,1)}, u32[]{:S(2)}, u32[]{:S(2)}) collective-permute-start(bf16[128,2048]{1,0:T(8,128)(2,1)} %get-tuple-element.65), channel_id=1, source_target_pairs={{2,0},{3,1},{4,2},{5,3},{6,4},{7,5},{0,6},{1,7},{10,8},{11,9},{12,... | collective-permute-start | bytes 1572872 | tf_op jit(solution)/shard_map/heads_out_line/ppermute | solution.py:68
  200.4 15.1 %collective-permute-start.16 = (bf16[128,2048]{1,0:T(8,128)(2,1)}, bf16[128,2048]{1,0:T(8,128)(2,1)S(1)}, u32[]{:S(2)}, u32[]{:S(2)}) collective-permute-start(bf16[128,2048]{1,0:T(8,128)(2,1)} %get-tuple-element.66), channel_id=1, source_target_pairs={{6,0},{7,1},{0,2},{1,3},{2,4},{3,5},{4,6},{5,7},{14,8},{15,9},{8,1... | collective-permute-start | bytes 1572872 | tf_op jit(solution)/shard_map/normed_two_line/ppermute | solution.py:68
  200.4 16.6 %collective-permute-start.15 = (bf16[128,2048]{1,0:T(8,128)(2,1)}, bf16[128,2048]{1,0:T(8,128)(2,1)S(1)}, u32[]{:S(2)}, u32[]{:S(2)}) collective-permute-start(bf16[128,2048]{1,0:T(8,128)(2,1)} %get-tuple-element.66), channel_id=1, source_target_pairs={{4,0},{5,1},{6,2},{7,3},{0,4},{1,5},{2,6},{3,7},{12,8},{13,9},{14,... | collective-permute-start | bytes 1572872 | tf_op jit(solution)/shard_map/normed_two_line/ppermute | solution.py:68
  200.4 26.1 %collective-permute-start.14 = (bf16[128,2048]{1,0:T(8,128)(2,1)}, bf16[128,2048]{1,0:T(8,128)(2,1)S(1)}, u32[]{:S(2)}, u32[]{:S(2)}) collective-permute-start(bf16[128,2048]{1,0:T(8,128)(2,1)} %get-tuple-element.66), channel_id=1, source_target_pairs={{2,0},{3,1},{4,2},{5,3},{6,4},{7,5},{0,6},{1,7},{10,8},{11,9},{12,... | collective-permute-start | bytes 1572872 | tf_op jit(solution)/shard_map/normed_two_line/ppermute | solution.py:68
  264.2 21.7 %collective-permute-start.18 = (bf16[512,2048]{1,0:T(8,128)(2,1)}, bf16[512,2048]{1,0:T(8,128)(2,1)}, u32[]{:S(2)}, u32[]{:S(2)}) collective-permute-start(bf16[512,2048]{1,0:T(8,128)(2,1)} %get-tuple-element.68), channel_id=1, source_target_pairs={{1,0},{0,1},{3,2},{2,3},{5,4},{4,5},{7,6},{6,7},{9,8},{8,9},{11,10... | collective-permute-start | bytes 6291464 | tf_op jit(solution)/shard_map/mixed_line/ppermute | solution.py:68
  264.3 12.5 %collective-permute-start.22 = (bf16[512,2048]{1,0:T(8,128)(2,1)}, bf16[512,2048]{1,0:T(8,128)(2,1)S(1)}, u32[]{:S(2)}, u32[]{:S(2)}) collective-permute-start(bf16[512,2048]{1,0:T(8,128)(2,1)} %get-tuple-element.75), channel_id=1, source_target_pairs={{1,0},{0,1},{3,2},{2,3},{5,4},{4,5},{7,6},{6,7},{9,8},{8,9},{11,10... | collective-permute-start | bytes 6291464 | tf_op jit(solution)/shard_map/grad_normed_two_line/ppermute | solution.py:68
  283.0 15.2 %collective-permute-start.23 = (bf16[128,2048]{1,0:T(8,128)(2,1)}, bf16[128,2048]{1,0:T(8,128)(2,1)S(1)}, u32[]{:S(2)}, u32[]{:S(2)}) collective-permute-start(bf16[128,2048]{1,0:T(8,128)(2,1)} %get-tuple-element.79), channel_id=1, source_target_pairs={{6,0},{7,1},{0,2},{1,3},{2,4},{3,5},{4,6},{5,7},{14,8},{15,9},{8,1... | collective-permute-start | bytes 1572872 | tf_op jit(solution)/shard_map/grad_normed_two_line/ppermute | solution.py:68
  283.6 16.6 %collective-permute-start.24 = (bf16[128,2048]{1,0:T(8,128)(2,1)}, bf16[128,2048]{1,0:T(8,128)(2,1)S(1)}, u32[]{:S(2)}, u32[]{:S(2)}) collective-permute-start(bf16[128,2048]{1,0:T(8,128)(2,1)} %get-tuple-element.80), channel_id=1, source_target_pairs={{4,0},{5,1},{6,2},{7,3},{0,4},{1,5},{2,6},{3,7},{12,8},{13,9},{14,... | collective-permute-start | bytes 1572872 | tf_op jit(solution)/shard_map/grad_normed_two_line/ppermute | solution.py:68
  285.9 24.2 %collective-permute-start.25 = (bf16[128,2048]{1,0:T(8,128)(2,1)}, bf16[128,2048]{1,0:T(8,128)(2,1)S(1)}, u32[]{:S(2)}, u32[]{:S(2)}) collective-permute-start(bf16[128,2048]{1,0:T(8,128)(2,1)} %get-tuple-element.81), channel_id=1, source_target_pairs={{2,0},{3,1},{4,2},{5,3},{6,4},{7,5},{0,6},{1,7},{10,8},{11,9},{12,... | collective-permute-start | bytes 1572872 | tf_op jit(solution)/shard_map/grad_normed_two_line/ppermute | solution.py:68
  315.1 15.0 %collective-permute-start.28 = (bf16[128,2048]{1,0:T(8,128)(2,1)}, bf16[128,2048]{1,0:T(8,128)(2,1)S(1)}, u32[]{:S(2)}, u32[]{:S(2)}) collective-permute-start(bf16[128,2048]{1,0:T(8,128)(2,1)} %get-tuple-element.84), channel_id=1, source_target_pairs={{6,0},{7,1},{0,2},{1,3},{2,4},{3,5},{4,6},{5,7},{14,8},{15,9},{8,1... | collective-permute-start | bytes 1572872 | tf_op jit(solution)/shard_map/grad_attn_line/ppermute | solution.py:68
  316.2 16.6 %collective-permute-start.27 = (bf16[128,2048]{1,0:T(8,128)(2,1)}, bf16[128,2048]{1,0:T(8,128)(2,1)S(1)}, u32[]{:S(2)}, u32[]{:S(2)}) collective-permute-start(bf16[128,2048]{1,0:T(8,128)(2,1)} %get-tuple-element.84), channel_id=1, source_target_pairs={{4,0},{5,1},{6,2},{7,3},{0,4},{1,5},{2,6},{3,7},{12,8},{13,9},{14,... | collective-permute-start | bytes 1572872 | tf_op jit(solution)/shard_map/grad_attn_line/ppermute | solution.py:68
  318.1 23.9 %collective-permute-start.26 = (bf16[128,2048]{1,0:T(8,128)(2,1)}, bf16[128,2048]{1,0:T(8,128)(2,1)S(1)}, u32[]{:S(2)}, u32[]{:S(2)}) collective-permute-start(bf16[128,2048]{1,0:T(8,128)(2,1)} %get-tuple-element.84), channel_id=1, source_target_pairs={{2,0},{3,1},{4,2},{5,3},{6,4},{7,5},{0,6},{1,7},{10,8},{11,9},{12,... | collective-permute-start | bytes 1572872 | tf_op jit(solution)/shard_map/grad_attn_line/ppermute | solution.py:68
  344.6 10.5 %collective-permute-start.29 = (bf16[512,2048]{1,0:T(8,128)(2,1)}, bf16[512,2048]{1,0:T(8,128)(2,1)}, u32[]{:S(2)}, u32[]{:S(2)}) collective-permute-start(bf16[512,2048]{1,0:T(8,128)(2,1)} %pad_maximum_fusion.3.refs_0_.g_near_ref), channel_id=1, source_target_pairs={{1,0},{0,1},{3,2},{2,3},{5,4},{4,5},{7,6},{6,7},{9,8},{8,9},{11,10... | collective-permute-start | bytes 6291464 | tf_op jit(solution)/shard_map/grad_attn_line/ppermute | solution.py:68
  345.5 32.5 %collective-permute-start.19 = (bf16[128,2048]{1,0:T(8,128)(2,1)}, bf16[128,2048]{1,0:T(8,128)(2,1)S(1)}, u32[]{:S(2)}, u32[]{:S(2)}) collective-permute-start(bf16[128,2048]{1,0:T(8,128)(2,1)} %get-tuple-element.70), channel_id=1, source_target_pairs={{6,0},{7,1},{0,2},{1,3},{2,4},{3,5},{4,6},{5,7},{14,8},{15,9},{8,1... | collective-permute-start | bytes 1572872 | tf_op jit(solution)/shard_map/mixed_line/ppermute | solution.py:68
  346.6 31.4 %collective-permute-start.20 = (bf16[128,2048]{1,0:T(8,128)(2,1)}, bf16[128,2048]{1,0:T(8,128)(2,1)}, u32[]{:S(2)}, u32[]{:S(2)}) collective-permute-start(bf16[128,2048]{1,0:T(8,128)(2,1)} %get-tuple-element.71), channel_id=1, source_target_pairs={{4,0},{5,1},{6,2},{7,3},{0,4},{1,5},{2,6},{3,7},{12,8},{13,9},{14,... | collective-permute-start | bytes 1572872 | tf_op jit(solution)/shard_map/mixed_line/ppermute | solution.py:68
  347.7 30.3 %collective-permute-start.21 = (bf16[128,2048]{1,0:T(8,128)(2,1)}, bf16[128,2048]{1,0:T(8,128)(2,1)}, u32[]{:S(2)}, u32[]{:S(2)}) collective-permute-start(bf16[128,2048]{1,0:T(8,128)(2,1)} %get-tuple-element.72), channel_id=1, source_target_pairs={{2,0},{3,1},{4,2},{5,3},{6,4},{7,5},{0,6},{1,7},{10,8},{11,9},{12,... | collective-permute-start | bytes 1572872 | tf_op jit(solution)/shard_map/mixed_line/ppermute | solution.py:68
  348.7 57.2 %all-to-all-start.4 = ((bf16[8,88,2048]{2,1,0:T(8,128)(2,1)}), bf16[8,88,2048]{2,1,0:T(8,128)(2,1)S(1)}, u32[]{:S(2)}, u32[]{:S(2)}) async-start(bf16[8,88,2048]{2,1,0:T(8,128)(2,1)} %bitcast.27), calls=%async_computation.4 | async-start | bytes 5767168 | tf_op jit(solution)/shard_map/grad_down_plane/all_to_all | solution.py:115
  414.2 31.5 %all-to-all-start.5 = ((bf16[8,256,384]{2,1,0:T(8,128)(2,1)}), bf16[8,256,384]{2,1,0:T(8,128)(2,1)S(1)}, u32[]{:S(2)}, u32[]{:S(2)}) async-start(bf16[8,256,384]{2,1,0:T(8,128)(2,1)} %bitcast.68), calls=%async_computation.5 | async-start | bytes 3145728 | tf_op jit(solution)/shard_map/grad_qkv/all_to_all | solution.py:115
  423.4 27.0 %collective-permute-start.31 = (bf16[128,2048]{1,0:T(8,128)(2,1)}, bf16[128,2048]{1,0:T(8,128)(2,1)S(1)}, u32[]{:S(2)}, u32[]{:S(2)}) collective-permute-start(bf16[128,2048]{1,0:T(8,128)(2,1)} %get-tuple-element.91), channel_id=1, source_target_pairs={{6,0},{7,1},{0,2},{1,3},{2,4},{3,5},{4,6},{5,7},{14,8},{15,9},{8,1... | collective-permute-start | bytes 1572872 | tf_op jit(solution)/shard_map/grad_normed_line/ppermute | solution.py:68
  426.4 34.9 %collective-permute-start.32 = (bf16[128,2048]{1,0:T(8,128)(2,1)}, bf16[128,2048]{1,0:T(8,128)(2,1)S(1)}, u32[]{:S(2)}, u32[]{:S(2)}) collective-permute-start(bf16[128,2048]{1,0:T(8,128)(2,1)} %get-tuple-element.92), channel_id=1, source_target_pairs={{4,0},{5,1},{6,2},{7,3},{0,4},{1,5},{2,6},{3,7},{12,8},{13,9},{14,... | collective-permute-start | bytes 1572872 | tf_op jit(solution)/shard_map/grad_normed_line/ppermute | solution.py:68
  426.6 34.8 %collective-permute-start.33 = (bf16[128,2048]{1,0:T(8,128)(2,1)}, bf16[128,2048]{1,0:T(8,128)(2,1)S(1)}, u32[]{:S(2)}, u32[]{:S(2)}) collective-permute-start(bf16[128,2048]{1,0:T(8,128)(2,1)} %get-tuple-element.93), channel_id=1, source_target_pairs={{2,0},{3,1},{4,2},{5,3},{6,4},{7,5},{0,6},{1,7},{10,8},{11,9},{12,... | collective-permute-start | bytes 1572872 | tf_op jit(solution)/shard_map/grad_normed_line/ppermute | solution.py:68
  453.6 15.2 %collective-permute-start.34 = (bf16[256,384]{1,0:T(8,128)(2,1)}, bf16[256,384]{1,0:T(8,128)(2,1)S(1)}, u32[]{:S(2)}, u32[]{:S(2)}) collective-permute-start(bf16[256,384]{1,0:T(8,128)(2,1)} %get-tuple-element.96), channel_id=1, source_target_pairs={{64,0},{65,1},{66,2},{67,3},{68,4},{69,5},{70,6},{71,7},{72,8},{73... | collective-permute-start | bytes 589832 | tf_op jit(solution)/shard_map/grad_qkv/ppermute | solution.py:68
  459.6 15.9 %collective-permute-start.38 = (bf16[88,2048]{1,0:T(8,128)(2,1)}, bf16[88,2048]{1,0:T(8,128)(2,1)S(1)}, u32[]{:S(2)}, u32[]{:S(2)}) collective-permute-start(bf16[88,2048]{1,0:T(8,128)(2,1)} %get-tuple-element.100), channel_id=1, source_target_pairs={{64,0},{65,1},{66,2},{67,3},{68,4},{69,5},{70,6},{71,7},{72,8},{73... | collective-permute-start | bytes 1081352 | tf_op jit(solution)/shard_map/grad_down_rep/ppermute | solution.py:68
  469.5 11.1 %all-to-all-start.6 = ((bf16[8,32,384]{2,1,0:T(8,128)(2,1)}), bf16[8,32,384]{2,1,0:T(8,128)(2,1)S(1)}, u32[]{:S(2)}, u32[]{:S(2)}) async-start(bf16[8,32,384]{2,1,0:T(8,128)(2,1)} %bitcast.29), calls=%async_computation.6 | async-start | bytes 393216 | tf_op jit(solution)/shard_map/grad_qkv/all_to_all | solution.py:138
  476.4 58.6 %collective-permute-start.39 = (bf16[88,2048]{1,0:T(8,128)(2,1)}, bf16[88,2048]{1,0:T(8,128)(2,1)}, u32[]{:S(2)}, u32[]{:S(2)}) collective-permute-start(bf16[88,2048]{1,0:T(8,128)(2,1)} %fusion.8), channel_id=1, source_target_pairs={{0,0},{8,1},{16,2},{24,3},{32,4},{40,5},{48,6},{56,7},{1,8},{9,9},... | collective-permute-start | bytes 1081352 | tf_op jit(solution)/shard_map/grad_down_rep/ppermute | solution.py:73
  480.6 26.5 %all-to-all-start.7 = ((bf16[8,32,2048]{2,1,0:T(8,128)(2,1)}), bf16[8,32,2048]{2,1,0:T(8,128)(2,1)S(1)}, u32[]{:S(2)}, u32[]{:S(2)}) async-start(bf16[8,32,2048]{2,1,0:T(8,128)(2,1)} %bitcast.34), calls=%async_computation.7 | async-start | bytes 2097152 | tf_op jit(solution)/shard_map/grad_out_rep/all_to_all | solution.py:115
  487.9 29.4 %collective-permute-start.35 = (bf16[256,1408]{1,0:T(8,128)(2,1)}, bf16[256,1408]{1,0:T(8,128)(2,1)S(1)}, u32[]{:S(2)}, u32[]{:S(2)}) collective-permute-start(bf16[256,1408]{1,0:T(8,128)(2,1)} %broadcast_select_fusion), channel_id=1, source_target_pairs={{64,0},{65,1},{66,2},{67,3},{68,4},{69,5},{70,6},{71,7},{72,8},{73... | collective-permute-start | bytes 2162696 | tf_op jit(solution)/shard_map/grad_gate_rep/ppermute | solution.py:68
  520.2 10.1 %collective-permute-start.36 = (bf16[32,2048]{1,0:T(8,128)(2,1)}, bf16[32,2048]{1,0:T(8,128)(2,1)S(1)}, u32[]{:S(2)}, u32[]{:S(2)}) collective-permute-start(bf16[32,2048]{1,0:T(8,128)(2,1)} %get-tuple-element.98), channel_id=1, source_target_pairs={{64,0},{65,1},{66,2},{67,3},{68,4},{69,5},{70,6},{71,7},{72,8},{73... | collective-permute-start | bytes 393224 | tf_op jit(solution)/shard_map/grad_out_rep/ppermute | solution.py:68
  525.0 23.4 %all-to-all-start.8 = ((bf16[8,32,1408]{2,1,0:T(8,128)(2,1)}), bf16[8,32,1408]{2,1,0:T(8,128)(2,1)S(1)}, u32[]{:S(2)}, u32[]{:S(2)}) async-start(bf16[8,32,1408]{2,1,0:T(8,128)(2,1)} %bitcast.36), calls=%async_computation.9 | async-start | bytes 1441792 | tf_op jit(solution)/shard_map/grad_gate_line/all_to_all | solution.py:138
  530.5 17.0 %collective-permute-start.37 = (bf16[32,2048]{1,0:T(8,128)(2,1)S(1)}, bf16[32,2048]{1,0:T(8,128)(2,1)S(1)}, u32[]{:S(2)}, u32[]{:S(2)}) collective-permute-start(bf16[32,2048]{1,0:T(8,128)(2,1)S(1)} %add_convert_fusion.3), channel_id=1, source_target_pairs={{0,0},{8,1},{16,2},{24,3},{32,4},{40,5},{48,6},{56,7},{1,8},{9,9},... | collective-permute-start | bytes 393224 | tf_op jit(solution)/shard_map/grad_out_rep/ppermute | solution.py:73
  (47 other events, 365.1 us)
Sparse Core Ops, SparseCore 0:
  60.5 176.6 all-gather.1
  276.9 169.2 reduce-scatter.1

commit v3 on v2

--- a/solution.py
+++ b/solution.py
@@ -737,14 +737,10 @@
         (d_tokens,) = row_kernel(
             tokens_back_kernel, own, pieces, [tokens, grad_middle], [F32]
         )
-    with jax.named_scope("grad_out_rep"):
-        out_parts = plane_exchange(after(grad_out.reshape(8, 32, D), qkv_parts, own))
-        out_owned, out_low = parts_sum(out_parts, 32, gate_from_rep)
-        out_sum = out_owned + come_from(out_low, zz=2).astype(F32)
-        grad_out = turned(out_sum.astype(BF)).astype(F32)
     with jax.named_scope("grad_gate_line"):
         gate_sum = after(gate_sum.astype(BF), pieces[0])
-        parts = line_exchange(gate_sum.reshape(8, 32, 2 * FF_HERE)).astype(F32)
+        gate_line_parts = line_exchange(gate_sum.reshape(8, 32, 2 * FF_HERE))
+        parts = gate_line_parts.astype(F32)
         main, rest = 2 * FF_MAIN, 2 * FF_MAIN + FF_REST
         grad_gate = jnp.stack(
             [
@@ -753,6 +749,11 @@
             ]
         )
         grad_gate = grad_gate.transpose(2, 0, 1, 3).reshape(32, 2 * FF)
+    with jax.named_scope("grad_out_rep"):
+        out_parts = plane_exchange(after(grad_out.reshape(8, 32, D), gate_line_parts))
+        out_owned, out_low = parts_sum(out_parts, 32)
+        out_sum = out_owned + come_from(out_low, zz=2).astype(F32)
+        grad_out = turned(out_sum.astype(BF)).astype(F32)
     with jax.named_scope("grad_qkv"):
         qkv_sum, qkv_low_sum = parts_sum(qkv_parts, 256, pieces[0])
         qkv_sum = qkv_sum + come_from(qkv_low_sum, zz=2).astype(F32)

time: 575 us -> 578 us (level)
  waiting for transfers between devices: 197 us -> 204 us
    all_to_all x3, waiting for transfers between devices: 1.88 us -> 10.2 us  [line_exchange(): return lax.all_to_all(v, 'shard', 0, 0, tiled=True, axis_index_groups=LINES)]
    all_to_all x6, waiting for transfers between devices: 98.6 us -> 91 us  [plane_exchange(): lax.all_to_all(v, 'shard', 0, 0, tiled=True, axis_index_groups=PLANES)]
    ppermute x36, waiting for transfers between devices: 82.5 us -> 89.5 us  [come_from(): return lax.ppermute(v, BOTH, pairs)]
  transfers between devices with their start and end apart: 51 -> 51, of which waited for: 21 -> 25; matrix products, arithmetic and copies ran while one was open for 10% -> 11% of each run, Pallas kernels for 22% -> 20%
where the time goes in v3:
time: 578 us; the launch traced here: 570 us
  waiting for transfers between devices  204 us (35%)
  Pallas kernels  153 us (26%)
  starting transfers between devices  118 us (20%)
  other arithmetic  40.8 us (7%)
  local copies, waits for them, and re-layouts  31.5 us (5%)
  between operations  23.3 us (4%)
    all_to_all x6, waiting for transfers between devices, plane_exchange(): lax.all_to_all(v, 'shard', 0, 0, tiled=True, axis_index_groups=PLANES)  91 us
    ppermute x36, waiting for transfers between devices, come_from(): return lax.ppermute(v, BOTH, pairs)  89.5 us
    all_to_all x6, starting transfers between devices, plane_exchange(): lax.all_to_all(v, 'shard', 0, 0, tiled=True, axis_index_groups=PLANES)  43.8 us
    ppermute x36, starting transfers between devices, come_from(): return lax.ppermute(v, BOTH, pairs)  34 us
    pallas_call x4, Pallas kernels, weight_grad(): pl.pallas_call(weight_grad_kernel, grid=(grid,), in_specs=[rows, rows, *g...  31.9 us
    pallas_call x1, Pallas kernels, feed_forward(): pl.pallas_call(feed_forward_kernel, grid=(4,), in_specs=[side(D)] * 4 + [...  27 us
    all_to_all x3, starting transfers between devices, line_exchange(): return lax.all_to_all(v, 'shard', 0, 0, tiled=True, axis_index_groups=LINES)  23.2 us
    pallas_call x1, Pallas kernels, attend_back(): pl.pallas_call(backward_kernel, grid=(TOK // Q_BLOCK,), in_specs=[near_bl...  22.8 us
  transfers between devices with their start and end apart: 51, of which 25 were waited for; matrix products, arithmetic and copies ran while one was open for 11% of the time, Pallas kernels for 20%

profile of v3, /device:TPU:6, one launch (start us, length us, event | category | flops | bytes accessed | tf_op | source)
XLA Modules:
  0.0 570.1 jit_solution(1723639989918653346)
XLA Ops:
  17.9 6.7 %all-to-all-start = ((bf16[8,40,1792]{2,1,0:T(8,128)(2,1)}), bf16[8,40,1792]{2,1,0:T(8,128)(2,1)S(1)}, u32[]{:S(2)}, u32[]{:S(2)}) async-start(bf16[8,40,1792]{2,1,0:T(8,128)(2,1)} %copy.121), calls=%async_computation | async-start | bytes 2293760 | tf_op jit(solution)/shard_map/gate_weights_line/all_to_all | solution.py:138
  25.3 4.4 collective-permute-start.7
  29.8 8.2 %collective-permute-done = bf16[128,2048]{1,0:T(8,128)(2,1)} collective-permute-done((bf16[128,2048]{1,0:T(8,128)(2,1)S(1)}, bf16[128,2048]{1,0:T(8,128)(2,1)}, u32[]{:S(2)}, u32[]{:S(2)}) %collective-permute-start) | collective-permute-done | bytes 524320 | tf_op jit(solution)/shard_map/normed_line/ppermute | solution.py:68
  51.6 5.7 %all-to-all-start.1 = ((bf16[8,256,384]{2,1,0:T(8,128)(2,1)}), bf16[8,256,384]{2,1,0:T(8,128)(2,1)S(1)}, u32[]{:S(2)}, u32[]{:S(2)}) async-start(bf16[8,256,384]{2,1,0:T(8,128)(2,1)} %broadcast_in_dim.43), calls=%async_computation.1 | async-start | bytes 3145728 | tf_op jit(solution)/shard_map/qkv_weights_plane/all_to_all | solution.py:115
  70.4 9.8 %all-to-all-done.1 = bf16[8,256,384]{2,1,0:T(8,128)(2,1)S(1)} async-done(((bf16[8,256,384]{2,1,0:T(8,128)(2,1)}), bf16[8,256,384]{2,1,0:T(8,128)(2,1)S(1)}, u32[]{:S(2)}, u32[]{:S(2)}) %all-to-all-start.1) | async-done | bytes 1572896 | tf_op jit(solution)/shard_map/qkv_weights_plane/all_to_all | solution.py:115
  87.6 6.2 %all-to-all-start.2 = ((bf16[8,32,2048]{2,1,0:T(8,128)(2,1)}), bf16[8,32,2048]{2,1,0:T(8,128)(2,1)}, u32[]{:S(2)}, u32[]{:S(2)}) async-start(bf16[8,32,2048]{2,1,0:T(8,128)(2,1)} %broadcast_in_dim.45), calls=%async_computation.2 | async-start | bytes 2097152 | tf_op jit(solution)/shard_map/out_weights_plane/all_to_all | solution.py:115
  93.9 16.9 %attention_forward.1 = (bf16[1024,256]{1,0:T(8,128)(2,1)}, bf16[1024,256]{1,0:T(8,128)(2,1)}, bf16[1024,128]{1,0:T(8,128)(2,1)}, f32[1024,128]{1,0:T(8,128)}) custom-call(bf16[512,2048]{1,0:T(8,128)(2,1)} %pad_maximum_fusion.refs_0_.near_ref, bf16[512,2048]{1,0:T(8,128)(2,1)} %collective-permute-done.3.refs_1_.far_ref, bf16[2048,384]{1,0:T(8,128)(2,1)} %bitcast.69, ...), custom_call_target="tpu_custom_call" | custom-call | flops 30000001024 | bytes 1 | tf_op jit(solution)/shard_map/attention_forward/pallas_call | solution.py:408
  117.1 5.7 line_dot.2
  127.6 16.7 %all-to-all-start.3 = ((bf16[8,88,2048]{2,1,0:T(8,128)(2,1)}), bf16[8,88,2048]{2,1,0:T(8,128)(2,1)}, u32[]{:S(2)}, u32[]{:S(2)}) async-start(bf16[8,88,2048]{2,1,0:T(8,128)(2,1)} %broadcast_in_dim.46), calls=%async_computation.3 | async-start | bytes 5767168 | tf_op jit(solution)/shard_map/down_weights_plane/all_to_all | solution.py:115
  144.6 4.9 core_sum.4
  151.5 44.6 %all-to-all-done.3 = bf16[8,88,2048]{2,1,0:T(8,128)(2,1)} async-done(((bf16[8,88,2048]{2,1,0:T(8,128)(2,1)}), bf16[8,88,2048]{2,1,0:T(8,128)(2,1)}, u32[]{:S(2)}, u32[]{:S(2)}) %all-to-all-start.3) | async-done | bytes 2883616 | tf_op jit(solution)/shard_map/down_weights_plane/all_to_all | solution.py:115
  197.1 3.4 middle_kernel.1
  202.4 13.0 %collective-permute-done.16 = bf16[128,2048]{1,0:T(8,128)(2,1)S(1)} collective-permute-done((bf16[128,2048]{1,0:T(8,128)(2,1)}, bf16[128,2048]{1,0:T(8,128)(2,1)S(1)}, u32[]{:S(2)}, u32[]{:S(2)}) %collective-permute-start.16) | collective-permute-done | bytes 524320 | tf_op jit(solution)/shard_map/normed_two_line/ppermute | solution.py:68
  217.0 9.5 %collective-permute-done.14 = bf16[128,2048]{1,0:T(8,128)(2,1)S(1)} collective-permute-done((bf16[128,2048]{1,0:T(8,128)(2,1)}, bf16[128,2048]{1,0:T(8,128)(2,1)S(1)}, u32[]{:S(2)}, u32[]{:S(2)}) %collective-permute-start.14) | collective-permute-done | bytes 524320 | tf_op jit(solution)/shard_map/normed_two_line/ppermute | solution.py:68
  228.0 4.3 collective-permute-done.17.far_ref
  232.3 4.9 all-gather.2.cloned.1.call-done.gate_ref
  237.2 27.0 %feed_forward.1 = (bf16[512,704]{1,0:T(8,128)(2,1)}, bf16[512,704]{1,0:T(8,128)(2,1)}, bf16[512,1408]{1,0:T(8,128)(2,1)}, bf16[512,1408]{1,0:T(8,128)(2,1)}, bf1...) custom-call(bf16[512,2048]{1,0:T(8,128)(2,1)} %copy-done.13, ...), custom_call_target="tpu_custom_call" | custom-call | flops 30000001024 | bytes 1 | tf_op jit(solution)/shard_map/feed_forward/pallas_call | solution.py:551
  264.2 12.0 %weight_grad.4.refs_0_ = bf16[2048,1408]{1,0:T(8,128)(2,1)} custom-call(bf16[512,2048]{1,0:T(8,128)(2,1)} %copy-done.13, bf16[512,2048]{1,0:T(8,128)(2,1)} %collective-permute-done.17.far_ref, bf16[512,1408]{1,0:T(8,128)(2,1)} %get-tuple-element.76.g_near_ref, bf16[512,1408]{1,0:T(8,128)(2,1)} %get-tuple-element.77.g_far_ref), custom_call_target="tpu_custom_call" | custom-call | flops 15000000512 | bytes 1 | tf_op jit(solution)/shard_map/grad_gate_plane/weight_grad/pallas_call | solution.py:580
  276.8 5.9 %collective-permute-done.22.came_ref = bf16[512,2048]{1,0:T(8,128)(2,1)S(1)} collective-permute-done((bf16[512,2048]{1,0:T(8,128)(2,1)}, bf16[512,2048]{1,0:T(8,128)(2,1)S(1)}, u32[]{:S(2)}, u32[]{:S(2)}) %collective-permute-start.22) | collective-permute-done | bytes 2097184 | tf_op jit(solution)/shard_map/grad_normed_two_line/ppermute | solution.py:68
  284.1 4.9 core_sum.6
  291.9 4.9 core_sum.5
  296.7 7.0 %weight_grad.5.refs_6_ = bf16[704,2048]{1,0:T(8,128)(2,1)} custom-call(bf16[512,704]{1,0:T(8,128)(2,1)} %get-tuple-element.82.near_ref, bf16[512,704]{1,0:T(8,128)(2,1)} %get-tuple-element.83.far_ref, bf16[512,2048]{1,0:T(8,128)(2,1)} %pad_maximum_fusion.1.refs_2_.grads_near_ref.g_near_ref, ...), custom_call_target="tpu_custom_call" | custom-call | flops 1 | bytes 1 | tf_op jit(solution)/shard_map/grad_down_plane/weight_grad/pallas_call | solution.py:580
  306.1 10.1 %collective-permute-done.25.refs_3_ = bf16[128,2048]{1,0:T(8,128)(2,1)S(1)} collective-permute-done((bf16[128,2048]{1,0:T(8,128)(2,1)}, bf16[128,2048]{1,0:T(8,128)(2,1)S(1)}, u32[]{:S(2)}, u32[]{:S(2)}) %collective-permute-start.25) | collective-permute-done | bytes 524320 | tf_op jit(solution)/shard_map/grad_normed_two_line/ppermute | solution.py:68
  316.9 4.1 middle_back_kernel.1
  324.2 11.8 %collective-permute-done.28 = bf16[128,2048]{1,0:T(8,128)(2,1)S(1)} collective-permute-done((bf16[128,2048]{1,0:T(8,128)(2,1)}, bf16[128,2048]{1,0:T(8,128)(2,1)S(1)}, u32[]{:S(2)}, u32[]{:S(2)}) %collective-permute-start.28) | collective-permute-done | bytes 524320 | tf_op jit(solution)/shard_map/grad_attn_line/ppermute | solution.py:68
  338.7 9.2 %collective-permute-done.26 = bf16[128,2048]{1,0:T(8,128)(2,1)S(1)} collective-permute-done((bf16[128,2048]{1,0:T(8,128)(2,1)}, bf16[128,2048]{1,0:T(8,128)(2,1)S(1)}, u32[]{:S(2)}, u32[]{:S(2)}) %collective-permute-start.26) | collective-permute-done | bytes 524320 | tf_op jit(solution)/shard_map/grad_attn_line/ppermute | solution.py:68
  354.6 6.7 %all-to-all-start.4 = ((bf16[8,88,2048]{2,1,0:T(8,128)(2,1)}), bf16[8,88,2048]{2,1,0:T(8,128)(2,1)S(1)}, u32[]{:S(2)}, u32[]{:S(2)}) async-start(bf16[8,88,2048]{2,1,0:T(8,128)(2,1)} %bitcast.27), calls=%async_computation.4 | async-start | bytes 5767168 | tf_op jit(solution)/shard_map/grad_down_plane/all_to_all | solution.py:115
  361.3 22.8 %attention_backward.1.refs_5_.g_near_ref.g_far_ref.refs_0_ = bf16[1024,384]{1,0:T(8,128)(2,1)} custom-call(bf16[512,2048]{1,0:T(8,128)(2,1)} %pad_maximum_fusion.3.refs_0_.g_near_ref, bf16[512,2048]{1,0:T(8,128)(2,1)} %collective-permute-done.29.refs_1_.g_far_ref, bf16[256,2048]{1,0:T(8,128)(2,1)} %bitcast.22.refs_1_.refs_2_, ...), custom_call_target="tpu_custom_call" | custom-call | flops 30000001024 | bytes 1 | tf_op jit(solution)/shard_map/attention_backward/pallas_call | solution.py:447
  388.2 7.9 %weight_grad.6.refs_0_ = bf16[2048,384]{1,0:T(8,128)(2,1)} custom-call(bf16[512,2048]{1,0:T(8,128)(2,1)} %pad_maximum_fusion.refs_0_.near_ref, bf16[512,2048]{1,0:T(8,128)(2,1)} %collective-permute-done.3.refs_1_.far_ref, bf16[1024,384]{1,0:T(8,128)(2,1)} %attention_backward.1.refs_5_.g_near_ref.g_far_ref.refs_0_, ...), custom_call_target="tpu_custom_call" | custom-call | flops 5000000000 | bytes 1 | tf_op jit(solution)/shard_map/grad_qkv/weight_grad/pallas_call | solution.py:580
  396.2 5.0 weight_grad.7.refs_2_
  401.1 11.5 %all-to-all-done.4.refs_3_.parts_ref = bf16[8,88,2048]{2,1,0:T(8,128)(2,1)S(1)} async-done(((bf16[8,88,2048]{2,1,0:T(8,128)(2,1)}), bf16[8,88,2048]{2,1,0:T(8,128)(2,1)S(1)}, u32[]{:S(2)}, u32[]{:S(2)}) %all-to-all-start.4) | async-done | bytes 2883616 | tf_op jit(solution)/shard_map/grad_down_plane/all_to_all | solution.py:115
  414.2 6.6 %line_dot.3 = (bf16[512,2048]{1,0:T(8,128)(2,1)}, bf16[512,2048]{1,0:T(8,128)(2,1)}) custom-call(bf16[1024,384]{1,0:T(8,128)(2,1)} %attention_backward.1.refs_5_.g_near_ref.g_far_ref.refs_0_, bf16[2048,384]{1,0:T(8,128)(2,1)} %bitcast.70, bf16[256,2048]{1,0:T(8,128)(2,1)} %weight_grad.7.refs_2_, bf16[8,88,2048]{2,1,0:T(8,128)(2,1)} %copy-done), custom_call_target="tpu_custom_call" | custom-call | flops 1 | bytes 1 | tf_op jit(solution)/shard_map/grad_normed_line/line_dot/pallas_call | solution.py:495
  420.8 3.6 all-to-all-start.5
  425.3 4.9 core_sum.7
  434.6 15.1 %all-to-all-done.5.parts_ref = bf16[8,256,384]{2,1,0:T(8,128)(2,1)S(1)} async-done(((bf16[8,256,384]{2,1,0:T(8,128)(2,1)}), bf16[8,256,384]{2,1,0:T(8,128)(2,1)S(1)}, u32[]{:S(2)}, u32[]{:S(2)}) %all-to-all-start.5) | async-done | bytes 1572896 | tf_op jit(solution)/shard_map/grad_qkv/all_to_all | solution.py:115
  449.7 6.4 %collective-permute-done.31.refs_1_.refs_0_ = bf16[128,2048]{1,0:T(8,128)(2,1)S(1)} collective-permute-done((bf16[128,2048]{1,0:T(8,128)(2,1)}, bf16[128,2048]{1,0:T(8,128)(2,1)S(1)}, u32[]{:S(2)}, u32[]{:S(2)}) %collective-permute-start.31) | collective-permute-done | bytes 524320 | tf_op jit(solution)/shard_map/grad_normed_line/ppermute | solution.py:68
  467.1 3.9 tokens_back_kernel.1
  476.8 6.9 %all-to-all-start.6 = ((bf16[8,32,384]{2,1,0:T(8,128)(2,1)}), bf16[8,32,384]{2,1,0:T(8,128)(2,1)S(1)}, u32[]{:S(2)}, u32[]{:S(2)}) async-start(bf16[8,32,384]{2,1,0:T(8,128)(2,1)} %bitcast.29), calls=%async_computation.6 | async-start | bytes 393216 | tf_op jit(solution)/shard_map/grad_qkv/all_to_all | solution.py:138
  485.5 4.2 collective-permute-start.39
  489.7 3.5 collective-permute-done.35
  494.3 9.6 %all-to-all-start.7 = ((bf16[8,32,1408]{2,1,0:T(8,128)(2,1)}), bf16[8,32,1408]{2,1,0:T(8,128)(2,1)S(1)}, u32[]{:S(2)}, u32[]{:S(2)}) async-start(bf16[8,32,1408]{2,1,0:T(8,128)(2,1)} %bitcast.33), calls=%async_computation.8 | async-start | bytes 1441792 | tf_op jit(solution)/shard_map/grad_gate_line/all_to_all | solution.py:138
  505.9 8.3 %all-to-all-done.7 = bf16[8,32,1408]{2,1,0:T(8,128)(2,1)S(1)} async-done(((bf16[8,32,1408]{2,1,0:T(8,128)(2,1)}), bf16[8,32,1408]{2,1,0:T(8,128)(2,1)S(1)}, u32[]{:S(2)}, u32[]{:S(2)}) %all-to-all-start.7) | async-done | bytes 720928 | tf_op jit(solution)/shard_map/grad_gate_line/all_to_all | solution.py:138
  517.2 4.9 all-to-all-start.8
  528.1 9.1 %all-to-all-done.8.parts_ref = bf16[8,32,2048]{2,1,0:T(8,128)(2,1)} async-done(((bf16[8,32,2048]{2,1,0:T(8,128)(2,1)}), bf16[8,32,2048]{2,1,0:T(8,128)(2,1)}, u32[]{:S(2)}, u32[]{:S(2)}) %all-to-all-start.8) | async-done | bytes 1048608 | tf_op jit(solution)/shard_map/grad_out_rep/all_to_all | solution.py:115
  539.4 3.4 collective-permute-start.36
  542.8 5.3 multiply_subtract_fusion
  548.1 4.5 collective-permute-start.37
  553.2 8.5 %collective-permute-done.37 = bf16[32,2048]{1,0:T(8,128)(2,1)S(1)} collective-permute-done((bf16[32,2048]{1,0:T(8,128)(2,1)S(1)}, bf16[32,2048]{1,0:T(8,128)(2,1)S(1)}, u32[]{:S(2)}, u32[]{:S(2)}) %collective-permute-start.37) | collective-permute-done | bytes 131104 | tf_op jit(solution)/shard_map/grad_out_rep/ppermute | solution.py:73
  (255 shorter events, 122.4 us)
Async XLA Ops:
  9.8 20.0 %collective-permute-start.2 = (bf16[128,2048]{1,0:T(8,128)(2,1)S(1)}, bf16[128,2048]{1,0:T(8,128)(2,1)}, u32[]{:S(2)}, u32[]{:S(2)}) collective-permute-start(bf16[128,2048]{1,0:T(8,128)(2,1)S(1)} %fusion.4), channel_id=1, source_target_pairs={{6,0},{7,1},{0,2},{1,3},{2,4},{3,5},{4,6},{5,7},{14,8},{15,9},{8,1... | collective-permute-start | bytes 1572872 | tf_op jit(solution)/shard_map/normed_line/ppermute | solution.py:68
  10.2 19.6 %collective-permute-start.1 = (bf16[128,2048]{1,0:T(8,128)(2,1)S(1)}, bf16[128,2048]{1,0:T(8,128)(2,1)}, u32[]{:S(2)}, u32[]{:S(2)}) collective-permute-start(bf16[128,2048]{1,0:T(8,128)(2,1)S(1)} %fusion.4), channel_id=1, source_target_pairs={{4,0},{5,1},{6,2},{7,3},{0,4},{1,5},{2,6},{3,7},{12,8},{13,9},{14,... | collective-permute-start | bytes 1572872 | tf_op jit(solution)/shard_map/normed_line/ppermute | solution.py:68
  12.7 25.3 %collective-permute-start = (bf16[128,2048]{1,0:T(8,128)(2,1)S(1)}, bf16[128,2048]{1,0:T(8,128)(2,1)}, u32[]{:S(2)}, u32[]{:S(2)}) collective-permute-start(bf16[128,2048]{1,0:T(8,128)(2,1)S(1)} %fusion.4), channel_id=1, source_target_pairs={{2,0},{3,1},{4,2},{5,3},{6,4},{7,5},{0,6},{1,7},{10,8},{11,9},{12,... | collective-permute-start | bytes 1572872 | tf_op jit(solution)/shard_map/normed_line/ppermute | solution.py:68
  17.9 32.4 %all-to-all-start = ((bf16[8,40,1792]{2,1,0:T(8,128)(2,1)}), bf16[8,40,1792]{2,1,0:T(8,128)(2,1)S(1)}, u32[]{:S(2)}, u32[]{:S(2)}) async-start(bf16[8,40,1792]{2,1,0:T(8,128)(2,1)} %copy.121), calls=%async_computation | async-start | bytes 2293760 | tf_op jit(solution)/shard_map/gate_weights_line/all_to_all | solution.py:138
  25.3 57.0 %collective-permute-start.7 = (bf16[32,2048]{1,0:T(8,128)(2,1)}, bf16[32,2048]{1,0:T(8,128)(2,1)}, u32[]{:S(2)}, u32[]{:S(2)}) collective-permute-start(bf16[32,2048]{1,0:T(8,128)(2,1)} %convert_element_type.113), channel_id=1, source_target_pairs={{0,0},{8,1},{16,2},{24,3},{32,4},{40,5},{48,6},{56,7},{1,8},{9,9},... | collective-permute-start | bytes 393224 | tf_op jit(solution)/shard_map/out_turn/ppermute | solution.py:73
  44.4 49.5 %collective-permute-start.6 = (bf16[128,2048]{1,0:T(8,128)(2,1)}, bf16[128,2048]{1,0:T(8,128)(2,1)}, u32[]{:S(2)}, u32[]{:S(2)}) collective-permute-start(bf16[128,2048]{1,0:T(8,128)(2,1)} %broadcast_select_fusion.3), channel_id=1, source_target_pairs={{6,0},{7,1},{0,2},{1,3},{2,4},{3,5},{4,6},{5,7},{14,8},{15,9},{8,1... | collective-permute-start | bytes 1572872 | tf_op jit(solution)/shard_map/cotangent_line/ppermute | solution.py:68
  45.0 48.8 %collective-permute-start.5 = (bf16[128,2048]{1,0:T(8,128)(2,1)}, bf16[128,2048]{1,0:T(8,128)(2,1)}, u32[]{:S(2)}, u32[]{:S(2)}) collective-permute-start(bf16[128,2048]{1,0:T(8,128)(2,1)} %broadcast_select_fusion.3), channel_id=1, source_target_pairs={{4,0},{5,1},{6,2},{7,3},{0,4},{1,5},{2,6},{3,7},{12,8},{13,9},{14,... | collective-permute-start | bytes 1572872 | tf_op jit(solution)/shard_map/cotangent_line/ppermute | solution.py:68
  47.3 46.6 %collective-permute-start.4 = (bf16[128,2048]{1,0:T(8,128)(2,1)}, bf16[128,2048]{1,0:T(8,128)(2,1)}, u32[]{:S(2)}, u32[]{:S(2)}) collective-permute-start(bf16[128,2048]{1,0:T(8,128)(2,1)} %broadcast_select_fusion.3), channel_id=1, source_target_pairs={{2,0},{3,1},{4,2},{5,3},{6,4},{7,5},{0,6},{1,7},{10,8},{11,9},{12,... | collective-permute-start | bytes 1572872 | tf_op jit(solution)/shard_map/cotangent_line/ppermute | solution.py:68
  48.4 45.5 %collective-permute-start.3 = (bf16[512,2048]{1,0:T(8,128)(2,1)}, bf16[512,2048]{1,0:T(8,128)(2,1)}, u32[]{:S(2)}, u32[]{:S(2)}) collective-permute-start(bf16[512,2048]{1,0:T(8,128)(2,1)} %pad_maximum_fusion.refs_0_.near_ref), channel_id=1, source_target_pairs={{1,0},{0,1},{3,2},{2,3},{5,4},{4,5},{7,6},{6,7},{9,8},{8,9},{11,10... | collective-permute-start | bytes 6291464 | tf_op jit(solution)/shard_map/normed_line/ppermute | solution.py:68
  51.6 28.6 %all-to-all-start.1 = ((bf16[8,256,384]{2,1,0:T(8,128)(2,1)}), bf16[8,256,384]{2,1,0:T(8,128)(2,1)S(1)}, u32[]{:S(2)}, u32[]{:S(2)}) async-start(bf16[8,256,384]{2,1,0:T(8,128)(2,1)} %broadcast_in_dim.43), calls=%async_computation.1 | async-start | bytes 3145728 | tf_op jit(solution)/shard_map/qkv_weights_plane/all_to_all | solution.py:115
  57.4 179.8 %all-gather.2.cloned.1.call-start = ((), (), s32[]{:S(2)}) async-start(), calls=%async_computation.10 | async-start | bytes 6488064 | tf_op jit(solution)/shard_map/gate_weights_plane/all_gather | solution.py:124
  82.3 43.2 %collective-permute-start.13 = (bf16[88,2048]{1,0:T(8,128)(2,1)S(1)}, bf16[88,2048]{1,0:T(8,128)(2,1)S(1)}, u32[]{:S(2)}, u32[]{:S(2)}) collective-permute-start(bf16[88,2048]{1,0:T(8,128)(2,1)S(1)} %copy-done.29), channel_id=1, source_target_pairs={{0,0},{8,1},{16,2},{24,3},{32,4},{40,5},{48,6},{56,7},{1,8},{9,9},... | collective-permute-start | bytes 1081352 | tf_op jit(solution)/shard_map/down_turn/ppermute | solution.py:73
  87.6 29.5 %all-to-all-start.2 = ((bf16[8,32,2048]{2,1,0:T(8,128)(2,1)}), bf16[8,32,2048]{2,1,0:T(8,128)(2,1)}, u32[]{:S(2)}, u32[]{:S(2)}) async-start(bf16[8,32,2048]{2,1,0:T(8,128)(2,1)} %broadcast_in_dim.45), calls=%async_computation.2 | async-start | bytes 2097152 | tf_op jit(solution)/shard_map/out_weights_plane/all_to_all | solution.py:115
  125.4 19.2 %collective-permute-start.8 = (bf16[512,2048]{1,0:T(8,128)(2,1)}, bf16[512,2048]{1,0:T(8,128)(2,1)}, u32[]{:S(2)}, u32[]{:S(2)}) collective-permute-start(bf16[512,2048]{1,0:T(8,128)(2,1)} %get-tuple-element.61), channel_id=1, source_target_pairs={{1,0},{0,1},{3,2},{2,3},{5,4},{4,5},{7,6},{6,7},{9,8},{8,9},{11,10... | collective-permute-start | bytes 6291464 | tf_op jit(solution)/shard_map/heads_out_line/ppermute | solution.py:68
  127.6 68.5 %all-to-all-start.3 = ((bf16[8,88,2048]{2,1,0:T(8,128)(2,1)}), bf16[8,88,2048]{2,1,0:T(8,128)(2,1)}, u32[]{:S(2)}, u32[]{:S(2)}) async-start(bf16[8,88,2048]{2,1,0:T(8,128)(2,1)} %broadcast_in_dim.46), calls=%async_computation.3 | async-start | bytes 5767168 | tf_op jit(solution)/shard_map/down_weights_plane/all_to_all | solution.py:115
  144.2 329.4 %reduce-scatter.2.cloned.1.call-start = ((), (), s32[]{:S(2)}) async-start(), calls=%async_computation.11 | async-start | bytes 6488064 | tf_op jit(solution)/shard_map/grad_gate_plane/reduce_scatter | solution.py:128
  144.3 7.2 %collective-permute-start.12 = (bf16[512,2048]{1,0:T(8,128)(2,1)S(1)}, bf16[512,2048]{1,0:T(8,128)(2,1)}, u32[]{:S(2)}, u32[]{:S(2)}) collective-permute-start(bf16[512,2048]{1,0:T(8,128)(2,1)S(1)} %copy-done.1), channel_id=1, source_target_pairs={{1,0},{0,1},{3,2},{2,3},{5,4},{4,5},{7,6},{6,7},{9,8},{8,9},{11,10... | collective-permute-start | bytes 6291464 | tf_op jit(solution)/shard_map/cotangent_line/ppermute | solution.py:68
  149.4 46.7 %collective-permute-start.9 = (bf16[128,2048]{1,0:T(8,128)(2,1)}, bf16[128,2048]{1,0:T(8,128)(2,1)S(1)}, u32[]{:S(2)}, u32[]{:S(2)}) collective-permute-start(bf16[128,2048]{1,0:T(8,128)(2,1)} %get-tuple-element.63), channel_id=1, source_target_pairs={{6,0},{7,1},{0,2},{1,3},{2,4},{3,5},{4,6},{5,7},{14,8},{15,9},{8,1... | collective-permute-start | bytes 1572872 | tf_op jit(solution)/shard_map/heads_out_line/ppermute | solution.py:68
  149.4 46.7 %collective-permute-start.10 = (bf16[128,2048]{1,0:T(8,128)(2,1)}, bf16[128,2048]{1,0:T(8,128)(2,1)S(1)}, u32[]{:S(2)}, u32[]{:S(2)}) collective-permute-start(bf16[128,2048]{1,0:T(8,128)(2,1)} %get-tuple-element.64), channel_id=1, source_target_pairs={{4,0},{5,1},{6,2},{7,3},{0,4},{1,5},{2,6},{3,7},{12,8},{13,9},{14,... | collective-permute-start | bytes 1572872 | tf_op jit(solution)/shard_map/heads_out_line/ppermute | solution.py:68
  149.4 46.7 %collective-permute-start.11 = (bf16[128,2048]{1,0:T(8,128)(2,1)}, bf16[128,2048]{1,0:T(8,128)(2,1)}, u32[]{:S(2)}, u32[]{:S(2)}) collective-permute-start(bf16[128,2048]{1,0:T(8,128)(2,1)} %get-tuple-element.65), channel_id=1, source_target_pairs={{2,0},{3,1},{4,2},{5,3},{6,4},{7,5},{0,6},{1,7},{10,8},{11,9},{12,... | collective-permute-start | bytes 1572872 | tf_op jit(solution)/shard_map/heads_out_line/ppermute | solution.py:68
  200.4 15.1 %collective-permute-start.16 = (bf16[128,2048]{1,0:T(8,128)(2,1)}, bf16[128,2048]{1,0:T(8,128)(2,1)S(1)}, u32[]{:S(2)}, u32[]{:S(2)}) collective-permute-start(bf16[128,2048]{1,0:T(8,128)(2,1)} %get-tuple-element.66), channel_id=1, source_target_pairs={{6,0},{7,1},{0,2},{1,3},{2,4},{3,5},{4,6},{5,7},{14,8},{15,9},{8,1... | collective-permute-start | bytes 1572872 | tf_op jit(solution)/shard_map/normed_two_line/ppermute | solution.py:68
  200.4 16.6 %collective-permute-start.15 = (bf16[128,2048]{1,0:T(8,128)(2,1)}, bf16[128,2048]{1,0:T(8,128)(2,1)S(1)}, u32[]{:S(2)}, u32[]{:S(2)}) collective-permute-start(bf16[128,2048]{1,0:T(8,128)(2,1)} %get-tuple-element.66), channel_id=1, source_target_pairs={{4,0},{5,1},{6,2},{7,3},{0,4},{1,5},{2,6},{3,7},{12,8},{13,9},{14,... | collective-permute-start | bytes 1572872 | tf_op jit(solution)/shard_map/normed_two_line/ppermute | solution.py:68
  200.4 26.1 %collective-permute-start.14 = (bf16[128,2048]{1,0:T(8,128)(2,1)}, bf16[128,2048]{1,0:T(8,128)(2,1)S(1)}, u32[]{:S(2)}, u32[]{:S(2)}) collective-permute-start(bf16[128,2048]{1,0:T(8,128)(2,1)} %get-tuple-element.66), channel_id=1, source_target_pairs={{2,0},{3,1},{4,2},{5,3},{6,4},{7,5},{0,6},{1,7},{10,8},{11,9},{12,... | collective-permute-start | bytes 1572872 | tf_op jit(solution)/shard_map/normed_two_line/ppermute | solution.py:68
  276.3 15.6 %collective-permute-start.18 = (bf16[512,2048]{1,0:T(8,128)(2,1)}, bf16[512,2048]{1,0:T(8,128)(2,1)}, u32[]{:S(2)}, u32[]{:S(2)}) collective-permute-start(bf16[512,2048]{1,0:T(8,128)(2,1)} %get-tuple-element.68), channel_id=1, source_target_pairs={{1,0},{0,1},{3,2},{2,3},{5,4},{4,5},{7,6},{6,7},{9,8},{8,9},{11,10... | collective-permute-start | bytes 6291464 | tf_op jit(solution)/shard_map/mixed_line/ppermute | solution.py:68
  288.9 15.0 %collective-permute-start.23 = (bf16[128,2048]{1,0:T(8,128)(2,1)}, bf16[128,2048]{1,0:T(8,128)(2,1)S(1)}, u32[]{:S(2)}, u32[]{:S(2)}) collective-permute-start(bf16[128,2048]{1,0:T(8,128)(2,1)} %get-tuple-element.79), channel_id=1, source_target_pairs={{6,0},{7,1},{0,2},{1,3},{2,4},{3,5},{4,6},{5,7},{14,8},{15,9},{8,1... | collective-permute-start | bytes 1572872 | tf_op jit(solution)/shard_map/grad_normed_two_line/ppermute | solution.py:68
  289.5 16.6 %collective-permute-start.24 = (bf16[128,2048]{1,0:T(8,128)(2,1)}, bf16[128,2048]{1,0:T(8,128)(2,1)S(1)}, u32[]{:S(2)}, u32[]{:S(2)}) collective-permute-start(bf16[128,2048]{1,0:T(8,128)(2,1)} %get-tuple-element.80), channel_id=1, source_target_pairs={{4,0},{5,1},{6,2},{7,3},{0,4},{1,5},{2,6},{3,7},{12,8},{13,9},{14,... | collective-permute-start | bytes 1572872 | tf_op jit(solution)/shard_map/grad_normed_two_line/ppermute | solution.py:68
  291.9 24.3 %collective-permute-start.25 = (bf16[128,2048]{1,0:T(8,128)(2,1)}, bf16[128,2048]{1,0:T(8,128)(2,1)S(1)}, u32[]{:S(2)}, u32[]{:S(2)}) collective-permute-start(bf16[128,2048]{1,0:T(8,128)(2,1)} %get-tuple-element.81), channel_id=1, source_target_pairs={{2,0},{3,1},{4,2},{5,3},{6,4},{7,5},{0,6},{1,7},{10,8},{11,9},{12,... | collective-permute-start | bytes 1572872 | tf_op jit(solution)/shard_map/grad_normed_two_line/ppermute | solution.py:68
  321.0 15.0 %collective-permute-start.28 = (bf16[128,2048]{1,0:T(8,128)(2,1)}, bf16[128,2048]{1,0:T(8,128)(2,1)S(1)}, u32[]{:S(2)}, u32[]{:S(2)}) collective-permute-start(bf16[128,2048]{1,0:T(8,128)(2,1)} %get-tuple-element.84), channel_id=1, source_target_pairs={{6,0},{7,1},{0,2},{1,3},{2,4},{3,5},{4,6},{5,7},{14,8},{15,9},{8,1... | collective-permute-start | bytes 1572872 | tf_op jit(solution)/shard_map/grad_attn_line/ppermute | solution.py:68
  322.1 16.6 %collective-permute-start.27 = (bf16[128,2048]{1,0:T(8,128)(2,1)}, bf16[128,2048]{1,0:T(8,128)(2,1)S(1)}, u32[]{:S(2)}, u32[]{:S(2)}) collective-permute-start(bf16[128,2048]{1,0:T(8,128)(2,1)} %get-tuple-element.84), channel_id=1, source_target_pairs={{4,0},{5,1},{6,2},{7,3},{0,4},{1,5},{2,6},{3,7},{12,8},{13,9},{14,... | collective-permute-start | bytes 1572872 | tf_op jit(solution)/shard_map/grad_attn_line/ppermute | solution.py:68
  324.0 23.9 %collective-permute-start.26 = (bf16[128,2048]{1,0:T(8,128)(2,1)}, bf16[128,2048]{1,0:T(8,128)(2,1)S(1)}, u32[]{:S(2)}, u32[]{:S(2)}) collective-permute-start(bf16[128,2048]{1,0:T(8,128)(2,1)} %get-tuple-element.84), channel_id=1, source_target_pairs={{2,0},{3,1},{4,2},{5,3},{6,4},{7,5},{0,6},{1,7},{10,8},{11,9},{12,... | collective-permute-start | bytes 1572872 | tf_op jit(solution)/shard_map/grad_attn_line/ppermute | solution.py:68
  350.6 10.8 %collective-permute-start.29 = (bf16[512,2048]{1,0:T(8,128)(2,1)}, bf16[512,2048]{1,0:T(8,128)(2,1)}, u32[]{:S(2)}, u32[]{:S(2)}) collective-permute-start(bf16[512,2048]{1,0:T(8,128)(2,1)} %pad_maximum_fusion.3.refs_0_.g_near_ref), channel_id=1, source_target_pairs={{1,0},{0,1},{3,2},{2,3},{5,4},{4,5},{7,6},{6,7},{9,8},{8,9},{11,10... | collective-permute-start | bytes 6291464 | tf_op jit(solution)/shard_map/grad_attn_line/ppermute | solution.py:68
  351.4 32.8 %collective-permute-start.19 = (bf16[128,2048]{1,0:T(8,128)(2,1)}, bf16[128,2048]{1,0:T(8,128)(2,1)S(1)}, u32[]{:S(2)}, u32[]{:S(2)}) collective-permute-start(bf16[128,2048]{1,0:T(8,128)(2,1)} %get-tuple-element.70), channel_id=1, source_target_pairs={{6,0},{7,1},{0,2},{1,3},{2,4},{3,5},{4,6},{5,7},{14,8},{15,9},{8,1... | collective-permute-start | bytes 1572872 | tf_op jit(solution)/shard_map/mixed_line/ppermute | solution.py:68
  352.4 31.7 %collective-permute-start.20 = (bf16[128,2048]{1,0:T(8,128)(2,1)}, bf16[128,2048]{1,0:T(8,128)(2,1)}, u32[]{:S(2)}, u32[]{:S(2)}) collective-permute-start(bf16[128,2048]{1,0:T(8,128)(2,1)} %get-tuple-element.71), channel_id=1, source_target_pairs={{4,0},{5,1},{6,2},{7,3},{0,4},{1,5},{2,6},{3,7},{12,8},{13,9},{14,... | collective-permute-start | bytes 1572872 | tf_op jit(solution)/shard_map/mixed_line/ppermute | solution.py:68
  353.7 30.5 %collective-permute-start.21 = (bf16[128,2048]{1,0:T(8,128)(2,1)}, bf16[128,2048]{1,0:T(8,128)(2,1)}, u32[]{:S(2)}, u32[]{:S(2)}) collective-permute-start(bf16[128,2048]{1,0:T(8,128)(2,1)} %get-tuple-element.72), channel_id=1, source_target_pairs={{2,0},{3,1},{4,2},{5,3},{6,4},{7,5},{0,6},{1,7},{10,8},{11,9},{12,... | collective-permute-start | bytes 1572872 | tf_op jit(solution)/shard_map/mixed_line/ppermute | solution.py:68
  354.6 58.0 %all-to-all-start.4 = ((bf16[8,88,2048]{2,1,0:T(8,128)(2,1)}), bf16[8,88,2048]{2,1,0:T(8,128)(2,1)S(1)}, u32[]{:S(2)}, u32[]{:S(2)}) async-start(bf16[8,88,2048]{2,1,0:T(8,128)(2,1)} %bitcast.27), calls=%async_computation.4 | async-start | bytes 5767168 | tf_op jit(solution)/shard_map/grad_down_plane/all_to_all | solution.py:115
  420.8 28.9 %all-to-all-start.5 = ((bf16[8,256,384]{2,1,0:T(8,128)(2,1)}), bf16[8,256,384]{2,1,0:T(8,128)(2,1)S(1)}, u32[]{:S(2)}, u32[]{:S(2)}) async-start(bf16[8,256,384]{2,1,0:T(8,128)(2,1)} %bitcast.67), calls=%async_computation.5 | async-start | bytes 3145728 | tf_op jit(solution)/shard_map/grad_qkv/all_to_all | solution.py:115
  430.2 25.9 %collective-permute-start.31 = (bf16[128,2048]{1,0:T(8,128)(2,1)}, bf16[128,2048]{1,0:T(8,128)(2,1)S(1)}, u32[]{:S(2)}, u32[]{:S(2)}) collective-permute-start(bf16[128,2048]{1,0:T(8,128)(2,1)} %get-tuple-element.91), channel_id=1, source_target_pairs={{6,0},{7,1},{0,2},{1,3},{2,4},{3,5},{4,6},{5,7},{14,8},{15,9},{8,1... | collective-permute-start | bytes 1572872 | tf_op jit(solution)/shard_map/grad_normed_line/ppermute | solution.py:68
  433.1 33.0 %collective-permute-start.32 = (bf16[128,2048]{1,0:T(8,128)(2,1)}, bf16[128,2048]{1,0:T(8,128)(2,1)S(1)}, u32[]{:S(2)}, u32[]{:S(2)}) collective-permute-start(bf16[128,2048]{1,0:T(8,128)(2,1)} %get-tuple-element.92), channel_id=1, source_target_pairs={{4,0},{5,1},{6,2},{7,3},{0,4},{1,5},{2,6},{3,7},{12,8},{13,9},{14,... | collective-permute-start | bytes 1572872 | tf_op jit(solution)/shard_map/grad_normed_line/ppermute | solution.py:68
  433.2 32.8 %collective-permute-start.33 = (bf16[128,2048]{1,0:T(8,128)(2,1)}, bf16[128,2048]{1,0:T(8,128)(2,1)S(1)}, u32[]{:S(2)}, u32[]{:S(2)}) collective-permute-start(bf16[128,2048]{1,0:T(8,128)(2,1)} %get-tuple-element.93), channel_id=1, source_target_pairs={{2,0},{3,1},{4,2},{5,3},{6,4},{7,5},{0,6},{1,7},{10,8},{11,9},{12,... | collective-permute-start | bytes 1572872 | tf_op jit(solution)/shard_map/grad_normed_line/ppermute | solution.py:68
  459.4 16.7 %collective-permute-start.34 = (bf16[256,384]{1,0:T(8,128)(2,1)}, bf16[256,384]{1,0:T(8,128)(2,1)S(1)}, u32[]{:S(2)}, u32[]{:S(2)}) collective-permute-start(bf16[256,384]{1,0:T(8,128)(2,1)} %get-tuple-element.96), channel_id=1, source_target_pairs={{64,0},{65,1},{66,2},{67,3},{68,4},{69,5},{70,6},{71,7},{72,8},{73... | collective-permute-start | bytes 589832 | tf_op jit(solution)/shard_map/grad_qkv/ppermute | solution.py:68
  463.6 20.0 %collective-permute-start.38 = (bf16[88,2048]{1,0:T(8,128)(2,1)}, bf16[88,2048]{1,0:T(8,128)(2,1)}, u32[]{:S(2)}, u32[]{:S(2)}) collective-permute-start(bf16[88,2048]{1,0:T(8,128)(2,1)} %get-tuple-element.100), channel_id=1, source_target_pairs={{64,0},{65,1},{66,2},{67,3},{68,4},{69,5},{70,6},{71,7},{72,8},{73... | collective-permute-start | bytes 1081352 | tf_op jit(solution)/shard_map/grad_down_rep/ppermute | solution.py:68
  474.9 18.3 %collective-permute-start.35 = (bf16[256,1408]{1,0:T(8,128)(2,1)S(1)}, bf16[256,1408]{1,0:T(8,128)(2,1)S(1)}, u32[]{:S(2)}, u32[]{:S(2)}) collective-permute-start(bf16[256,1408]{1,0:T(8,128)(2,1)S(1)} %broadcast_select_fusion.1), channel_id=1, source_target_pairs={{64,0},{65,1},{66,2},{67,3},{68,4},{69,5},{70,6},{71,7},{72,8},{73... | collective-permute-start | bytes 2162696 | tf_op jit(solution)/shard_map/grad_gate_rep/ppermute | solution.py:68
  476.8 12.9 %all-to-all-start.6 = ((bf16[8,32,384]{2,1,0:T(8,128)(2,1)}), bf16[8,32,384]{2,1,0:T(8,128)(2,1)S(1)}, u32[]{:S(2)}, u32[]{:S(2)}) async-start(bf16[8,32,384]{2,1,0:T(8,128)(2,1)} %bitcast.29), calls=%async_computation.6 | async-start | bytes 393216 | tf_op jit(solution)/shard_map/grad_qkv/all_to_all | solution.py:138
  485.5 36.6 %collective-permute-start.39 = (bf16[88,2048]{1,0:T(8,128)(2,1)}, bf16[88,2048]{1,0:T(8,128)(2,1)}, u32[]{:S(2)}, u32[]{:S(2)}) collective-permute-start(bf16[88,2048]{1,0:T(8,128)(2,1)} %fusion.8), channel_id=1, source_target_pairs={{0,0},{8,1},{16,2},{24,3},{32,4},{40,5},{48,6},{56,7},{1,8},{9,9},... | collective-permute-start | bytes 1081352 | tf_op jit(solution)/shard_map/grad_down_rep/ppermute | solution.py:73
  494.3 19.9 %all-to-all-start.7 = ((bf16[8,32,1408]{2,1,0:T(8,128)(2,1)}), bf16[8,32,1408]{2,1,0:T(8,128)(2,1)S(1)}, u32[]{:S(2)}, u32[]{:S(2)}) async-start(bf16[8,32,1408]{2,1,0:T(8,128)(2,1)} %bitcast.33), calls=%async_computation.8 | async-start | bytes 1441792 | tf_op jit(solution)/shard_map/grad_gate_line/all_to_all | solution.py:138
  517.2 20.1 %all-to-all-start.8 = ((bf16[8,32,2048]{2,1,0:T(8,128)(2,1)}), bf16[8,32,2048]{2,1,0:T(8,128)(2,1)}, u32[]{:S(2)}, u32[]{:S(2)}) async-start(bf16[8,32,2048]{2,1,0:T(8,128)(2,1)} %bitcast.35), calls=%async_computation.9 | async-start | bytes 2097152 | tf_op jit(solution)/shard_map/grad_out_rep/all_to_all | solution.py:115
  539.4 8.7 %collective-permute-start.36 = (bf16[32,2048]{1,0:T(8,128)(2,1)}, bf16[32,2048]{1,0:T(8,128)(2,1)S(1)}, u32[]{:S(2)}, u32[]{:S(2)}) collective-permute-start(bf16[32,2048]{1,0:T(8,128)(2,1)} %get-tuple-element.98), channel_id=1, source_target_pairs={{64,0},{65,1},{66,2},{67,3},{68,4},{69,5},{70,6},{71,7},{72,8},{73... | collective-permute-start | bytes 393224 | tf_op jit(solution)/shard_map/grad_out_rep/ppermute | solution.py:68
  548.1 13.7 %collective-permute-start.37 = (bf16[32,2048]{1,0:T(8,128)(2,1)S(1)}, bf16[32,2048]{1,0:T(8,128)(2,1)S(1)}, u32[]{:S(2)}, u32[]{:S(2)}) collective-permute-start(bf16[32,2048]{1,0:T(8,128)(2,1)S(1)} %add_convert_fusion.3), channel_id=1, source_target_pairs={{0,0},{8,1},{16,2},{24,3},{32,4},{40,5},{48,6},{56,7},{1,8},{9,9},... | collective-permute-start | bytes 393224 | tf_op jit(solution)/shard_map/grad_out_rep/ppermute | solution.py:73
  (47 other events, 432.0 us)
Sparse Core Ops, SparseCore 0:
  60.5 176.6 all-gather.1
  276.3 153.8 reduce-scatter.1

commit v4 on v3

--- a/solution.py
+++ b/solution.py
@@ -700,7 +700,6 @@
         own, pieces = line_scatter(dn_near, dn_far, grad_gate)
     with jax.named_scope("grad_down_plane"):
         grad_down = weight_grad(hid_near, hid_far, cot_near, cot_far, 0, 512, 1, own)
-        down_parts = plane_exchange(grad_down.reshape(8, 88, D))
     with jax.named_scope("mixed_line"):
         mixed_own, mixed_pieces = line_scatter(mix_near, mix_far)
     with jax.named_scope("grad_normed_two_line"):
@@ -710,6 +709,11 @@
     with jax.named_scope("grad_attn_line"):
         pieces = line_pieces(grad_attn)
         attn_near, attn_far = line_halves(grad_attn, pieces)
+    with jax.named_scope("grad_out_down_plane"):
+        grad_out = weight_grad(heads_out[:HALF], heads_out[HALF:], attn_near, attn_far, 0, 512, 1)
+        grad_out_down = jnp.concatenate([grad_out.reshape(8, 32, D), grad_down.reshape(8, 88, D)], axis=1)
+        od_parts = plane_exchange(grad_out_down)
+
     grad_proj = attend_back(
         attn_near, attn_far, out_full, queries, pair, totals, cosine, sine, column, row,
         mixed_own,
@@ -721,14 +725,13 @@
             near, far, grad_proj, grad_proj, 1, PROJ_HERE, 5e9, mixed
         )
         qkv_parts = plane_exchange(grad_qkv_local.reshape(8, 256, PROJ_HERE))
-    with jax.named_scope("grad_out_plane"):
-        grad_out = weight_grad(heads_out[:HALF], heads_out[HALF:], attn_near, attn_far, 0, 512, 1, grad_qkv_local)
     with jax.named_scope("grad_normed_line"):
-        own, pieces = line_scatter(*line_dot(grad_proj, qkv_full, True, grad_out, down_parts))
-    with jax.named_scope("grad_down_rep"):
-        down_owned, down_low = parts_sum(down_parts, 88, pieces[0])
-        down_sum = down_owned + come_from(down_low, zz=2).astype(F32)
-        grad_down = turned(after(down_sum.astype(BF), pieces[0])).astype(F32)
+        own, pieces = line_scatter(*line_dot(grad_proj, qkv_full, True, grad_qkv_local, od_parts))
+    with jax.named_scope("grad_out_down_rep"):
+        od_owned, od_low = parts_sum(od_parts, 120, pieces[0])
+        od_sum = od_owned + come_from(od_low, zz=2).astype(F32)
+        grad_out_down = turned(od_sum.astype(BF)).astype(F32)
+        grad_out, grad_down = grad_out_down[:32], grad_out_down[32:]
     with jax.named_scope("grad_gate_rep"):
         gate_low_sum = after(gate_owned, pieces[0])
         gate_from_rep = come_from(gate_low_sum, zz=2)
@@ -749,11 +752,6 @@
             ]
         )
         grad_gate = grad_gate.transpose(2, 0, 1, 3).reshape(32, 2 * FF)
-    with jax.named_scope("grad_out_rep"):
-        out_parts = plane_exchange(after(grad_out.reshape(8, 32, D), gate_line_parts))
-        out_owned, out_low = parts_sum(out_parts, 32)
-        out_sum = out_owned + come_from(out_low, zz=2).astype(F32)
-        grad_out = turned(out_sum.astype(BF)).astype(F32)
     with jax.named_scope("grad_qkv"):
         qkv_sum, qkv_low_sum = parts_sum(qkv_parts, 256, pieces[0])
         qkv_sum = qkv_sum + come_from(qkv_low_sum, zz=2).astype(F32)

time: 578 us -> 570 us (0.986)
  starting transfers between devices: 118 us -> 98.4 us
  waiting for transfers between devices: 204 us -> 211 us
    all_to_all x6 -> x5, waiting for transfers between devices: 91 us -> 101 us  [plane_exchange(): lax.all_to_all(v, 'shard', 0, 0, tiled=True, axis_index_groups=PLANES)]
    ppermute x4 -> x3, waiting for transfers between devices: 8.55 us -> 17.7 us  [turned(): return lax.ppermute(v, BOTH, pairs)]
    ppermute x36 -> x35, waiting for transfers between devices: 89.5 us -> 80.7 us  [come_from(): return lax.ppermute(v, BOTH, pairs)]
    all_to_all x3, starting transfers between devices: 23.2 us -> 16.4 us  [line_exchange(): return lax.all_to_all(v, 'shard', 0, 0, tiled=True, axis_index_groups=LINES)]
    ppermute x4 -> x3, starting transfers between devices: 16.4 us -> 11.1 us  [turned(): return lax.ppermute(v, BOTH, pairs)]
    ppermute x36 -> x35, starting transfers between devices: 34 us -> 29 us  [come_from(): return lax.ppermute(v, BOTH, pairs)]
    all_to_all x6 -> x5, starting transfers between devices: 43.8 us -> 41.9 us  [plane_exchange(): lax.all_to_all(v, 'shard', 0, 0, tiled=True, axis_index_groups=PLANES)]
  transfers between devices with their start and end apart: 51 -> 48, of which waited for: 25 -> 22; matrix products, arithmetic and copies ran while one was open for 11% -> 10% of each run, Pallas kernels for 20% -> 22%
where the time goes in v4:
time: 570 us; the launch traced here: 561 us
  waiting for transfers between devices  211 us (37%)
  Pallas kernels  152 us (27%)
  starting transfers between devices  98.4 us (17%)
  other arithmetic  44.4 us (8%)
  local copies, waits for them, and re-layouts  33.5 us (6%)
  between operations  22 us (4%)
    all_to_all x5, waiting for transfers between devices, plane_exchange(): lax.all_to_all(v, 'shard', 0, 0, tiled=True, axis_index_groups=PLANES)  101 us
    ppermute x35, waiting for transfers between devices, come_from(): return lax.ppermute(v, BOTH, pairs)  80.7 us
    all_to_all x5, starting transfers between devices, plane_exchange(): lax.all_to_all(v, 'shard', 0, 0, tiled=True, axis_index_groups=PLANES)  41.9 us
    pallas_call x4, Pallas kernels, weight_grad(): pl.pallas_call(weight_grad_kernel, grid=(grid,), in_specs=[rows, rows, *g...  32.1 us
    ppermute x35, starting transfers between devices, come_from(): return lax.ppermute(v, BOTH, pairs)  29 us
    pallas_call x1, Pallas kernels, feed_forward(): pl.pallas_call(feed_forward_kernel, grid=(4,), in_specs=[side(D)] * 4 + [...  27 us
    pallas_call x1, Pallas kernels, attend_back(): pl.pallas_call(backward_kernel, grid=(TOK // Q_BLOCK,), in_specs=[near_bl...  22.8 us
    pallas_call x4, Pallas kernels, line_scatter(): pl.pallas_call(core_sum_kernel, grid=(4,), in_specs=[pl.BlockSpec((ROWS,...  19.9 us
  transfers between devices with their start and end apart: 48, of which 22 were waited for; matrix products, arithmetic and copies ran while one was open for 10% of the time, Pallas kernels for 22%

profile of v4, /device:TPU:6, one launch (start us, length us, event | category | flops | bytes accessed | tf_op | source)
XLA Modules:
  0.0 561.4 jit_solution(2499868680160744525)
XLA Ops:
  17.9 6.7 %all-to-all-start = ((bf16[8,40,1792]{2,1,0:T(8,128)(2,1)}), bf16[8,40,1792]{2,1,0:T(8,128)(2,1)S(1)}, u32[]{:S(2)}, u32[]{:S(2)}) async-start(bf16[8,40,1792]{2,1,0:T(8,128)(2,1)} %copy.121), calls=%async_computation | async-start | bytes 2293760 | tf_op jit(solution)/shard_map/gate_weights_line/all_to_all | solution.py:138
  25.3 4.4 collective-permute-start.7
  29.8 8.2 %collective-permute-done = bf16[128,2048]{1,0:T(8,128)(2,1)} collective-permute-done((bf16[128,2048]{1,0:T(8,128)(2,1)S(1)}, bf16[128,2048]{1,0:T(8,128)(2,1)}, u32[]{:S(2)}, u32[]{:S(2)}) %collective-permute-start) | collective-permute-done | bytes 524320 | tf_op jit(solution)/shard_map/normed_line/ppermute | solution.py:68
  51.6 5.7 %all-to-all-start.1 = ((bf16[8,256,384]{2,1,0:T(8,128)(2,1)}), bf16[8,256,384]{2,1,0:T(8,128)(2,1)S(1)}, u32[]{:S(2)}, u32[]{:S(2)}) async-start(bf16[8,256,384]{2,1,0:T(8,128)(2,1)} %broadcast_in_dim.40), calls=%async_computation.1 | async-start | bytes 3145728 | tf_op jit(solution)/shard_map/qkv_weights_plane/all_to_all | solution.py:115
  70.4 9.8 %all-to-all-done.1 = bf16[8,256,384]{2,1,0:T(8,128)(2,1)S(1)} async-done(((bf16[8,256,384]{2,1,0:T(8,128)(2,1)}), bf16[8,256,384]{2,1,0:T(8,128)(2,1)S(1)}, u32[]{:S(2)}, u32[]{:S(2)}) %all-to-all-start.1) | async-done | bytes 1572896 | tf_op jit(solution)/shard_map/qkv_weights_plane/all_to_all | solution.py:115
  82.2 3.3 collective-permute-start.13
  87.6 6.3 %all-to-all-start.2 = ((bf16[8,32,2048]{2,1,0:T(8,128)(2,1)}), bf16[8,32,2048]{2,1,0:T(8,128)(2,1)}, u32[]{:S(2)}, u32[]{:S(2)}) async-start(bf16[8,32,2048]{2,1,0:T(8,128)(2,1)} %broadcast_in_dim.42), calls=%async_computation.2 | async-start | bytes 2097152 | tf_op jit(solution)/shard_map/out_weights_plane/all_to_all | solution.py:115
  93.9 16.9 %attention_forward.1 = (bf16[1024,256]{1,0:T(8,128)(2,1)}, bf16[1024,256]{1,0:T(8,128)(2,1)}, bf16[1024,128]{1,0:T(8,128)(2,1)}, f32[1024,128]{1,0:T(8,128)}) custom-call(bf16[512,2048]{1,0:T(8,128)(2,1)} %pad_maximum_fusion.1.refs_0_.near_ref, bf16[512,2048]{1,0:T(8,128)(2,1)} %collective-permute-done.3.refs_1_.far_ref, bf16[2048,384]{1,0:T(8,128)(2,1)} %bitcast.68, ...), custom_call_target="tpu_custom_call" | custom-call | flops 30000001024 | bytes 1 | tf_op jit(solution)/shard_map/attention_forward/pallas_call | solution.py:408
  117.2 5.7 %line_dot.2 = (bf16[512,2048]{1,0:T(8,128)(2,1)}, bf16[512,2048]{1,0:T(8,128)(2,1)}) custom-call(bf16[1024,256]{1,0:T(8,128)(2,1)} %get-tuple-element.57.refs_0_, bf16[256,2048]{1,0:T(8,128)(2,1)} %bitcast.22.refs_1_.refs_2_, bf16[512,2048]{1,0:T(8,128)(2,1)} %pad_maximum_fusion.2.refs_2_.grads_near_ref.g_near_ref), custom_call_target="tpu_custom_call" | custom-call | flops 1 | bytes 1 | tf_op jit(solution)/shard_map/heads_out_line/line_dot/pallas_call | solution.py:495
  127.6 16.7 %all-to-all-start.3 = ((bf16[8,88,2048]{2,1,0:T(8,128)(2,1)}), bf16[8,88,2048]{2,1,0:T(8,128)(2,1)}, u32[]{:S(2)}, u32[]{:S(2)}) async-start(bf16[8,88,2048]{2,1,0:T(8,128)(2,1)} %broadcast_in_dim.43), calls=%async_computation.3 | async-start | bytes 5767168 | tf_op jit(solution)/shard_map/down_weights_plane/all_to_all | solution.py:115
  144.6 4.9 core_sum.4
  151.4 44.6 %all-to-all-done.3 = bf16[8,88,2048]{2,1,0:T(8,128)(2,1)} async-done(((bf16[8,88,2048]{2,1,0:T(8,128)(2,1)}), bf16[8,88,2048]{2,1,0:T(8,128)(2,1)}, u32[]{:S(2)}, u32[]{:S(2)}) %all-to-all-start.3) | async-done | bytes 2883616 | tf_op jit(solution)/shard_map/down_weights_plane/all_to_all | solution.py:115
  197.0 3.4 middle_kernel.1
  202.4 13.0 %collective-permute-done.16 = bf16[128,2048]{1,0:T(8,128)(2,1)S(1)} collective-permute-done((bf16[128,2048]{1,0:T(8,128)(2,1)}, bf16[128,2048]{1,0:T(8,128)(2,1)S(1)}, u32[]{:S(2)}, u32[]{:S(2)}) %collective-permute-start.16) | collective-permute-done | bytes 524320 | tf_op jit(solution)/shard_map/normed_two_line/ppermute | solution.py:68
  217.0 7.6 %collective-permute-done.14 = bf16[128,2048]{1,0:T(8,128)(2,1)S(1)} collective-permute-done((bf16[128,2048]{1,0:T(8,128)(2,1)}, bf16[128,2048]{1,0:T(8,128)(2,1)S(1)}, u32[]{:S(2)}, u32[]{:S(2)}) %collective-permute-start.14) | collective-permute-done | bytes 524320 | tf_op jit(solution)/shard_map/normed_two_line/ppermute | solution.py:68
  226.1 4.2 collective-permute-done.17.far_ref
  230.3 6.9 %all-gather.2.cloned.1.call-done.gate_ref = bf16[2048,1408]{1,0:T(8,128)(2,1)} async-done(((bf16[256,1408]{1,0:T(8,128)(2,1)}), bf16[2048,1408]{1,0:T(8,128)(2,1)}) %all-gather.2.cloned.1.call-update) | async-done | bytes 5767184 | tf_op jit(solution)/shard_map/gate_weights_plane/all_gather | solution.py:124
  237.2 27.0 %feed_forward.1 = (bf16[512,704]{1,0:T(8,128)(2,1)}, bf16[512,704]{1,0:T(8,128)(2,1)}, bf16[512,1408]{1,0:T(8,128)(2,1)}, bf16[512,1408]{1,0:T(8,128)(2,1)}, bf1...) custom-call(bf16[512,2048]{1,0:T(8,128)(2,1)} %copy-done.13, ...), custom_call_target="tpu_custom_call" | custom-call | flops 30000001024 | bytes 1 | tf_op jit(solution)/shard_map/feed_forward/pallas_call | solution.py:551
  264.8 11.9 %weight_grad.4.refs_0_ = bf16[2048,1408]{1,0:T(8,128)(2,1)} custom-call(bf16[512,2048]{1,0:T(8,128)(2,1)} %copy-done.13, bf16[512,2048]{1,0:T(8,128)(2,1)} %collective-permute-done.17.far_ref, bf16[512,1408]{1,0:T(8,128)(2,1)} %get-tuple-element.74.g_near_ref, bf16[512,1408]{1,0:T(8,128)(2,1)} %get-tuple-element.75.g_far_ref), custom_call_target="tpu_custom_call" | custom-call | flops 15000000512 | bytes 1 | tf_op jit(solution)/shard_map/grad_gate_plane/weight_grad/pallas_call | solution.py:580
  278.1 4.9 core_sum.6
  285.9 5.3 core_sum.5
  291.2 7.1 %weight_grad.5.refs_6_ = bf16[704,2048]{1,0:T(8,128)(2,1)} custom-call(bf16[512,704]{1,0:T(8,128)(2,1)} %get-tuple-element.80.near_ref, bf16[512,704]{1,0:T(8,128)(2,1)} %get-tuple-element.81.far_ref, bf16[512,2048]{1,0:T(8,128)(2,1)} %pad_maximum_fusion.2.refs_2_.grads_near_ref.g_near_ref, ...), custom_call_target="tpu_custom_call" | custom-call | flops 1 | bytes 1 | tf_op jit(solution)/shard_map/grad_down_plane/weight_grad/pallas_call | solution.py:580
  300.2 10.0 %collective-permute-done.25.refs_3_ = bf16[128,2048]{1,0:T(8,128)(2,1)S(1)} collective-permute-done((bf16[128,2048]{1,0:T(8,128)(2,1)}, bf16[128,2048]{1,0:T(8,128)(2,1)S(1)}, u32[]{:S(2)}, u32[]{:S(2)}) %collective-permute-start.25) | collective-permute-done | bytes 524320 | tf_op jit(solution)/shard_map/grad_normed_two_line/ppermute | solution.py:68
  311.0 4.1 middle_back_kernel.1
  318.3 11.8 %collective-permute-done.28 = bf16[128,2048]{1,0:T(8,128)(2,1)S(1)} collective-permute-done((bf16[128,2048]{1,0:T(8,128)(2,1)}, bf16[128,2048]{1,0:T(8,128)(2,1)S(1)}, u32[]{:S(2)}, u32[]{:S(2)}) %collective-permute-start.28) | collective-permute-done | bytes 524320 | tf_op jit(solution)/shard_map/grad_attn_line/ppermute | solution.py:68
  332.8 9.2 %collective-permute-done.26 = bf16[128,2048]{1,0:T(8,128)(2,1)S(1)} collective-permute-done((bf16[128,2048]{1,0:T(8,128)(2,1)}, bf16[128,2048]{1,0:T(8,128)(2,1)S(1)}, u32[]{:S(2)}, u32[]{:S(2)}) %collective-permute-start.26) | collective-permute-done | bytes 524320 | tf_op jit(solution)/shard_map/grad_attn_line/ppermute | solution.py:68
  344.4 3.2 collective-permute-done.29.refs_1_.g_far_ref
  348.9 5.2 weight_grad.7
  354.0 3.7 pad_maximum_fusion
  357.8 6.7 %all-to-all-start.4 = ((bf16[8,120,2048]{2,1,0:T(8,128)(2,1)}), bf16[8,120,2048]{2,1,0:T(8,128)(2,1)}, u32[]{:S(2)}, u32[]{:S(2)}) async-start(bf16[8,120,2048]{2,1,0:T(8,128)(2,1)} %pad_maximum_fusion), calls=%async_computation.4 | async-start | bytes 7864320 | tf_op jit(solution)/shard_map/grad_out_down_plane/all_to_all | solution.py:115
  367.9 22.8 %attention_backward.1.refs_5_.g_near_ref.g_far_ref.refs_0_ = bf16[1024,384]{1,0:T(8,128)(2,1)} custom-call(bf16[512,2048]{1,0:T(8,128)(2,1)} %copy-done.2, bf16[512,2048]{1,0:T(8,128)(2,1)} %copy-done.14, bf16[256,2048]{1,0:T(8,128)(2,1)} %bitcast.22.refs_1_.refs_2_, bf16[1024,256]{1,0:T(8,128)(2,1)} %get-tuple-element.83.refs_3_, ...), custom_call_target="tpu_custom_call" | custom-call | flops 30000001024 | bytes 1 | tf_op jit(solution)/shard_map/attention_backward/pallas_call | solution.py:447
  392.5 3.2 mixed_kernel.1.refs_0_
  395.7 7.9 %weight_grad.6.refs_2_ = bf16[2048,384]{1,0:T(8,128)(2,1)} custom-call(bf16[512,2048]{1,0:T(8,128)(2,1)} %pad_maximum_fusion.1.refs_0_.near_ref, bf16[512,2048]{1,0:T(8,128)(2,1)} %collective-permute-done.3.refs_1_.far_ref, bf16[1024,384]{1,0:T(8,128)(2,1)} %attention_backward.1.refs_5_.g_near_ref.g_far_ref.refs_0_, ...), custom_call_target="tpu_custom_call" | custom-call | flops 5000000000 | bytes 1 | tf_op jit(solution)/shard_map/grad_qkv/weight_grad/pallas_call | solution.py:580
  403.6 28.7 %all-to-all-done.4.refs_3_.parts_ref = bf16[8,120,2048]{2,1,0:T(8,128)(2,1)} async-done(((bf16[8,120,2048]{2,1,0:T(8,128)(2,1)}), bf16[8,120,2048]{2,1,0:T(8,128)(2,1)}, u32[]{:S(2)}, u32[]{:S(2)}) %all-to-all-start.4) | async-done | bytes 3932192 | tf_op jit(solution)/shard_map/grad_out_down_plane/all_to_all | solution.py:115
  432.3 6.6 %line_dot.3 = (bf16[512,2048]{1,0:T(8,128)(2,1)}, bf16[512,2048]{1,0:T(8,128)(2,1)}) custom-call(bf16[1024,384]{1,0:T(8,128)(2,1)} %attention_backward.1.refs_5_.g_near_ref.g_far_ref.refs_0_, bf16[2048,384]{1,0:T(8,128)(2,1)} %bitcast.69, bf16[2048,384]{1,0:T(8,128)(2,1)} %weight_grad.6.refs_2_, bf16[8,120,2048]{2,1,0:T(8,128)(2,1)} %all-to-all-done.4.refs_3_.parts_ref), custom_call_target="tpu_custom_call" | custom-call | flops 1 | bytes 1 | tf_op jit(solution)/shard_map/grad_normed_line/line_dot/pallas_call | solution.py:495
  439.0 6.5 %all-to-all-start.5 = ((bf16[8,256,384]{2,1,0:T(8,128)(2,1)}), bf16[8,256,384]{2,1,0:T(8,128)(2,1)S(1)}, u32[]{:S(2)}, u32[]{:S(2)}) async-start(bf16[8,256,384]{2,1,0:T(8,128)(2,1)} %bitcast.29), calls=%async_computation.5 | async-start | bytes 3145728 | tf_op jit(solution)/shard_map/grad_qkv/all_to_all | solution.py:115
  445.5 4.9 core_sum.7
  453.5 17.0 %all-to-all-done.5.parts_ref = bf16[8,256,384]{2,1,0:T(8,128)(2,1)S(1)} async-done(((bf16[8,256,384]{2,1,0:T(8,128)(2,1)}), bf16[8,256,384]{2,1,0:T(8,128)(2,1)S(1)}, u32[]{:S(2)}, u32[]{:S(2)}) %all-to-all-start.5) | async-done | bytes 1572896 | tf_op jit(solution)/shard_map/grad_qkv/all_to_all | solution.py:115
  474.8 3.7 parts_sum.3
  478.5 3.5 collective-permute-start.35
  483.0 3.9 tokens_back_kernel.1
  490.2 4.8 all-to-all-start.6
  496.6 3.2 all-to-all-done.6
  506.5 3.3 collective-permute-start.36
  509.8 6.4 %collective-permute-done.37 = bf16[256,1408]{1,0:T(8,128)(2,1)S(1)} collective-permute-done((bf16[256,1408]{1,0:T(8,128)(2,1)S(1)}, bf16[256,1408]{1,0:T(8,128)(2,1)S(1)}, u32[]{:S(2)}, u32[]{:S(2)}) %collective-permute-start.37) | collective-permute-done | bytes 720928 | tf_op jit(solution)/shard_map/grad_gate_rep/ppermute | solution.py:68
  517.4 4.9 all-to-all-start.7
  522.3 17.7 %collective-permute-done.36 = bf16[120,2048]{1,0:T(8,128)(2,1)} collective-permute-done((bf16[120,2048]{1,0:T(8,128)(2,1)}, bf16[120,2048]{1,0:T(8,128)(2,1)}, u32[]{:S(2)}, u32[]{:S(2)}) %collective-permute-start.36) | collective-permute-done | bytes 491552 | tf_op jit(solution)/shard_map/grad_out_down_rep/ppermute | solution.py:73
  548.2 5.3 multiply_subtract_fusion
  (249 shorter events, 106.8 us)
Async XLA Ops:
  9.8 20.0 %collective-permute-start.2 = (bf16[128,2048]{1,0:T(8,128)(2,1)S(1)}, bf16[128,2048]{1,0:T(8,128)(2,1)}, u32[]{:S(2)}, u32[]{:S(2)}) collective-permute-start(bf16[128,2048]{1,0:T(8,128)(2,1)S(1)} %fusion.4), channel_id=1, source_target_pairs={{6,0},{7,1},{0,2},{1,3},{2,4},{3,5},{4,6},{5,7},{14,8},{15,9},{8,1... | collective-permute-start | bytes 1572872 | tf_op jit(solution)/shard_map/normed_line/ppermute | solution.py:68
  10.2 19.6 %collective-permute-start.1 = (bf16[128,2048]{1,0:T(8,128)(2,1)S(1)}, bf16[128,2048]{1,0:T(8,128)(2,1)}, u32[]{:S(2)}, u32[]{:S(2)}) collective-permute-start(bf16[128,2048]{1,0:T(8,128)(2,1)S(1)} %fusion.4), channel_id=1, source_target_pairs={{4,0},{5,1},{6,2},{7,3},{0,4},{1,5},{2,6},{3,7},{12,8},{13,9},{14,... | collective-permute-start | bytes 1572872 | tf_op jit(solution)/shard_map/normed_line/ppermute | solution.py:68
  12.7 25.3 %collective-permute-start = (bf16[128,2048]{1,0:T(8,128)(2,1)S(1)}, bf16[128,2048]{1,0:T(8,128)(2,1)}, u32[]{:S(2)}, u32[]{:S(2)}) collective-permute-start(bf16[128,2048]{1,0:T(8,128)(2,1)S(1)} %fusion.4), channel_id=1, source_target_pairs={{2,0},{3,1},{4,2},{5,3},{6,4},{7,5},{0,6},{1,7},{10,8},{11,9},{12,... | collective-permute-start | bytes 1572872 | tf_op jit(solution)/shard_map/normed_line/ppermute | solution.py:68
  17.9 32.4 %all-to-all-start = ((bf16[8,40,1792]{2,1,0:T(8,128)(2,1)}), bf16[8,40,1792]{2,1,0:T(8,128)(2,1)S(1)}, u32[]{:S(2)}, u32[]{:S(2)}) async-start(bf16[8,40,1792]{2,1,0:T(8,128)(2,1)} %copy.121), calls=%async_computation | async-start | bytes 2293760 | tf_op jit(solution)/shard_map/gate_weights_line/all_to_all | solution.py:138
  25.3 56.9 %collective-permute-start.7 = (bf16[32,2048]{1,0:T(8,128)(2,1)}, bf16[32,2048]{1,0:T(8,128)(2,1)}, u32[]{:S(2)}, u32[]{:S(2)}) collective-permute-start(bf16[32,2048]{1,0:T(8,128)(2,1)} %convert_element_type.104), channel_id=1, source_target_pairs={{0,0},{8,1},{16,2},{24,3},{32,4},{40,5},{48,6},{56,7},{1,8},{9,9},... | collective-permute-start | bytes 393224 | tf_op jit(solution)/shard_map/out_turn/ppermute | solution.py:73
  44.3 49.6 %collective-permute-start.6 = (bf16[128,2048]{1,0:T(8,128)(2,1)}, bf16[128,2048]{1,0:T(8,128)(2,1)}, u32[]{:S(2)}, u32[]{:S(2)}) collective-permute-start(bf16[128,2048]{1,0:T(8,128)(2,1)} %broadcast_select_fusion.2), channel_id=1, source_target_pairs={{6,0},{7,1},{0,2},{1,3},{2,4},{3,5},{4,6},{5,7},{14,8},{15,9},{8,1... | collective-permute-start | bytes 1572872 | tf_op jit(solution)/shard_map/cotangent_line/ppermute | solution.py:68
  45.0 48.9 %collective-permute-start.5 = (bf16[128,2048]{1,0:T(8,128)(2,1)}, bf16[128,2048]{1,0:T(8,128)(2,1)}, u32[]{:S(2)}, u32[]{:S(2)}) collective-permute-start(bf16[128,2048]{1,0:T(8,128)(2,1)} %broadcast_select_fusion.2), channel_id=1, source_target_pairs={{4,0},{5,1},{6,2},{7,3},{0,4},{1,5},{2,6},{3,7},{12,8},{13,9},{14,... | collective-permute-start | bytes 1572872 | tf_op jit(solution)/shard_map/cotangent_line/ppermute | solution.py:68
  47.2 46.7 %collective-permute-start.4 = (bf16[128,2048]{1,0:T(8,128)(2,1)}, bf16[128,2048]{1,0:T(8,128)(2,1)}, u32[]{:S(2)}, u32[]{:S(2)}) collective-permute-start(bf16[128,2048]{1,0:T(8,128)(2,1)} %broadcast_select_fusion.2), channel_id=1, source_target_pairs={{2,0},{3,1},{4,2},{5,3},{6,4},{7,5},{0,6},{1,7},{10,8},{11,9},{12,... | collective-permute-start | bytes 1572872 | tf_op jit(solution)/shard_map/cotangent_line/ppermute | solution.py:68
  48.3 45.6 %collective-permute-start.3 = (bf16[512,2048]{1,0:T(8,128)(2,1)}, bf16[512,2048]{1,0:T(8,128)(2,1)}, u32[]{:S(2)}, u32[]{:S(2)}) collective-permute-start(bf16[512,2048]{1,0:T(8,128)(2,1)} %pad_maximum_fusion.1.refs_0_.near_ref), channel_id=1, source_target_pairs={{1,0},{0,1},{3,2},{2,3},{5,4},{4,5},{7,6},{6,7},{9,8},{8,9},{11,10... | collective-permute-start | bytes 6291464 | tf_op jit(solution)/shard_map/normed_line/ppermute | solution.py:68
  51.6 28.6 %all-to-all-start.1 = ((bf16[8,256,384]{2,1,0:T(8,128)(2,1)}), bf16[8,256,384]{2,1,0:T(8,128)(2,1)S(1)}, u32[]{:S(2)}, u32[]{:S(2)}) async-start(bf16[8,256,384]{2,1,0:T(8,128)(2,1)} %broadcast_in_dim.40), calls=%async_computation.1 | async-start | bytes 3145728 | tf_op jit(solution)/shard_map/qkv_weights_plane/all_to_all | solution.py:115
  57.4 179.8 %all-gather.2.cloned.1.call-start = ((), (), s32[]{:S(2)}) async-start(), calls=%async_computation.9 | async-start | bytes 6488064 | tf_op jit(solution)/shard_map/gate_weights_plane/all_gather | solution.py:124
  82.2 43.2 %collective-permute-start.13 = (bf16[88,2048]{1,0:T(8,128)(2,1)S(1)}, bf16[88,2048]{1,0:T(8,128)(2,1)S(1)}, u32[]{:S(2)}, u32[]{:S(2)}) collective-permute-start(bf16[88,2048]{1,0:T(8,128)(2,1)S(1)} %copy-done.32), channel_id=1, source_target_pairs={{0,0},{8,1},{16,2},{24,3},{32,4},{40,5},{48,6},{56,7},{1,8},{9,9},... | collective-permute-start | bytes 1081352 | tf_op jit(solution)/shard_map/down_turn/ppermute | solution.py:73
  87.6 29.6 %all-to-all-start.2 = ((bf16[8,32,2048]{2,1,0:T(8,128)(2,1)}), bf16[8,32,2048]{2,1,0:T(8,128)(2,1)}, u32[]{:S(2)}, u32[]{:S(2)}) async-start(bf16[8,32,2048]{2,1,0:T(8,128)(2,1)} %broadcast_in_dim.42), calls=%async_computation.2 | async-start | bytes 2097152 | tf_op jit(solution)/shard_map/out_weights_plane/all_to_all | solution.py:115
  125.4 19.2 %collective-permute-start.8 = (bf16[512,2048]{1,0:T(8,128)(2,1)}, bf16[512,2048]{1,0:T(8,128)(2,1)}, u32[]{:S(2)}, u32[]{:S(2)}) collective-permute-start(bf16[512,2048]{1,0:T(8,128)(2,1)} %get-tuple-element.59), channel_id=1, source_target_pairs={{1,0},{0,1},{3,2},{2,3},{5,4},{4,5},{7,6},{6,7},{9,8},{8,9},{11,10... | collective-permute-start | bytes 6291464 | tf_op jit(solution)/shard_map/heads_out_line/ppermute | solution.py:68
  127.6 68.5 %all-to-all-start.3 = ((bf16[8,88,2048]{2,1,0:T(8,128)(2,1)}), bf16[8,88,2048]{2,1,0:T(8,128)(2,1)}, u32[]{:S(2)}, u32[]{:S(2)}) async-start(bf16[8,88,2048]{2,1,0:T(8,128)(2,1)} %broadcast_in_dim.43), calls=%async_computation.3 | async-start | bytes 5767168 | tf_op jit(solution)/shard_map/down_weights_plane/all_to_all | solution.py:115
  144.2 350.8 %reduce-scatter.2.cloned.1.call-start = ((), (), s32[]{:S(2)}) async-start(), calls=%async_computation.10 | async-start | bytes 6488064 | tf_op jit(solution)/shard_map/grad_gate_plane/reduce_scatter | solution.py:128
  144.3 7.2 %collective-permute-start.12 = (bf16[512,2048]{1,0:T(8,128)(2,1)S(1)}, bf16[512,2048]{1,0:T(8,128)(2,1)}, u32[]{:S(2)}, u32[]{:S(2)}) collective-permute-start(bf16[512,2048]{1,0:T(8,128)(2,1)S(1)} %copy-done.1), channel_id=1, source_target_pairs={{1,0},{0,1},{3,2},{2,3},{5,4},{4,5},{7,6},{6,7},{9,8},{8,9},{11,10... | collective-permute-start | bytes 6291464 | tf_op jit(solution)/shard_map/cotangent_line/ppermute | solution.py:68
  149.4 46.7 %collective-permute-start.9 = (bf16[128,2048]{1,0:T(8,128)(2,1)}, bf16[128,2048]{1,0:T(8,128)(2,1)S(1)}, u32[]{:S(2)}, u32[]{:S(2)}) collective-permute-start(bf16[128,2048]{1,0:T(8,128)(2,1)} %get-tuple-element.61), channel_id=1, source_target_pairs={{6,0},{7,1},{0,2},{1,3},{2,4},{3,5},{4,6},{5,7},{14,8},{15,9},{8,1... | collective-permute-start | bytes 1572872 | tf_op jit(solution)/shard_map/heads_out_line/ppermute | solution.py:68
  149.4 46.7 %collective-permute-start.10 = (bf16[128,2048]{1,0:T(8,128)(2,1)}, bf16[128,2048]{1,0:T(8,128)(2,1)S(1)}, u32[]{:S(2)}, u32[]{:S(2)}) collective-permute-start(bf16[128,2048]{1,0:T(8,128)(2,1)} %get-tuple-element.62), channel_id=1, source_target_pairs={{4,0},{5,1},{6,2},{7,3},{0,4},{1,5},{2,6},{3,7},{12,8},{13,9},{14,... | collective-permute-start | bytes 1572872 | tf_op jit(solution)/shard_map/heads_out_line/ppermute | solution.py:68
  149.4 46.7 %collective-permute-start.11 = (bf16[128,2048]{1,0:T(8,128)(2,1)}, bf16[128,2048]{1,0:T(8,128)(2,1)}, u32[]{:S(2)}, u32[]{:S(2)}) collective-permute-start(bf16[128,2048]{1,0:T(8,128)(2,1)} %get-tuple-element.63), channel_id=1, source_target_pairs={{2,0},{3,1},{4,2},{5,3},{6,4},{7,5},{0,6},{1,7},{10,8},{11,9},{12,... | collective-permute-start | bytes 1572872 | tf_op jit(solution)/shard_map/heads_out_line/ppermute | solution.py:68
  200.4 15.1 %collective-permute-start.16 = (bf16[128,2048]{1,0:T(8,128)(2,1)}, bf16[128,2048]{1,0:T(8,128)(2,1)S(1)}, u32[]{:S(2)}, u32[]{:S(2)}) collective-permute-start(bf16[128,2048]{1,0:T(8,128)(2,1)} %get-tuple-element.64), channel_id=1, source_target_pairs={{6,0},{7,1},{0,2},{1,3},{2,4},{3,5},{4,6},{5,7},{14,8},{15,9},{8,1... | collective-permute-start | bytes 1572872 | tf_op jit(solution)/shard_map/normed_two_line/ppermute | solution.py:68
  200.4 16.6 %collective-permute-start.15 = (bf16[128,2048]{1,0:T(8,128)(2,1)}, bf16[128,2048]{1,0:T(8,128)(2,1)S(1)}, u32[]{:S(2)}, u32[]{:S(2)}) collective-permute-start(bf16[128,2048]{1,0:T(8,128)(2,1)} %get-tuple-element.64), channel_id=1, source_target_pairs={{4,0},{5,1},{6,2},{7,3},{0,4},{1,5},{2,6},{3,7},{12,8},{13,9},{14,... | collective-permute-start | bytes 1572872 | tf_op jit(solution)/shard_map/normed_two_line/ppermute | solution.py:68
  200.4 24.2 %collective-permute-start.14 = (bf16[128,2048]{1,0:T(8,128)(2,1)}, bf16[128,2048]{1,0:T(8,128)(2,1)S(1)}, u32[]{:S(2)}, u32[]{:S(2)}) collective-permute-start(bf16[128,2048]{1,0:T(8,128)(2,1)} %get-tuple-element.64), channel_id=1, source_target_pairs={{2,0},{3,1},{4,2},{5,3},{6,4},{7,5},{0,6},{1,7},{10,8},{11,9},{12,... | collective-permute-start | bytes 1572872 | tf_op jit(solution)/shard_map/normed_two_line/ppermute | solution.py:68
  225.8 4.5 collective-permute-start.17
  264.2 21.7 %collective-permute-start.18 = (bf16[512,2048]{1,0:T(8,128)(2,1)}, bf16[512,2048]{1,0:T(8,128)(2,1)}, u32[]{:S(2)}, u32[]{:S(2)}) collective-permute-start(bf16[512,2048]{1,0:T(8,128)(2,1)} %get-tuple-element.66), channel_id=1, source_target_pairs={{1,0},{0,1},{3,2},{2,3},{5,4},{4,5},{7,6},{6,7},{9,8},{8,9},{11,10... | collective-permute-start | bytes 6291464 | tf_op jit(solution)/shard_map/mixed_line/ppermute | solution.py:68
  264.3 12.5 %collective-permute-start.22 = (bf16[512,2048]{1,0:T(8,128)(2,1)}, bf16[512,2048]{1,0:T(8,128)(2,1)S(1)}, u32[]{:S(2)}, u32[]{:S(2)}) collective-permute-start(bf16[512,2048]{1,0:T(8,128)(2,1)} %get-tuple-element.73), channel_id=1, source_target_pairs={{1,0},{0,1},{3,2},{2,3},{5,4},{4,5},{7,6},{6,7},{9,8},{8,9},{11,10... | collective-permute-start | bytes 6291464 | tf_op jit(solution)/shard_map/grad_normed_two_line/ppermute | solution.py:68
  283.0 15.3 %collective-permute-start.23 = (bf16[128,2048]{1,0:T(8,128)(2,1)}, bf16[128,2048]{1,0:T(8,128)(2,1)S(1)}, u32[]{:S(2)}, u32[]{:S(2)}) collective-permute-start(bf16[128,2048]{1,0:T(8,128)(2,1)} %get-tuple-element.77), channel_id=1, source_target_pairs={{6,0},{7,1},{0,2},{1,3},{2,4},{3,5},{4,6},{5,7},{14,8},{15,9},{8,1... | collective-permute-start | bytes 1572872 | tf_op jit(solution)/shard_map/grad_normed_two_line/ppermute | solution.py:68
  283.6 16.6 %collective-permute-start.24 = (bf16[128,2048]{1,0:T(8,128)(2,1)}, bf16[128,2048]{1,0:T(8,128)(2,1)S(1)}, u32[]{:S(2)}, u32[]{:S(2)}) collective-permute-start(bf16[128,2048]{1,0:T(8,128)(2,1)} %get-tuple-element.78), channel_id=1, source_target_pairs={{4,0},{5,1},{6,2},{7,3},{0,4},{1,5},{2,6},{3,7},{12,8},{13,9},{14,... | collective-permute-start | bytes 1572872 | tf_op jit(solution)/shard_map/grad_normed_two_line/ppermute | solution.py:68
  285.9 24.3 %collective-permute-start.25 = (bf16[128,2048]{1,0:T(8,128)(2,1)}, bf16[128,2048]{1,0:T(8,128)(2,1)S(1)}, u32[]{:S(2)}, u32[]{:S(2)}) collective-permute-start(bf16[128,2048]{1,0:T(8,128)(2,1)} %get-tuple-element.79), channel_id=1, source_target_pairs={{2,0},{3,1},{4,2},{5,3},{6,4},{7,5},{0,6},{1,7},{10,8},{11,9},{12,... | collective-permute-start | bytes 1572872 | tf_op jit(solution)/shard_map/grad_normed_two_line/ppermute | solution.py:68
  315.1 15.0 %collective-permute-start.28 = (bf16[128,2048]{1,0:T(8,128)(2,1)}, bf16[128,2048]{1,0:T(8,128)(2,1)S(1)}, u32[]{:S(2)}, u32[]{:S(2)}) collective-permute-start(bf16[128,2048]{1,0:T(8,128)(2,1)} %get-tuple-element.82), channel_id=1, source_target_pairs={{6,0},{7,1},{0,2},{1,3},{2,4},{3,5},{4,6},{5,7},{14,8},{15,9},{8,1... | collective-permute-start | bytes 1572872 | tf_op jit(solution)/shard_map/grad_attn_line/ppermute | solution.py:68
  316.2 16.6 %collective-permute-start.27 = (bf16[128,2048]{1,0:T(8,128)(2,1)}, bf16[128,2048]{1,0:T(8,128)(2,1)S(1)}, u32[]{:S(2)}, u32[]{:S(2)}) collective-permute-start(bf16[128,2048]{1,0:T(8,128)(2,1)} %get-tuple-element.82), channel_id=1, source_target_pairs={{4,0},{5,1},{6,2},{7,3},{0,4},{1,5},{2,6},{3,7},{12,8},{13,9},{14,... | collective-permute-start | bytes 1572872 | tf_op jit(solution)/shard_map/grad_attn_line/ppermute | solution.py:68
  318.0 24.0 %collective-permute-start.26 = (bf16[128,2048]{1,0:T(8,128)(2,1)}, bf16[128,2048]{1,0:T(8,128)(2,1)S(1)}, u32[]{:S(2)}, u32[]{:S(2)}) collective-permute-start(bf16[128,2048]{1,0:T(8,128)(2,1)} %get-tuple-element.82), channel_id=1, source_target_pairs={{2,0},{3,1},{4,2},{5,3},{6,4},{7,5},{0,6},{1,7},{10,8},{11,9},{12,... | collective-permute-start | bytes 1572872 | tf_op jit(solution)/shard_map/grad_attn_line/ppermute | solution.py:68
  343.3 4.2 collective-permute-start.29
  357.8 74.5 %all-to-all-start.4 = ((bf16[8,120,2048]{2,1,0:T(8,128)(2,1)}), bf16[8,120,2048]{2,1,0:T(8,128)(2,1)}, u32[]{:S(2)}, u32[]{:S(2)}) async-start(bf16[8,120,2048]{2,1,0:T(8,128)(2,1)} %pad_maximum_fusion), calls=%async_computation.4 | async-start | bytes 7864320 | tf_op jit(solution)/shard_map/grad_out_down_plane/all_to_all | solution.py:115
  364.5 26.2 %collective-permute-start.19 = (bf16[128,2048]{1,0:T(8,128)(2,1)S(1)}, bf16[128,2048]{1,0:T(8,128)(2,1)S(1)}, u32[]{:S(2)}, u32[]{:S(2)}) collective-permute-start(bf16[128,2048]{1,0:T(8,128)(2,1)S(1)} %copy-done.44), channel_id=1, source_target_pairs={{6,0},{7,1},{0,2},{1,3},{2,4},{3,5},{4,6},{5,7},{14,8},{15,9},{8,1... | collective-permute-start | bytes 1572872 | tf_op jit(solution)/shard_map/mixed_line/ppermute | solution.py:68
  365.5 25.2 %collective-permute-start.20 = (bf16[128,2048]{1,0:T(8,128)(2,1)S(1)}, bf16[128,2048]{1,0:T(8,128)(2,1)S(1)}, u32[]{:S(2)}, u32[]{:S(2)}) collective-permute-start(bf16[128,2048]{1,0:T(8,128)(2,1)S(1)} %copy-done.43), channel_id=1, source_target_pairs={{4,0},{5,1},{6,2},{7,3},{0,4},{1,5},{2,6},{3,7},{12,8},{13,9},{14,... | collective-permute-start | bytes 1572872 | tf_op jit(solution)/shard_map/mixed_line/ppermute | solution.py:68
  367.6 24.0 %collective-permute-start.21 = (bf16[128,2048]{1,0:T(8,128)(2,1)S(1)}, bf16[128,2048]{1,0:T(8,128)(2,1)S(1)}, u32[]{:S(2)}, u32[]{:S(2)}) collective-permute-start(bf16[128,2048]{1,0:T(8,128)(2,1)S(1)} %copy-done.42), channel_id=1, source_target_pairs={{2,0},{3,1},{4,2},{5,3},{6,4},{7,5},{0,6},{1,7},{10,8},{11,9},{12,... | collective-permute-start | bytes 1572872 | tf_op jit(solution)/shard_map/mixed_line/ppermute | solution.py:68
  439.0 6.6 %collective-permute-start.30 = (bf16[512,2048]{1,0:T(8,128)(2,1)}, bf16[512,2048]{1,0:T(8,128)(2,1)}, u32[]{:S(2)}, u32[]{:S(2)}) collective-permute-start(bf16[512,2048]{1,0:T(8,128)(2,1)} %get-tuple-element.87), channel_id=1, source_target_pairs={{1,0},{0,1},{3,2},{2,3},{5,4},{4,5},{7,6},{6,7},{9,8},{8,9},{11,10... | collective-permute-start | bytes 6291464 | tf_op jit(solution)/shard_map/grad_normed_line/ppermute | solution.py:68
  439.0 31.5 %all-to-all-start.5 = ((bf16[8,256,384]{2,1,0:T(8,128)(2,1)}), bf16[8,256,384]{2,1,0:T(8,128)(2,1)S(1)}, u32[]{:S(2)}, u32[]{:S(2)}) async-start(bf16[8,256,384]{2,1,0:T(8,128)(2,1)} %bitcast.29), calls=%async_computation.5 | async-start | bytes 3145728 | tf_op jit(solution)/shard_map/grad_qkv/all_to_all | solution.py:115
  450.4 20.1 %collective-permute-start.31 = (bf16[128,2048]{1,0:T(8,128)(2,1)}, bf16[128,2048]{1,0:T(8,128)(2,1)S(1)}, u32[]{:S(2)}, u32[]{:S(2)}) collective-permute-start(bf16[128,2048]{1,0:T(8,128)(2,1)} %get-tuple-element.89), channel_id=1, source_target_pairs={{6,0},{7,1},{0,2},{1,3},{2,4},{3,5},{4,6},{5,7},{14,8},{15,9},{8,1... | collective-permute-start | bytes 1572872 | tf_op jit(solution)/shard_map/grad_normed_line/ppermute | solution.py:68
  451.1 31.0 %collective-permute-start.32 = (bf16[128,2048]{1,0:T(8,128)(2,1)}, bf16[128,2048]{1,0:T(8,128)(2,1)S(1)}, u32[]{:S(2)}, u32[]{:S(2)}) collective-permute-start(bf16[128,2048]{1,0:T(8,128)(2,1)} %get-tuple-element.90), channel_id=1, source_target_pairs={{4,0},{5,1},{6,2},{7,3},{0,4},{1,5},{2,6},{3,7},{12,8},{13,9},{14,... | collective-permute-start | bytes 1572872 | tf_op jit(solution)/shard_map/grad_normed_line/ppermute | solution.py:68
  453.2 28.8 %collective-permute-start.33 = (bf16[128,2048]{1,0:T(8,128)(2,1)}, bf16[128,2048]{1,0:T(8,128)(2,1)S(1)}, u32[]{:S(2)}, u32[]{:S(2)}) collective-permute-start(bf16[128,2048]{1,0:T(8,128)(2,1)} %get-tuple-element.91), channel_id=1, source_target_pairs={{2,0},{3,1},{4,2},{5,3},{6,4},{7,5},{0,6},{1,7},{10,8},{11,9},{12,... | collective-permute-start | bytes 1572872 | tf_op jit(solution)/shard_map/grad_normed_line/ppermute | solution.py:68
  474.8 14.7 %collective-permute-start.34 = (bf16[256,384]{1,0:T(8,128)(2,1)}, bf16[256,384]{1,0:T(8,128)(2,1)S(1)}, u32[]{:S(2)}, u32[]{:S(2)}) collective-permute-start(bf16[256,384]{1,0:T(8,128)(2,1)} %get-tuple-element.94), channel_id=1, source_target_pairs={{64,0},{65,1},{66,2},{67,3},{68,4},{69,5},{70,6},{71,7},{72,8},{73... | collective-permute-start | bytes 589832 | tf_op jit(solution)/shard_map/grad_qkv/ppermute | solution.py:68
  478.5 26.0 %collective-permute-start.35 = (bf16[120,2048]{1,0:T(8,128)(2,1)}, bf16[120,2048]{1,0:T(8,128)(2,1)}, u32[]{:S(2)}, u32[]{:S(2)}) collective-permute-start(bf16[120,2048]{1,0:T(8,128)(2,1)} %get-tuple-element.96), channel_id=1, source_target_pairs={{64,0},{65,1},{66,2},{67,3},{68,4},{69,5},{70,6},{71,7},{72,8},{73... | collective-permute-start | bytes 1474568 | tf_op jit(solution)/shard_map/grad_out_down_rep/ppermute | solution.py:68
  490.2 9.5 %all-to-all-start.6 = ((bf16[8,32,384]{2,1,0:T(8,128)(2,1)}), bf16[8,32,384]{2,1,0:T(8,128)(2,1)S(1)}, u32[]{:S(2)}, u32[]{:S(2)}) async-start(bf16[8,32,384]{2,1,0:T(8,128)(2,1)} %bitcast.30), calls=%async_computation.6 | async-start | bytes 393216 | tf_op jit(solution)/shard_map/grad_qkv/all_to_all | solution.py:138
  496.2 20.1 %collective-permute-start.37 = (bf16[256,1408]{1,0:T(8,128)(2,1)S(1)}, bf16[256,1408]{1,0:T(8,128)(2,1)S(1)}, u32[]{:S(2)}, u32[]{:S(2)}) collective-permute-start(bf16[256,1408]{1,0:T(8,128)(2,1)S(1)} %broadcast_select_fusion), channel_id=1, source_target_pairs={{64,0},{65,1},{66,2},{67,3},{68,4},{69,5},{70,6},{71,7},{72,8},{73... | collective-permute-start | bytes 2162696 | tf_op jit(solution)/shard_map/grad_gate_rep/ppermute | solution.py:68
  506.5 33.5 %collective-permute-start.36 = (bf16[120,2048]{1,0:T(8,128)(2,1)}, bf16[120,2048]{1,0:T(8,128)(2,1)}, u32[]{:S(2)}, u32[]{:S(2)}) collective-permute-start(bf16[120,2048]{1,0:T(8,128)(2,1)} %add_convert_fusion.1), channel_id=1, source_target_pairs={{0,0},{8,1},{16,2},{24,3},{32,4},{40,5},{48,6},{56,7},{1,8},{9,9},... | collective-permute-start | bytes 1474568 | tf_op jit(solution)/shard_map/grad_out_down_rep/ppermute | solution.py:73
  517.4 27.5 %all-to-all-start.7 = ((bf16[8,32,1408]{2,1,0:T(8,128)(2,1)}), bf16[8,32,1408]{2,1,0:T(8,128)(2,1)S(1)}, u32[]{:S(2)}, u32[]{:S(2)}) async-start(bf16[8,32,1408]{2,1,0:T(8,128)(2,1)} %bitcast.34), calls=%async_computation.8 | async-start | bytes 1441792 | tf_op jit(solution)/shard_map/grad_gate_line/all_to_all | solution.py:138
  (45 other events, 355.2 us)
Sparse Core Ops, SparseCore 0:
  60.5 176.6 all-gather.1
  276.9 164.4 reduce-scatter.1
